TPU v7x, 32 devices: a whole 2x2x4 slice. The times are simulated.
32 devices in a mesh: grp: 2 (over core), seq: 4 (over z), head: 4 (over y, x).
Axes of the slice: x: 2, y: 2, z: 4, core: 2. Of those that a mesh axis runs over, the one named last changes fastest.
Arguments:
- queries: bfloat16 [2048, 8192], P('seq', ('grp', 'head')), may hold values from -140 to 140
- key_rows: bfloat16 [2048, 1024], P('seq', ('grp', 'head')), may hold values from -6 to 6
- values: bfloat16 [2048, 1024], P('seq', ('grp', 'head')), may hold values from -6 to 6
- out_grad: bfloat16 [2048, 8192], P('seq', ('grp', 'head')), may hold values from -6 to 6
- teacher_window: bfloat16 [16, 3, 64, 128, 128], P('seq', None, ('grp', 'head')), may hold values from -16 to 250
- teacher_global: bfloat16 [16, 2, 64, 128, 128], P('seq', None, ('grp', 'head')), may hold values from -16 to 250
- global_picks: int32 [16, 2], P('seq'), may hold values from -1 to 3, as said below
- mix_weight: float32 [2048], P('seq'), may hold values from 0.05 to 0.95
Outputs:
- query_grad: bfloat16 [2048, 8192], P('seq', ('grp', 'head'))
- key_grad: bfloat16 [2048, 1024], P('seq', ('grp', 'head'))
- value_grad: bfloat16 [2048, 1024], P('seq', ('grp', 'head'))
- row_loss: float32 [2048], P('seq')
Inputs may be any that keep to these rules, and one draw needn't show every extreme that they name: `global_picks`: in each row the non-negative entries are distinct, and an entry of query block b is below b - 2.
All inputs are finite; a program needn't handle non-finite values.
Results may differ from a plain program's by a relative error of at most 0.005.
Values may be sent and summed in bfloat16 or wider, within the bound.
No kernel may reach another device: no remote copies, remote signals or barrier semaphores. Data moves between devices by JAX's collectives and lax.ppermute only.
A program may use at most 128 MiB of HBM per device.

v0:
```python
import functools
import math

import jax
import jax.numpy as jnp
from jax import lax
from jax.experimental import pallas as pl
from jax.experimental.pallas import tpu as pltpu
from jax.sharding import PartitionSpec as P

E = 128
BLK = 128
WIN = 3
NGLOB = 4
LEAD = WIN - 1
FAN = 4
LOG2E = math.log2(math.e)
LN2 = math.log(2.0)
NT = (((1,), (1,)), ((), ()))
BF = jnp.bfloat16
F32 = jnp.float32


def shift(block, axis, distance):
    count = lax.axis_size(axis)
    route = [(i, i + distance) for i in range(count) if 0 <= i + distance < count]
    return lax.ppermute(block, axis, route)


def sum_over(block, axis):
    count = lax.axis_size(axis)
    if count & (count - 1):
        return lax.psum(block, axis)
    step = 1
    while step < count:
        block = block + lax.ppermute(block, axis, [(i, i ^ step) for i in range(count)])
        step *= 2
    return block


def block_kernel(
    first, crossing, slots, chained,
    base_ref, picks_ref, q_ref, g_ref, *rest,
):
    teacher_refs = rest[:slots]
    rest = rest[slots:]
    own_k, own_v, sink_k, sink_v, w_ref = rest[:5]
    rest = rest[5:]
    if crossing:
        before_ref, rest = rest[0], rest[1:]
    if chained:
        acc_in, rest = rest[:4], rest[4:]
    dq_ref, loss_ref, dk_ref, dv_ref, dsk_ref, dsv_ref = rest[:6]
    rest = rest[6:]
    if crossing:
        back_ref, rest = rest[0], rest[1:]
    ds_scr, pb_scr = rest
    step = pl.program_id(0)
    block = first + step
    heads = q_ref.shape[1] // E
    scale = 1.0 / math.sqrt(E)
    factor = scale * LOG2E

    @pl.when(step == 0)
    def _():
        if chained:
            for out, given in zip((dk_ref, dv_ref, dsk_ref, dsv_ref), acc_in):
                out[...] = given[...]
        else:
            for out in (dk_ref, dv_ref, dsk_ref, dsv_ref):
                out[...] = jnp.zeros_like(out)

    picks = [picks_ref[block, g] for g in range(slots - WIN)]
    live = [None] + [base_ref[0] + block - d >= 0 for d in range(1, WIN)] + [p >= 0 for p in picks]
    sink_at = [pl.multiple_of(jnp.maximum(p, 0) * BLK, BLK) for p in picks]

    def rows_of(d):
        return pl.ds(pl.multiple_of((block - d) * BLK, BLK), BLK)

    keys, vals = [], []
    for d in range(WIN):
        if d in crossing:
            at = first + LEAD - d
            keys.append(before_ref[0, at])
            vals.append(before_ref[1, at])
        else:
            keys.append(own_k[rows_of(d), :])
            vals.append(own_v[rows_of(d), :])
    for at in sink_at:
        keys.append(sink_k[pl.ds(at, BLK), :])
        vals.append(sink_v[pl.ds(at, BLK), :])
    kcat = jnp.concatenate(keys, axis=0)
    vcat = jnp.concatenate(vals, axis=0)
    kcat_t = kcat.T

    w1 = w_ref[0]
    w2 = jnp.concatenate([w1, w1], axis=1)
    slope = (w2 - 1.0) * LN2
    wide = 2 * BLK
    key_id = lax.broadcasted_iota(jnp.int32, (BLK, wide), 0)
    row_id = lax.broadcasted_iota(jnp.int32, (BLK, wide), 1) & (BLK - 1)
    causal = key_id <= row_id
    low = jnp.float32(-1e9)
    loss = jnp.zeros((1, wide), F32)

    def total(x):
        return jnp.sum(x, axis=0, keepdims=True)

    for pair in range(heads // 2):
        ha, hb = 2 * pair, 2 * pair + 1
        q2 = jnp.concatenate([q_ref[:, ha * E:(ha + 1) * E], q_ref[:, hb * E:(hb + 1) * E]], axis=0)
        g2 = jnp.concatenate([g_ref[:, ha * E:(ha + 1) * E], g_ref[:, hb * E:(hb + 1) * E]], axis=0)
        s_all = lax.dot_general(kcat, q2, NT, preferred_element_type=F32)
        pg_all = lax.dot_general(vcat, g2, NT, preferred_element_type=F32)
        held, stats = [], []
        for j in range(slots):
            s = s_all[j * BLK:(j + 1) * BLK]
            pg = pg_all[j * BLK:(j + 1) * BLK]
            t = jnp.concatenate([teacher_refs[j][0, 0, ha], teacher_refs[j][0, 0, hb]], axis=0)
            t = t.T.astype(F32)
            if j == 0:
                s = jnp.where(causal, s, low)
                t = jnp.where(causal, t, low)
            m = jnp.max(s, axis=0, keepdims=True)
            mt = jnp.max(t, axis=0, keepdims=True)
            x = (s - m) * factor
            y = (t - mt) * LOG2E
            es = jnp.exp2(x)
            et = jnp.exp2(y)
            gap = y - x
            u = pg + slope * gap
            stats.append((m, mt, total(es), total(et), total(et * gap), total(es * gap), total(es * u)))
            held.append((es, et, u))
        m = stats[0][0]
        mt = stats[0][1]
        for j in range(1, slots):
            m = jnp.maximum(m, jnp.where(live[j], stats[j][0], low))
            mt = jnp.maximum(mt, jnp.where(live[j], stats[j][1], low))
        a = [(st[0] - m) * factor for st in stats]
        b = [(st[1] - mt) * LOG2E for st in stats]
        fa = [jnp.exp2(v) for v in a]
        fb = [jnp.exp2(v) for v in b]
        for j in range(1, slots):
            fa[j] = jnp.where(live[j], fa[j], 0.0)
            fb[j] = jnp.where(live[j], fb[j], 0.0)
        z = functools.reduce(jnp.add, [f * st[2] for f, st in zip(fa, stats)])
        zt = functools.reduce(jnp.add, [f * st[3] for f, st in zip(fb, stats)])
        rz, rzt = 1.0 / z, 1.0 / zt
        both = jnp.log2(z) - jnp.log2(zt)
        off = [vb - va + both for va, vb in zip(a, b)]
        fwd = functools.reduce(jnp.add, [f * (st[4] + o * st[3]) for f, o, st in zip(fb, off, stats)])
        rev = functools.reduce(jnp.add, [f * (st[5] + o * st[2]) for f, o, st in zip(fa, off, stats)])
        mean_u = functools.reduce(
            jnp.add, [f * (st[6] + slope * o * st[2]) for f, o, st in zip(fa, off, stats)]
        )
        loss = loss + (w2 * LN2) * (rzt * fwd) + slope * (rz * rev)
        base = w2 - rz * mean_u
        cols = pl.ds(pair * wide, wide)
        for j in range(slots):
            es, et, u = held[j]
            p = es * (fa[j] * rz)
            ds = p * (u + (base + slope * off[j])) - et * (w2 * (fb[j] * rzt))
            ds_scr[j * BLK:(j + 1) * BLK, cols] = ds.astype(BF)
            pb_scr[j * BLK:(j + 1) * BLK, cols] = p.astype(BF)
        dq_t = jnp.dot(kcat_t, ds_scr[:, cols], preferred_element_type=F32) * scale
        dq2 = dq_t.T.astype(BF)
        dq_ref[:, ha * E:(ha + 1) * E] = dq2[:BLK]
        dq_ref[:, hb * E:(hb + 1) * E] = dq2[BLK:]
    loss_ref[0] = loss[:, :BLK] + loss[:, BLK:]

    q_all = jnp.concatenate([q_ref[:, h * E:(h + 1) * E] for h in range(heads)], axis=0)
    g_all = jnp.concatenate([g_ref[:, h * E:(h + 1) * E] for h in range(heads)], axis=0)
    dk = jnp.dot(ds_scr[...], q_all, preferred_element_type=F32) * scale
    dv = jnp.dot(pb_scr[...], g_all, preferred_element_type=F32)
    for d in range(WIN):
        part_k, part_v = dk[d * BLK:(d + 1) * BLK], dv[d * BLK:(d + 1) * BLK]
        if d in crossing:
            at = first + LEAD - d
            back_ref[0, at] = part_k
            back_ref[1, at] = part_v
        else:
            dk_ref[rows_of(d), :] += part_k
            dv_ref[rows_of(d), :] += part_v
    if crossing:
        untouched = [i for i in range(LEAD) if i not in [first + LEAD - d for d in crossing]]
        for i in untouched:
            back_ref[0, i] = jnp.zeros((BLK, E), F32)
            back_ref[1, i] = jnp.zeros((BLK, E), F32)
    for g, at in enumerate(sink_at):
        j = WIN + g
        dsk_ref[pl.ds(at, BLK), :] += dk[j * BLK:(j + 1) * BLK]
        dsv_ref[pl.ds(at, BLK), :] += dv[j * BLK:(j + 1) * BLK]


def run_blocks(first, count, base, picks, queries, out_grad, window, incoming, glob, own, sinks, weights,
               before, acc):
    crossing = [d for d in range(WIN) if d > first]
    assert not crossing or count == 1
    tokens, columns = queries.shape
    heads = window.shape[2]
    slots = WIN + picks.shape[1]
    tile = (1, 1, heads, BLK, BLK)
    whole = lambda i, *_: (0, 0)
    args = [queries, out_grad]
    specs = [pl.BlockSpec((BLK, columns), lambda i, *_: (first + i, 0))] * 2
    for d in range(WIN):
        if d in crossing:
            args.append(incoming[d])
            specs.append(pl.BlockSpec(tile, lambda i, *_: (0, 0, 0, 0, 0)))
        else:
            args.append(window)
            specs.append(pl.BlockSpec(tile, lambda i, *_, d=d: (first + i - d, d, 0, 0, 0)))
    for g in range(slots - WIN):
        args.append(glob)
        specs.append(pl.BlockSpec(tile, lambda i, *_, g=g: (first + i, g, 0, 0, 0)))
    for x in (*own, *sinks):
        args.append(x)
        specs.append(pl.BlockSpec(x.shape, whole))
    args.append(weights)
    specs.append(pl.BlockSpec((1, 1, BLK), lambda i, *_: (first + i, 0, 0)))
    if crossing:
        args.append(before)
        specs.append(pl.BlockSpec(before.shape, lambda i, *_: (0, 0, 0, 0)))
    chained = acc is not None
    acc_shapes = [(tokens, E)] * 2 + [(NGLOB * BLK, E)] * 2
    if chained:
        args.extend(acc)
        specs.extend(pl.BlockSpec(s, whole) for s in acc_shapes)
    outs = [
        jax.ShapeDtypeStruct((count * BLK, columns), BF),
        jax.ShapeDtypeStruct((count, 1, BLK), F32),
    ] + [jax.ShapeDtypeStruct(s, F32) for s in acc_shapes]
    out_specs = [
        pl.BlockSpec((BLK, columns), lambda i, *_: (i, 0)),
        pl.BlockSpec((1, 1, BLK), lambda i, *_: (i, 0, 0)),
    ] + [pl.BlockSpec(s, whole) for s in acc_shapes]
    if crossing:
        back = (2, LEAD, BLK, E)
        outs.append(jax.ShapeDtypeStruct(back, F32))
        out_specs.append(pl.BlockSpec(back, lambda i, *_: (0, 0, 0, 0)))
    elements = count * slots * heads * BLK * BLK
    return pl.pallas_call(
        functools.partial(block_kernel, first, crossing, slots, chained),
        out_shape=outs,
        grid_spec=pltpu.PrefetchScalarGridSpec(
            num_scalar_prefetch=2,
            grid=(count,),
            in_specs=specs,
            out_specs=out_specs,
            scratch_shapes=[pltpu.VMEM((slots * BLK, heads * BLK), BF)] * 2,
        ),
        compiler_params=pltpu.CompilerParams(vmem_limit_bytes=48 * 1024 * 1024),
        cost_estimate=pl.CostEstimate(
            flops=elements * E * 10, bytes_accessed=elements * 3, transcendentals=2 * elements
        ),
        name=f"blocks_from_{first}",
    )(base, picks, *args)


def local(queries, key_rows, values, out_grad, teacher_window, teacher_global, global_picks, mix_weight):
    tokens, columns = queries.shape
    blocks = tokens // BLK
    assert key_rows.shape[1] == E and blocks >= NGLOB
    where = lax.axis_index("seq")
    count = lax.axis_size("seq")
    base = (where * blocks).astype(jnp.int32).reshape(1)
    weights = mix_weight.reshape(blocks, 1, BLK)

    tail = slice(tokens - LEAD * BLK, tokens)
    first_rows = slice(0, NGLOB * BLK)
    pair = jnp.stack([key_rows, values])
    got = shift(pair, "seq", 1)
    before = got[:, tail].reshape(2, LEAD, BLK, E)
    sinks = jnp.where(where == 0, pair[:, first_rows], got[:, first_rows])
    span, known = 1, pair[:, first_rows]
    while span < count:
        for times in range(1, FAN):
            if span == 1 and times == 1:
                continue
            route = [(i, i + times * span) for i in range(span) if i + times * span < count]
            if route:
                more = lax.ppermute(known, "seq", route)
                sinks = jnp.where((where >= times * span) & (where < (times + 1) * span), more, sinks)
        span *= FAN
        known = sinks

    incoming = {}
    for block in range(LEAD - 1, -1, -1):
        offsets = list(range(block + 1, WIN))
        out = jnp.concatenate(
            [teacher_window[blocks + block - d:blocks + block - d + 1, d:d + 1] for d in offsets], axis=0
        )
        came = shift(out, "seq", 1)
        incoming[block] = {d: came[i:i + 1] for i, d in enumerate(offsets)}

    own = (key_rows, values)
    sink_arrays = (sinks[0], sinks[1])
    run = lambda first, n, acc: run_blocks(
        first, n, base, global_picks, queries, out_grad, teacher_window, incoming.get(first),
        teacher_global, own, sink_arrays, weights, before, acc,
    )
    dq, loss = {}, {}
    dq[LEAD], loss[LEAD], *acc = run(LEAD, blocks - LEAD, None)
    back = 0.0
    for block in range(LEAD - 1, -1, -1):
        dq[block], loss[block], *rest = run(block, 1, acc)
        acc, part = rest[:4], rest[4]
        back = back + part
    order = sorted(dq)
    query_grad = jnp.concatenate([dq[i] for i in order], axis=0)
    row_terms = jnp.concatenate([loss[i] for i in order], axis=0).reshape(tokens)

    dk, dv, dsk, dsv = acc
    sums = jnp.stack([dsk, dsv])
    leaving = jnp.concatenate([back.reshape(2, LEAD * BLK, E), sums], axis=1).astype(BF)
    arrived = shift(leaving, "seq", -1)
    returned = arrived[:, :LEAD * BLK].astype(F32)
    sums = sums + arrived[:, LEAD * BLK:].astype(F32)
    reach = 2
    while reach < count:
        route = [(i, i - reach) for i in range(reach, count, 2 * reach)]
        sums = sums + lax.ppermute(sums.astype(BF), "seq", route).astype(F32)
        reach *= 2
    row_loss = sum_over(sum_over(row_terms, "grp"), "head")
    own_sums = jnp.stack([dk, dv])
    own_sums = own_sums.at[:, tail].add(returned)
    own_sums = own_sums.at[:, first_rows].add(jnp.where(where == 0, sums, 0.0))
    grads = own_sums.astype(BF)
    return (query_grad, grads[0], grads[1], row_loss)


def solution(mesh):
    heads = ("grp", "head")
    placed = (
        P("seq", heads),
        P("seq", heads),
        P("seq", heads),
        P("seq", heads),
        P("seq", None, heads, None, None),
        P("seq", None, heads, None, None),
        P("seq", None),
        P("seq"),
    )
    return jax.shard_map(
        local,
        mesh=mesh,
        in_specs=placed,
        out_specs=(P("seq", heads), P("seq", heads), P("seq", heads), P("seq")),
        check_vma=False,
    )
```

profile of v0, /device:TPU:0, one launch (start us, length us, event | category | flops | bytes accessed | tf_op | source)
XLA Modules:
  0.0 71.3 jit_solution(8749652802023044492)
XLA Ops:
  0.7 1.7 %pad_maximum_fusion.5 = bf16[2,512,128]{2,1,0:T(8,128)(2,1)} fusion(bf16[1,512,128]{2,1,0:T(8,128)(2,1)} %bitcast.21, bf16[1,512,128]{2,1,0:T(8,128)(2,1)} %bitcast.19), kind=kLoop, calls=%fused_computation.14 | loop fusion | flops 131072 | bytes 524288 | tf_op jit(solution)/shard_map/stack | solution.py:271
  2.4 5.1 %collective-permute-start.3 = (bf16[2,512,128]{2,1,0:T(8,128)(2,1)}, bf16[2,512,128]{2,1,0:T(8,128)(2,1)S(1)}, u32[]{:S(2)}, u32[]{:S(2)}) collective-permute-start(bf16[2,512,128]{2,1,0:T(8,128)(2,1)} %pad_maximum_fusion.5), channel_id=1, source_target_pairs={{0,4},{4,8},{8,12},{1,5},{5,9},{9,13},{2,6},{6,10},{10,14},{3,7},{... | collective-permute-start | bytes 786440 | tf_op jit(solution)/shard_map/ppermute | solution.py:27
  7.5 5.2 %collective-permute-start.2 = (bf16[2,512,128]{2,1,0:T(8,128)(2,1)}, bf16[2,512,128]{2,1,0:T(8,128)(2,1)}, u32[]{:S(2)}, u32[]{:S(2)}) collective-permute-start(bf16[2,512,128]{2,1,0:T(8,128)(2,1)} %pad_maximum_fusion.5), channel_id=1, source_target_pairs={{0,8},{1,9},{2,10},{3,11},{16,24},{17,25},{18,26},{19,27}} | collective-permute-start | bytes 786440 | tf_op jit(solution)/shard_map/ppermute | solution.py:282
  12.7 2.0 %collective-permute-start.1 = (bf16[2,512,128]{2,1,0:T(8,128)(2,1)}, bf16[2,512,128]{2,1,0:T(8,128)(2,1)}, u32[]{:S(2)}, u32[]{:S(2)}) collective-permute-start(bf16[2,512,128]{2,1,0:T(8,128)(2,1)} %pad_maximum_fusion.5), channel_id=1, source_target_pairs={{0,12},{1,13},{2,14},{3,15},{16,28},{17,29},{18,30},{19,31}} | collective-permute-start | bytes 786440 | tf_op jit(solution)/shard_map/ppermute | solution.py:282
  14.7 1.9 %fusion.5 = (bf16[1,1,8,128,128]{4,3,2,1,0:T(8,128)(2,1)S(1)}, bf16[1,1,8,128,128]{4,3,2,1,0:T(8,128)(2,1)}, bf16[1,1,8,128,128]{4,3,2,1,0:T(8,128)(2,1)S(1)}) fusion(bf16[4,3,8,128,128]{4,3,2,1,0:T(8,128)(2,1)} %rest_0_.5), kind=kLoop, calls=%fused_computation.22 | loop fusion | bytes 1572864 | tf_op jit(solution)/shard_map/slice | solution.py:291
  16.6 1.3 %collective-permute-start.4 = (bf16[1,1,8,128,128]{4,3,2,1,0:T(8,128)(2,1)}, bf16[1,1,8,128,128]{4,3,2,1,0:T(8,128)(2,1)S(1)}, u32[]{:S(2)}, u32[]{:S(2)}) collective-permute-start(bf16[1,1,8,128,128]{4,3,2,1,0:T(8,128)(2,1)} %get-tuple-element.77), channel_id=1, source_target_pairs={{0,4},{4,8},{8,12},{1,5},{5,9},{9,13},{2,6},{6,10},{10,14},{3,7},{... | collective-permute-start | bytes 786440 | tf_op jit(solution)/shard_map/ppermute | solution.py:27
  17.9 0.8 %pad_maximum_fusion.2 = bf16[2,1,8,128,128]{4,3,2,1,0:T(8,128)(2,1)} fusion(bf16[1,1,8,128,128]{4,3,2,1,0:T(8,128)(2,1)S(1)} %get-tuple-element.78, bf16[1,1,8,128,128]{4,3,2,1,0:T(8,128)(2,1)S(1)} %get-tuple-element.76), kind=kLoop, calls=%fused_computation.4 | loop fusion | flops 262144 | bytes 1048576 | tf_op jit(solution)/shard_map/concatenate | solution.py:290
  18.7 1.3 %collective-permute-start = (bf16[2,1,8,128,128]{4,3,2,1,0:T(8,128)(2,1)}, bf16[2,1,8,128,128]{4,3,2,1,0:T(8,128)(2,1)S(1)}, u32[]{:S(2)}, u32[]{:S(2)}) collective-permute-start(bf16[2,1,8,128,128]{4,3,2,1,0:T(8,128)(2,1)} %pad_maximum_fusion.2), channel_id=1, source_target_pairs={{0,4},{4,8},{8,12},{1,5},{5,9},{9,13},{2,6},{6,10},{10,14},{3,7},{... | collective-permute-start | bytes 1572872 | tf_op jit(solution)/shard_map/ppermute | solution.py:27
  20.0 0.1 copy.14.picks_ref
  20.1 0.0 collective-permute-done.3
  20.1 0.0 collective-permute-done.2
  20.1 5.7 %collective-permute-done.1 = bf16[2,512,128]{2,1,0:T(8,128)(2,1)} collective-permute-done((bf16[2,512,128]{2,1,0:T(8,128)(2,1)}, bf16[2,512,128]{2,1,0:T(8,128)(2,1)}, u32[]{:S(2)}, u32[]{:S(2)}) %collective-permute-start.1) | collective-permute-done | bytes 262176 | tf_op jit(solution)/shard_map/ppermute | solution.py:282
  25.8 0.1 select_select_fusion
  26.0 10.2 %blocks_from_2.1 = (bf16[256,1024]{1,0:T(8,128)(2,1)S(1)}, f32[2,1,128]{2,1,0:T(1,128)S(1)}, f32[512,128]{1,0:T(8,128)S(1)}, f32[512,128]{1,0:T(8,128)S(1)}, f32...) custom-call(s32[1]{0:T(128)} %bitcast.base_ref, s32[4,2]{1,0:T(4,128)S(1)} %copy.14.picks_ref, bf16[512,1024]{1,0:T(8,128)(2,1)S(1)} %copy-done, ...), custom_call_target="tpu_custom_call" | custom-call | flops 1677721600 | bytes 3932160 | tf_op jit(solution)/shard_map/blocks_from_2/pallas_call | solution.py:242
  36.1 0.0 collective-permute-done.4.rest_2_
  36.1 5.8 %blocks_from_1.1 = (bf16[128,1024]{1,0:T(8,128)(2,1)S(1)}, f32[1,1,128]{2,1,0:T(1,128)S(1)}, f32[512,128]{1,0:T(8,128)S(1)}, f32[512,128]{1,0:T(8,128)S(1)}, f32...) custom-call(s32[1]{0:T(128)} %bitcast.base_ref, s32[4,2]{1,0:T(4,128)S(1)} %copy.14.picks_ref, ...), custom_call_target="tpu_custom_call" | custom-call | flops 838860800 | bytes 1966080 | tf_op jit(solution)/shard_map/blocks_from_1/pallas_call | solution.py:242
  41.9 0.0 collective-permute-done
  42.0 5.7 %blocks_from_0.1 = (bf16[128,1024]{1,0:T(8,128)(2,1)S(1)}, f32[1,1,128]{2,1,0:T(1,128)S(1)}, f32[512,128]{1,0:T(8,128)S(1)}, f32[512,128]{1,0:T(8,128)S(1)}, f32...) custom-call(s32[1]{0:T(128)} %bitcast.base_ref, s32[4,2]{1,0:T(4,128)S(1)} %copy.14.picks_ref, ...), custom_call_target="tpu_custom_call" | custom-call | flops 838860800 | bytes 1966080 | tf_op jit(solution)/shard_map/blocks_from_0/pallas_call | solution.py:242
  47.8 1.3 %collective-permute-start.5 = (bf16[2,768,128]{2,1,0:T(8,128)(2,1)S(1)}, bf16[2,768,128]{2,1,0:T(8,128)(2,1)S(1)}, u32[]{:S(2)}, u32[]{:S(2)}) collective-permute-start(bf16[2,768,128]{2,1,0:T(8,128)(2,1)S(1)} %pad_maximum_fusion.4), channel_id=1, source_target_pairs={{4,0},{8,4},{12,8},{5,1},{9,5},{13,9},{6,2},{10,6},{14,10},{7,3},{... | collective-permute-start | bytes 1179656 | tf_op jit(solution)/shard_map/ppermute | solution.py:27
  49.1 0.1 collective-permute-start.7
  49.2 1.1 %collective-permute-done.7 = f32[512]{0:T(512)S(1)} collective-permute-done((f32[512]{0:T(512)S(1)}, f32[512]{0:T(512)S(1)}, u32[]{:S(2)}, u32[]{:S(2)}) %collective-permute-start.7) | collective-permute-done | bytes 2080 | tf_op jit(solution)/shard_map/ppermute | solution.py:36
  50.3 1.5 %collective-permute-start.8 = (f32[512]{0:T(512)S(1)}, f32[512]{0:T(512)S(1)}, u32[]{:S(2)}, u32[]{:S(2)}) collective-permute-start(f32[512]{0:T(512)S(1)} %add.39), channel_id=1, source_target_pairs={{0,1},{1,0},{2,3},{3,2},{4,5},{5,4},{6,7},{7,6},{8,9},{9,8},{10,11... | collective-permute-start | bytes 6152 | tf_op jit(solution)/shard_map/ppermute | solution.py:36
  51.8 1.0 %pad_maximum_fusion = bf16[512,1024]{1,0:T(8,128)(2,1)} fusion(bf16[256,1024]{1,0:T(8,128)(2,1)S(1)} %get-tuple-element.66, bf16[128,1024]{1,0:T(8,128)(2,1)S(1)} %get-tuple-element.65, bf16[128,1024]{1,0:T(8,128)(2,1)S(1)} %get-tuple-element.64), kind=kLoop, calls=%fused_computation | loop fusion | flops 3145728 | bytes 2097152 | tf_op jit(solution)/shard_map/concatenate | solution.py:310
  52.9 1.1 %collective-permute-done.8 = f32[512]{0:T(512)S(1)} collective-permute-done((f32[512]{0:T(512)S(1)}, f32[512]{0:T(512)S(1)}, u32[]{:S(2)}, u32[]{:S(2)}) %collective-permute-start.8) | collective-permute-done | bytes 2080 | tf_op jit(solution)/shard_map/ppermute | solution.py:36
  53.9 1.5 %collective-permute-start.9 = (f32[512]{0:T(512)S(1)}, f32[512]{0:T(512)S(1)}, u32[]{:S(2)}, u32[]{:S(2)}) collective-permute-start(f32[512]{0:T(512)S(1)} %add.40), channel_id=1, source_target_pairs={{0,2},{1,3},{2,0},{3,1},{4,6},{5,7},{6,4},{7,5},{8,10},{9,11},{10,... | collective-permute-start | bytes 6152 | tf_op jit(solution)/shard_map/ppermute | solution.py:36
  55.4 4.8 %collective-permute-done.5 = bf16[2,768,128]{2,1,0:T(8,128)(2,1)S(1)} collective-permute-done((bf16[2,768,128]{2,1,0:T(8,128)(2,1)S(1)}, bf16[2,768,128]{2,1,0:T(8,128)(2,1)S(1)}, u32[]{:S(2)}, u32[]{:S(2)}) %collective-permute-start.5) | collective-permute-done | bytes 393248 | tf_op jit(solution)/shard_map/ppermute | solution.py:27
  60.2 0.1 fusion.1
  60.3 1.3 %collective-permute-start.6 = (bf16[2,512,128]{2,1,0:T(8,128)(2,1)S(1)}, bf16[2,512,128]{2,1,0:T(8,128)(2,1)S(1)}, u32[]{:S(2)}, u32[]{:S(2)}) collective-permute-start(bf16[2,512,128]{2,1,0:T(8,128)(2,1)S(1)} %fusion.1), channel_id=1, source_target_pairs={{8,0},{9,1},{10,2},{11,3},{24,16},{25,17},{26,18},{27,19}} | collective-permute-start | bytes 786440 | tf_op jit(solution)/shard_map/ppermute | solution.py:322
  61.6 0.6 add.41
  62.3 8.1 %collective-permute-done.6 = bf16[2,512,128]{2,1,0:T(8,128)(2,1)S(1)} collective-permute-done((bf16[2,512,128]{2,1,0:T(8,128)(2,1)S(1)}, bf16[2,512,128]{2,1,0:T(8,128)(2,1)S(1)}, u32[]{:S(2)}, u32[]{:S(2)}) %collective-permute-start.6) | collective-permute-done | bytes 262176 | tf_op jit(solution)/shard_map/ppermute | solution.py:322
  70.4 0.1 add_convert_fusion
  70.5 0.7 %slice_bitcast_fusion = (bf16[512,128]{1,0:T(8,128)(2,1)}, bf16[512,128]{1,0:T(8,128)(2,1)}) fusion(bf16[2,512,128]{2,1,0:T(8,128)(2,1)S(1)} %add_convert_fusion), kind=kLoop, calls=%fused_computation.17 | loop fusion | bytes 524288 | tf_op jit(solution)/shard_map/squeeze | solution.py:329
  (24 shorter events, 0.3 us)
Async XLA Ops:
  0.6 25.2 %copy-start.2 = (bf16[512,128]{1,0:T(8,128)(2,1)S(1)}, bf16[512,128]{1,0:T(8,128)(2,1)}, u32[]{:S(2)}) copy-start(bf16[512,128]{1,0:T(8,128)(2,1)} %rest_5_.5) | copy-start | bytes 393220
  0.6 25.2 %copy-start.3 = (bf16[512,128]{1,0:T(8,128)(2,1)S(1)}, bf16[512,128]{1,0:T(8,128)(2,1)}, u32[]{:S(2)}) copy-start(bf16[512,128]{1,0:T(8,128)(2,1)} %rest_6_.5) | copy-start | bytes 393220
  0.7 19.4 %copy-start.5 = (s32[4,2]{0,1:T(2,128)S(1)}, s32[4,2]{0,1:T(2,128)}, u32[]{:S(2)}) copy-start(s32[4,2]{0,1:T(2,128)} %param.20) | copy-start | bytes 100
  2.4 23.5 %copy-start = (bf16[512,1024]{1,0:T(8,128)(2,1)S(1)}, bf16[512,1024]{1,0:T(8,128)(2,1)}, u32[]{:S(2)}) copy-start(bf16[512,1024]{1,0:T(8,128)(2,1)} %q_ref.5) | copy-start | bytes 3145732
  2.4 23.5 %copy-start.1 = (bf16[512,1024]{1,0:T(8,128)(2,1)S(1)}, bf16[512,1024]{1,0:T(8,128)(2,1)}, u32[]{:S(2)}) copy-start(bf16[512,1024]{1,0:T(8,128)(2,1)} %g_ref.5) | copy-start | bytes 3145732
  2.4 23.5 %copy-start.4 = (f32[512]{0:T(512)S(1)}, f32[512]{0:T(512)}, u32[]{:S(2)}) copy-start(f32[512]{0:T(512)} %param.21) | copy-start | bytes 6148
  2.4 17.7 %collective-permute-start.3 = (bf16[2,512,128]{2,1,0:T(8,128)(2,1)}, bf16[2,512,128]{2,1,0:T(8,128)(2,1)S(1)}, u32[]{:S(2)}, u32[]{:S(2)}) collective-permute-start(bf16[2,512,128]{2,1,0:T(8,128)(2,1)} %pad_maximum_fusion.5), channel_id=1, source_target_pairs={{0,4},{4,8},{8,12},{1,5},{5,9},{9,13},{2,6},{6,10},{10,14},{3,7},{... | collective-permute-start | bytes 786440 | tf_op jit(solution)/shard_map/ppermute | solution.py:27
  7.5 12.7 %collective-permute-start.2 = (bf16[2,512,128]{2,1,0:T(8,128)(2,1)}, bf16[2,512,128]{2,1,0:T(8,128)(2,1)}, u32[]{:S(2)}, u32[]{:S(2)}) collective-permute-start(bf16[2,512,128]{2,1,0:T(8,128)(2,1)} %pad_maximum_fusion.5), channel_id=1, source_target_pairs={{0,8},{1,9},{2,10},{3,11},{16,24},{17,25},{18,26},{19,27}} | collective-permute-start | bytes 786440 | tf_op jit(solution)/shard_map/ppermute | solution.py:282
  12.7 13.1 %collective-permute-start.1 = (bf16[2,512,128]{2,1,0:T(8,128)(2,1)}, bf16[2,512,128]{2,1,0:T(8,128)(2,1)}, u32[]{:S(2)}, u32[]{:S(2)}) collective-permute-start(bf16[2,512,128]{2,1,0:T(8,128)(2,1)} %pad_maximum_fusion.5), channel_id=1, source_target_pairs={{0,12},{1,13},{2,14},{3,15},{16,28},{17,29},{18,30},{19,31}} | collective-permute-start | bytes 786440 | tf_op jit(solution)/shard_map/ppermute | solution.py:282
  16.6 19.6 %collective-permute-start.4 = (bf16[1,1,8,128,128]{4,3,2,1,0:T(8,128)(2,1)}, bf16[1,1,8,128,128]{4,3,2,1,0:T(8,128)(2,1)S(1)}, u32[]{:S(2)}, u32[]{:S(2)}) collective-permute-start(bf16[1,1,8,128,128]{4,3,2,1,0:T(8,128)(2,1)} %get-tuple-element.77), channel_id=1, source_target_pairs={{0,4},{4,8},{8,12},{1,5},{5,9},{9,13},{2,6},{6,10},{10,14},{3,7},{... | collective-permute-start | bytes 786440 | tf_op jit(solution)/shard_map/ppermute | solution.py:27
  18.7 23.2 %collective-permute-start = (bf16[2,1,8,128,128]{4,3,2,1,0:T(8,128)(2,1)}, bf16[2,1,8,128,128]{4,3,2,1,0:T(8,128)(2,1)S(1)}, u32[]{:S(2)}, u32[]{:S(2)}) collective-permute-start(bf16[2,1,8,128,128]{4,3,2,1,0:T(8,128)(2,1)} %pad_maximum_fusion.2), channel_id=1, source_target_pairs={{0,4},{4,8},{8,12},{1,5},{5,9},{9,13},{2,6},{6,10},{10,14},{3,7},{... | collective-permute-start | bytes 1572872 | tf_op jit(solution)/shard_map/ppermute | solution.py:27
  47.8 12.4 %collective-permute-start.5 = (bf16[2,768,128]{2,1,0:T(8,128)(2,1)S(1)}, bf16[2,768,128]{2,1,0:T(8,128)(2,1)S(1)}, u32[]{:S(2)}, u32[]{:S(2)}) collective-permute-start(bf16[2,768,128]{2,1,0:T(8,128)(2,1)S(1)} %pad_maximum_fusion.4), channel_id=1, source_target_pairs={{4,0},{8,4},{12,8},{5,1},{9,5},{13,9},{6,2},{10,6},{14,10},{7,3},{... | collective-permute-start | bytes 1179656 | tf_op jit(solution)/shard_map/ppermute | solution.py:27
  49.1 1.2 %collective-permute-start.7 = (f32[512]{0:T(512)S(1)}, f32[512]{0:T(512)S(1)}, u32[]{:S(2)}, u32[]{:S(2)}) collective-permute-start(f32[512]{0:T(512)S(1)} %bitcast.39), channel_id=1, source_target_pairs={{0,16},{16,0},{1,17},{17,1},{2,18},{18,2},{3,19},{19,3},{4,20},{20... | collective-permute-start | bytes 6152 | tf_op jit(solution)/shard_map/ppermute | solution.py:36
  50.3 3.6 %collective-permute-start.8 = (f32[512]{0:T(512)S(1)}, f32[512]{0:T(512)S(1)}, u32[]{:S(2)}, u32[]{:S(2)}) collective-permute-start(f32[512]{0:T(512)S(1)} %add.39), channel_id=1, source_target_pairs={{0,1},{1,0},{2,3},{3,2},{4,5},{5,4},{6,7},{7,6},{8,9},{9,8},{10,11... | collective-permute-start | bytes 6152 | tf_op jit(solution)/shard_map/ppermute | solution.py:36
  53.9 7.7 %collective-permute-start.9 = (f32[512]{0:T(512)S(1)}, f32[512]{0:T(512)S(1)}, u32[]{:S(2)}, u32[]{:S(2)}) collective-permute-start(f32[512]{0:T(512)S(1)} %add.40), channel_id=1, source_target_pairs={{0,2},{1,3},{2,0},{3,1},{4,6},{5,7},{6,4},{7,5},{8,10},{9,11},{10,... | collective-permute-start | bytes 6152 | tf_op jit(solution)/shard_map/ppermute | solution.py:36
  60.3 10.1 %collective-permute-start.6 = (bf16[2,512,128]{2,1,0:T(8,128)(2,1)S(1)}, bf16[2,512,128]{2,1,0:T(8,128)(2,1)S(1)}, u32[]{:S(2)}, u32[]{:S(2)}) collective-permute-start(bf16[2,512,128]{2,1,0:T(8,128)(2,1)S(1)} %fusion.1), channel_id=1, source_target_pairs={{8,0},{9,1},{10,2},{11,3},{24,16},{25,17},{26,18},{27,19}} | collective-permute-start | bytes 786440 | tf_op jit(solution)/shard_map/ppermute | solution.py:322
where the time goes:
time: 71.6 us; the launch traced here: 71.3 us
  Pallas kernels  21.6 us (30%)
  waiting for transfers between devices  20.8 us (29%)
  starting transfers between devices  20.5 us (29%)
  other arithmetic  4.66 us (7%)
  local copies, waits for them, and re-layouts  2.79 us (4%)
  between operations  0.88 us (1%)
    pallas_call x3, Pallas kernels, run_blocks(): pl.pallas_call(functools.partial(block_kernel, first, crossing, slots, ch...  21.6 us
    ppermute x4, starting transfers between devices, shift(): return lax.ppermute(block, axis, route)  8.96 us
    ppermute x1, waiting for transfers between devices, local(): sums = sums + lax.ppermute(sums.astype(BF), 'seq', route).astype(F32)  8.14 us
    ppermute x2, starting transfers between devices, local(): more = lax.ppermute(known, 'seq', route)  7.18 us
    ppermute x2, waiting for transfers between devices, local(): more = lax.ppermute(known, 'seq', route)  5.67 us
    ppermute x4, waiting for transfers between devices, shift(): return lax.ppermute(block, axis, route)  4.79 us
    ppermute x3, starting transfers between devices, sum_over(): lax.ppermute(block, axis, [(i, i ^ step) for i in range(count)])  3.08 us
    ppermute x3, waiting for transfers between devices, sum_over(): lax.ppermute(block, axis, [(i, i ^ step) for i in range(count)])  2.2 us
  transfers between devices with their start and end apart: 10, of which 5 were waited for; matrix products, arithmetic and copies ran while one was open for 7% of the time, Pallas kernels for 22%

commit v1 on v0

--- a/solution.py
+++ b/solution.py
@@ -311,21 +311,27 @@
     row_terms = jnp.concatenate([loss[i] for i in order], axis=0).reshape(tokens)
 
     dk, dv, dsk, dsv = acc
-    sums = jnp.stack([dsk, dsv])
-    leaving = jnp.concatenate([back.reshape(2, LEAD * BLK, E), sums], axis=1).astype(BF)
-    arrived = shift(leaving, "seq", -1)
-    returned = arrived[:, :LEAD * BLK].astype(F32)
-    sums = sums + arrived[:, LEAD * BLK:].astype(F32)
-    reach = 2
+    sums = [dsk, dsv]
+    steps = []
+    reach = 1
     while reach < count:
-        route = [(i, i - reach) for i in range(reach, count, 2 * reach)]
-        sums = sums + lax.ppermute(sums.astype(BF), "seq", route).astype(F32)
+        steps.append([(i, i - reach) for i in range(reach, count, 2 * reach)])
         reach *= 2
+    returned = None
+    for number, route in enumerate(steps):
+        low = [x.astype(BF) for x in sums]
+        if number == 1:
+            row_terms, low[1] = lax.optimization_barrier((row_terms, low[1]))
+        came = [lax.ppermute(x, "seq", route) for x in low]
+        if number == 0:
+            returned = shift(back.astype(BF), "seq", -1).astype(F32)
+        sums = [x + y.astype(F32) for x, y in zip(sums, came)]
     row_loss = sum_over(sum_over(row_terms, "grp"), "head")
-    own_sums = jnp.stack([dk, dv])
-    own_sums = own_sums.at[:, tail].add(returned)
-    own_sums = own_sums.at[:, first_rows].add(jnp.where(where == 0, sums, 0.0))
-    grads = own_sums.astype(BF)
+    grads = []
+    for which, own_sum in enumerate((dk, dv)):
+        whole = own_sum.at[tail].add(returned[which].reshape(LEAD * BLK, E))
+        whole = whole.at[first_rows].add(jnp.where(where == 0, sums[which], 0.0))
+        grads.append(whole.astype(BF))
     return (query_grad, grads[0], grads[1], row_loss)
 
 

time: 71.6 us -> 69.6 us (0.972)
  waiting for transfers between devices: 20.8 us -> 14.1 us
  starting transfers between devices: 20.5 us -> 24.4 us
  other arithmetic: 4.66 us -> 5.94 us
    ppermute x4, waiting for transfers between devices: 4.79 us -> 0.01 us  [shift(): return lax.ppermute(block, axis, route)]
    ppermute x1 -> x4, starting transfers between devices: 1.29 us -> 5.17 us  [local(): came = [lax.ppermute(x, 'seq', route) for x in low]]
    ppermute x1 -> x4, waiting for transfers between devices: 8.14 us -> 4.34 us  [local(): came = [lax.ppermute(x, 'seq', route) for x in low]]
    ppermute x3, waiting for transfers between devices: 2.2 us -> 4.09 us  [sum_over(): lax.ppermute(block, axis, [(i, i ^ step) for i in range(count)])]
    convert_element_type x2 -> x7, other arithmetic: 0.21 us -> 1.6 us  [the longest x2 1.47 us: local(): grads.append(whole.astype(BF))]
    squeeze x1 -> x0, local copies, waits for them, and re-layouts: 0.72 us -> none  [local(): return (query_grad, grads[0], grads[1], row_loss)]
  transfers between devices with their start and end apart: 10 -> 13, of which waited for: 5 -> 6; matrix products, arithmetic and copies ran while one was open for 7% -> 8% of each run, Pallas kernels for 22% -> 23%
where the time goes in v1:
time: 69.6 us; the launch traced here: 69.1 us
  starting transfers between devices  24.4 us (35%)
  Pallas kernels  21.6 us (31%)
  waiting for transfers between devices  14.1 us (20%)
  other arithmetic  5.94 us (9%)
  local copies, waits for them, and re-layouts  2.09 us (3%)
  between operations  0.91 us (1%)
    pallas_call x3, Pallas kernels, run_blocks(): pl.pallas_call(functools.partial(block_kernel, first, crossing, slots, ch...  21.6 us
    ppermute x4, starting transfers between devices, shift(): return lax.ppermute(block, axis, route)  8.96 us
    ppermute x2, starting transfers between devices, local(): more = lax.ppermute(known, 'seq', route)  7.16 us
    ppermute x2, waiting for transfers between devices, local(): more = lax.ppermute(known, 'seq', route)  5.69 us
    ppermute x4, starting transfers between devices, local(): came = [lax.ppermute(x, 'seq', route) for x in low]  5.17 us
    ppermute x4, waiting for transfers between devices, local(): came = [lax.ppermute(x, 'seq', route) for x in low]  4.34 us
    ppermute x3, waiting for transfers between devices, sum_over(): lax.ppermute(block, axis, [(i, i ^ step) for i in range(count)])  4.09 us
    ppermute x3, starting transfers between devices, sum_over(): lax.ppermute(block, axis, [(i, i ^ step) for i in range(count)])  3.15 us
  transfers between devices with their start and end apart: 13, of which 6 were waited for; matrix products, arithmetic and copies ran while one was open for 8% of the time, Pallas kernels for 23%

profile of v1, /device:TPU:0, one launch (start us, length us, event | category | flops | bytes accessed | tf_op | source)
XLA Modules:
  0.0 69.1 jit_solution(17780803217863385138)
XLA Ops:
  0.7 1.8 %pad_maximum_fusion.2 = bf16[2,512,128]{2,1,0:T(8,128)(2,1)} fusion(bf16[1,512,128]{2,1,0:T(8,128)(2,1)} %bitcast.16, bf16[1,512,128]{2,1,0:T(8,128)(2,1)} %bitcast.14), kind=kLoop, calls=%fused_computation.2 | loop fusion | flops 131072 | bytes 524288 | tf_op jit(solution)/shard_map/stack | solution.py:271
  2.4 5.1 %collective-permute-start.3 = (bf16[2,512,128]{2,1,0:T(8,128)(2,1)}, bf16[2,512,128]{2,1,0:T(8,128)(2,1)S(1)}, u32[]{:S(2)}, u32[]{:S(2)}) collective-permute-start(bf16[2,512,128]{2,1,0:T(8,128)(2,1)} %pad_maximum_fusion.2), channel_id=1, source_target_pairs={{0,4},{4,8},{8,12},{1,5},{5,9},{9,13},{2,6},{6,10},{10,14},{3,7},{... | collective-permute-start | bytes 786440 | tf_op jit(solution)/shard_map/ppermute | solution.py:27
  7.5 5.2 %collective-permute-start.2 = (bf16[2,512,128]{2,1,0:T(8,128)(2,1)}, bf16[2,512,128]{2,1,0:T(8,128)(2,1)}, u32[]{:S(2)}, u32[]{:S(2)}) collective-permute-start(bf16[2,512,128]{2,1,0:T(8,128)(2,1)} %pad_maximum_fusion.2), channel_id=1, source_target_pairs={{0,8},{1,9},{2,10},{3,11},{16,24},{17,25},{18,26},{19,27}} | collective-permute-start | bytes 786440 | tf_op jit(solution)/shard_map/ppermute | solution.py:282
  12.7 2.0 %collective-permute-start.1 = (bf16[2,512,128]{2,1,0:T(8,128)(2,1)}, bf16[2,512,128]{2,1,0:T(8,128)(2,1)}, u32[]{:S(2)}, u32[]{:S(2)}) collective-permute-start(bf16[2,512,128]{2,1,0:T(8,128)(2,1)} %pad_maximum_fusion.2), channel_id=1, source_target_pairs={{0,12},{1,13},{2,14},{3,15},{16,28},{17,29},{18,30},{19,31}} | collective-permute-start | bytes 786440 | tf_op jit(solution)/shard_map/ppermute | solution.py:282
  14.7 1.9 %fusion.2 = (bf16[1,1,8,128,128]{4,3,2,1,0:T(8,128)(2,1)S(1)}, bf16[1,1,8,128,128]{4,3,2,1,0:T(8,128)(2,1)}, bf16[1,1,8,128,128]{4,3,2,1,0:T(8,128)(2,1)S(1)}) fusion(bf16[4,3,8,128,128]{4,3,2,1,0:T(8,128)(2,1)} %rest_0_.5), kind=kLoop, calls=%fused_computation.18 | loop fusion | bytes 1572864 | tf_op jit(solution)/shard_map/slice | solution.py:291
  16.5 1.3 %collective-permute-start.4 = (bf16[1,1,8,128,128]{4,3,2,1,0:T(8,128)(2,1)}, bf16[1,1,8,128,128]{4,3,2,1,0:T(8,128)(2,1)S(1)}, u32[]{:S(2)}, u32[]{:S(2)}) collective-permute-start(bf16[1,1,8,128,128]{4,3,2,1,0:T(8,128)(2,1)} %get-tuple-element.113), channel_id=1, source_target_pairs={{0,4},{4,8},{8,12},{1,5},{5,9},{9,13},{2,6},{6,10},{10,14},{3,7},{... | collective-permute-start | bytes 786440 | tf_op jit(solution)/shard_map/ppermute | solution.py:27
  17.8 0.8 %pad_maximum_fusion.1 = bf16[2,1,8,128,128]{4,3,2,1,0:T(8,128)(2,1)} fusion(bf16[1,1,8,128,128]{4,3,2,1,0:T(8,128)(2,1)S(1)} %get-tuple-element.114, bf16[1,1,8,128,128]{4,3,2,1,0:T(8,128)(2,1)S(1)} %get-tuple-element.112), kind=kLoop, calls=%fused_computation.1 | loop fusion | flops 262144 | bytes 1048576 | tf_op jit(solution)/shard_map/concatenate | solution.py:290
  18.7 1.3 %collective-permute-start = (bf16[2,1,8,128,128]{4,3,2,1,0:T(8,128)(2,1)}, bf16[2,1,8,128,128]{4,3,2,1,0:T(8,128)(2,1)S(1)}, u32[]{:S(2)}, u32[]{:S(2)}) collective-permute-start(bf16[2,1,8,128,128]{4,3,2,1,0:T(8,128)(2,1)} %pad_maximum_fusion.1), channel_id=1, source_target_pairs={{0,4},{4,8},{8,12},{1,5},{5,9},{9,13},{2,6},{6,10},{10,14},{3,7},{... | collective-permute-start | bytes 1572872 | tf_op jit(solution)/shard_map/ppermute | solution.py:27
  20.0 0.1 copy.14.picks_ref
  20.1 0.0 collective-permute-done.2
  20.2 5.7 %collective-permute-done.1 = bf16[2,512,128]{2,1,0:T(8,128)(2,1)} collective-permute-done((bf16[2,512,128]{2,1,0:T(8,128)(2,1)}, bf16[2,512,128]{2,1,0:T(8,128)(2,1)}, u32[]{:S(2)}, u32[]{:S(2)}) %collective-permute-start.1) | collective-permute-done | bytes 262176 | tf_op jit(solution)/shard_map/ppermute | solution.py:282
  25.8 0.1 select_select_fusion
  26.0 10.1 %blocks_from_2.1 = (bf16[256,1024]{1,0:T(8,128)(2,1)S(1)}, f32[2,1,128]{2,1,0:T(1,128)S(1)}, f32[512,128]{1,0:T(8,128)S(1)}, f32[512,128]{1,0:T(8,128)S(1)}, f32...) custom-call(s32[1]{0:T(128)} %bitcast.base_ref, s32[4,2]{1,0:T(4,128)S(1)} %copy.14.picks_ref, bf16[512,1024]{1,0:T(8,128)(2,1)S(1)} %copy-done, ...), custom_call_target="tpu_custom_call" | custom-call | flops 1677721600 | bytes 3932160 | tf_op jit(solution)/shard_map/blocks_from_2/pallas_call | solution.py:242
  36.1 5.7 %blocks_from_1.1 = (bf16[128,1024]{1,0:T(8,128)(2,1)S(1)}, f32[1,1,128]{2,1,0:T(1,128)S(1)}, f32[512,128]{1,0:T(8,128)S(1)}, f32[512,128]{1,0:T(8,128)S(1)}, f32...) custom-call(s32[1]{0:T(128)} %bitcast.base_ref, s32[4,2]{1,0:T(4,128)S(1)} %copy.14.picks_ref, ...), custom_call_target="tpu_custom_call" | custom-call | flops 838860800 | bytes 1966080 | tf_op jit(solution)/shard_map/blocks_from_1/pallas_call | solution.py:242
  41.9 5.7 %blocks_from_0.1 = (bf16[128,1024]{1,0:T(8,128)(2,1)S(1)}, f32[1,1,128]{2,1,0:T(1,128)S(1)}, f32[512,128]{1,0:T(8,128)S(1)}, f32[512,128]{1,0:T(8,128)S(1)}, f32...) custom-call(s32[1]{0:T(128)} %bitcast.base_ref, s32[4,2]{1,0:T(4,128)S(1)} %copy.14.picks_ref, ...), custom_call_target="tpu_custom_call" | custom-call | flops 838860800 | bytes 1966080 | tf_op jit(solution)/shard_map/blocks_from_0/pallas_call | solution.py:242
  47.7 1.3 %collective-permute-start.8 = (bf16[512,128]{1,0:T(8,128)(2,1)S(1)}, bf16[512,128]{1,0:T(8,128)(2,1)S(1)}, u32[]{:S(2)}, u32[]{:S(2)}) collective-permute-start(bf16[512,128]{1,0:T(8,128)(2,1)S(1)} %convert_element_type.43), channel_id=1, source_target_pairs={{4,0},{12,8},{5,1},{13,9},{6,2},{14,10},{7,3},{15,11},{20,16},{28,... | collective-permute-start | bytes 393224 | tf_op jit(solution)/shard_map/ppermute | solution.py:325
  49.0 1.3 %collective-permute-start.6 = (bf16[512,128]{1,0:T(8,128)(2,1)S(1)}, bf16[512,128]{1,0:T(8,128)(2,1)S(1)}, u32[]{:S(2)}, u32[]{:S(2)}) collective-permute-start(bf16[512,128]{1,0:T(8,128)(2,1)S(1)} %convert_element_type.38), channel_id=1, source_target_pairs={{4,0},{12,8},{5,1},{13,9},{6,2},{14,10},{7,3},{15,11},{20,16},{28,... | collective-permute-start | bytes 393224 | tf_op jit(solution)/shard_map/ppermute | solution.py:325
  50.3 1.3 %collective-permute-start.5 = (bf16[2,2,128,128]{3,2,1,0:T(8,128)(2,1)S(1)}, bf16[2,2,128,128]{3,2,1,0:T(8,128)(2,1)S(1)}, u32[]{:S(2)}, u32[]{:S(2)}) collective-permute-start(bf16[2,2,128,128]{3,2,1,0:T(8,128)(2,1)S(1)} %add_convert_fusion.2), channel_id=1, source_target_pairs={{4,0},{8,4},{12,8},{5,1},{9,5},{13,9},{6,2},{10,6},{14,10},{7,3},{... | collective-permute-start | bytes 393224 | tf_op jit(solution)/shard_map/ppermute | solution.py:27
  51.7 1.0 %pad_maximum_fusion = bf16[512,1024]{1,0:T(8,128)(2,1)} fusion(bf16[256,1024]{1,0:T(8,128)(2,1)S(1)} %get-tuple-element.100, bf16[128,1024]{1,0:T(8,128)(2,1)S(1)} %get-tuple-element.99, bf16[128,1024]{1,0:T(8,128)(2,1)S(1)} %get-tuple-element.98), kind=kLoop, calls=%fused_computation | loop fusion | flops 3145728 | bytes 2097152 | tf_op jit(solution)/shard_map/concatenate | solution.py:310
  52.7 3.3 %collective-permute-done.8 = bf16[512,128]{1,0:T(8,128)(2,1)S(1)} collective-permute-done((bf16[512,128]{1,0:T(8,128)(2,1)S(1)}, bf16[512,128]{1,0:T(8,128)(2,1)S(1)}, u32[]{:S(2)}, u32[]{:S(2)}) %collective-permute-start.8) | collective-permute-done | bytes 131104 | tf_op jit(solution)/shard_map/ppermute | solution.py:325
  56.1 0.1 collective-permute-start.10
  56.2 1.3 %collective-permute-start.9 = (bf16[512,128]{1,0:T(8,128)(2,1)S(1)}, bf16[512,128]{1,0:T(8,128)(2,1)S(1)}, u32[]{:S(2)}, u32[]{:S(2)}) collective-permute-start(bf16[512,128]{1,0:T(8,128)(2,1)S(1)} %fusion.1), channel_id=1, source_target_pairs={{8,0},{9,1},{10,2},{11,3},{24,16},{25,17},{26,18},{27,19}} | collective-permute-start | bytes 393224 | tf_op jit(solution)/shard_map/ppermute | solution.py:325
  57.5 0.7 collective-permute-done.6
  58.2 1.3 %collective-permute-start.7 = (bf16[512,128]{1,0:T(8,128)(2,1)S(1)}, bf16[512,128]{1,0:T(8,128)(2,1)S(1)}, u32[]{:S(2)}, u32[]{:S(2)}) collective-permute-start(bf16[512,128]{1,0:T(8,128)(2,1)S(1)} %fusion), channel_id=1, source_target_pairs={{8,0},{9,1},{10,2},{11,3},{24,16},{25,17},{26,18},{27,19}} | collective-permute-start | bytes 393224 | tf_op jit(solution)/shard_map/ppermute | solution.py:325
  59.5 1.6 %collective-permute-start.11 = (f32[512]{0:T(512)S(1)}, f32[512]{0:T(512)S(1)}, u32[]{:S(2)}, u32[]{:S(2)}) collective-permute-start(f32[512]{0:T(512)S(1)} %add.65), channel_id=1, source_target_pairs={{0,1},{1,0},{2,3},{3,2},{4,5},{5,4},{6,7},{7,6},{8,9},{9,8},{10,11... | collective-permute-start | bytes 6152 | tf_op jit(solution)/shard_map/ppermute | solution.py:36
  61.1 2.1 %collective-permute-done.11 = f32[512]{0:T(512)S(1)} collective-permute-done((f32[512]{0:T(512)S(1)}, f32[512]{0:T(512)S(1)}, u32[]{:S(2)}, u32[]{:S(2)}) %collective-permute-start.11) | collective-permute-done | bytes 2080 | tf_op jit(solution)/shard_map/ppermute | solution.py:36
  63.1 1.5 %collective-permute-start.12 = (f32[512]{0:T(512)S(1)}, f32[512]{0:T(512)S(1)}, u32[]{:S(2)}, u32[]{:S(2)}) collective-permute-start(f32[512]{0:T(512)S(1)} %add.66), channel_id=1, source_target_pairs={{0,2},{1,3},{2,0},{3,1},{4,6},{5,7},{6,4},{7,5},{8,10},{9,11},{10,... | collective-permute-start | bytes 6152 | tf_op jit(solution)/shard_map/ppermute | solution.py:36
  64.7 2.0 %collective-permute-done.12 = f32[512]{0:T(512)S(1)} collective-permute-done((f32[512]{0:T(512)S(1)}, f32[512]{0:T(512)S(1)}, u32[]{:S(2)}, u32[]{:S(2)}) %collective-permute-start.12) | collective-permute-done | bytes 2080 | tf_op jit(solution)/shard_map/ppermute | solution.py:36
  66.7 0.6 add.67
  67.3 0.3 collective-permute-done.7
  67.6 0.7 %add_convert_fusion.1 = bf16[512,128]{1,0:T(8,128)(2,1)} fusion(f32[512,128]{1,0:T(8,128)S(1)} %get-tuple-element.122, bf16[512,128]{1,0:T(8,128)(2,1)S(1)} %collective-permute-done.7, f32[512,128]{1,0:T(8,128)S(1)} %get-tuple-element.104, bf16[512,128]{1,0:T(8,128)(2,1)S(1)} %collective-permute-done.6, pred[]{:T(512)S(6)} %eq.2), kind=kLoop, calls=%fused_computation.5 | loop fusion | flops 458752 | bytes 917505 | tf_op jit(solution)/shard_map/convert_element_type | solution.py:334
  68.4 0.7 %add_convert_fusion = bf16[512,128]{1,0:T(8,128)(2,1)} fusion(f32[512,128]{1,0:T(8,128)S(1)} %get-tuple-element.121, bf16[512,128]{1,0:T(8,128)(2,1)S(1)} %collective-permute-done.9, f32[512,128]{1,0:T(8,128)S(1)} %get-tuple-element.106, bf16[512,128]{1,0:T(8,128)(2,1)S(1)} %collective-permute-done.8, pred[]{:T(512)S(6)} %eq.2), kind=kLoop, calls=%fused_computation.3 | loop fusion | flops 458752 | bytes 917505 | tf_op jit(solution)/shard_map/convert_element_type | solution.py:334
  (31 shorter events, 0.3 us)
Async XLA Ops:
  0.6 25.2 %copy-start.2 = (bf16[512,128]{1,0:T(8,128)(2,1)S(1)}, bf16[512,128]{1,0:T(8,128)(2,1)}, u32[]{:S(2)}) copy-start(bf16[512,128]{1,0:T(8,128)(2,1)} %rest_5_.5) | copy-start | bytes 393220
  0.6 25.2 %copy-start.3 = (bf16[512,128]{1,0:T(8,128)(2,1)S(1)}, bf16[512,128]{1,0:T(8,128)(2,1)}, u32[]{:S(2)}) copy-start(bf16[512,128]{1,0:T(8,128)(2,1)} %rest_6_.5) | copy-start | bytes 393220
  0.7 19.4 %copy-start.5 = (s32[4,2]{0,1:T(2,128)S(1)}, s32[4,2]{0,1:T(2,128)}, u32[]{:S(2)}) copy-start(s32[4,2]{0,1:T(2,128)} %param.26) | copy-start | bytes 100
  2.4 23.5 %copy-start = (bf16[512,1024]{1,0:T(8,128)(2,1)S(1)}, bf16[512,1024]{1,0:T(8,128)(2,1)}, u32[]{:S(2)}) copy-start(bf16[512,1024]{1,0:T(8,128)(2,1)} %q_ref.5) | copy-start | bytes 3145732
  2.4 23.5 %copy-start.1 = (bf16[512,1024]{1,0:T(8,128)(2,1)S(1)}, bf16[512,1024]{1,0:T(8,128)(2,1)}, u32[]{:S(2)}) copy-start(bf16[512,1024]{1,0:T(8,128)(2,1)} %g_ref.5) | copy-start | bytes 3145732
  2.4 23.5 %copy-start.4 = (f32[512]{0:T(512)S(1)}, f32[512]{0:T(512)}, u32[]{:S(2)}) copy-start(f32[512]{0:T(512)} %param.27) | copy-start | bytes 6148
  2.4 17.7 %collective-permute-start.3 = (bf16[2,512,128]{2,1,0:T(8,128)(2,1)}, bf16[2,512,128]{2,1,0:T(8,128)(2,1)S(1)}, u32[]{:S(2)}, u32[]{:S(2)}) collective-permute-start(bf16[2,512,128]{2,1,0:T(8,128)(2,1)} %pad_maximum_fusion.2), channel_id=1, source_target_pairs={{0,4},{4,8},{8,12},{1,5},{5,9},{9,13},{2,6},{6,10},{10,14},{3,7},{... | collective-permute-start | bytes 786440 | tf_op jit(solution)/shard_map/ppermute | solution.py:27
  7.5 12.7 %collective-permute-start.2 = (bf16[2,512,128]{2,1,0:T(8,128)(2,1)}, bf16[2,512,128]{2,1,0:T(8,128)(2,1)}, u32[]{:S(2)}, u32[]{:S(2)}) collective-permute-start(bf16[2,512,128]{2,1,0:T(8,128)(2,1)} %pad_maximum_fusion.2), channel_id=1, source_target_pairs={{0,8},{1,9},{2,10},{3,11},{16,24},{17,25},{18,26},{19,27}} | collective-permute-start | bytes 786440 | tf_op jit(solution)/shard_map/ppermute | solution.py:282
  12.7 13.1 %collective-permute-start.1 = (bf16[2,512,128]{2,1,0:T(8,128)(2,1)}, bf16[2,512,128]{2,1,0:T(8,128)(2,1)}, u32[]{:S(2)}, u32[]{:S(2)}) collective-permute-start(bf16[2,512,128]{2,1,0:T(8,128)(2,1)} %pad_maximum_fusion.2), channel_id=1, source_target_pairs={{0,12},{1,13},{2,14},{3,15},{16,28},{17,29},{18,30},{19,31}} | collective-permute-start | bytes 786440 | tf_op jit(solution)/shard_map/ppermute | solution.py:282
  16.5 19.6 %collective-permute-start.4 = (bf16[1,1,8,128,128]{4,3,2,1,0:T(8,128)(2,1)}, bf16[1,1,8,128,128]{4,3,2,1,0:T(8,128)(2,1)S(1)}, u32[]{:S(2)}, u32[]{:S(2)}) collective-permute-start(bf16[1,1,8,128,128]{4,3,2,1,0:T(8,128)(2,1)} %get-tuple-element.113), channel_id=1, source_target_pairs={{0,4},{4,8},{8,12},{1,5},{5,9},{9,13},{2,6},{6,10},{10,14},{3,7},{... | collective-permute-start | bytes 786440 | tf_op jit(solution)/shard_map/ppermute | solution.py:27
  18.7 23.2 %collective-permute-start = (bf16[2,1,8,128,128]{4,3,2,1,0:T(8,128)(2,1)}, bf16[2,1,8,128,128]{4,3,2,1,0:T(8,128)(2,1)S(1)}, u32[]{:S(2)}, u32[]{:S(2)}) collective-permute-start(bf16[2,1,8,128,128]{4,3,2,1,0:T(8,128)(2,1)} %pad_maximum_fusion.1), channel_id=1, source_target_pairs={{0,4},{4,8},{8,12},{1,5},{5,9},{9,13},{2,6},{6,10},{10,14},{3,7},{... | collective-permute-start | bytes 1572872 | tf_op jit(solution)/shard_map/ppermute | solution.py:27
  47.7 8.3 %collective-permute-start.8 = (bf16[512,128]{1,0:T(8,128)(2,1)S(1)}, bf16[512,128]{1,0:T(8,128)(2,1)S(1)}, u32[]{:S(2)}, u32[]{:S(2)}) collective-permute-start(bf16[512,128]{1,0:T(8,128)(2,1)S(1)} %convert_element_type.43), channel_id=1, source_target_pairs={{4,0},{12,8},{5,1},{13,9},{6,2},{14,10},{7,3},{15,11},{20,16},{28,... | collective-permute-start | bytes 393224 | tf_op jit(solution)/shard_map/ppermute | solution.py:325
  49.0 9.1 %collective-permute-start.6 = (bf16[512,128]{1,0:T(8,128)(2,1)S(1)}, bf16[512,128]{1,0:T(8,128)(2,1)S(1)}, u32[]{:S(2)}, u32[]{:S(2)}) collective-permute-start(bf16[512,128]{1,0:T(8,128)(2,1)S(1)} %convert_element_type.38), channel_id=1, source_target_pairs={{4,0},{12,8},{5,1},{13,9},{6,2},{14,10},{7,3},{15,11},{20,16},{28,... | collective-permute-start | bytes 393224 | tf_op jit(solution)/shard_map/ppermute | solution.py:325
  50.3 10.7 %collective-permute-start.5 = (bf16[2,2,128,128]{3,2,1,0:T(8,128)(2,1)S(1)}, bf16[2,2,128,128]{3,2,1,0:T(8,128)(2,1)S(1)}, u32[]{:S(2)}, u32[]{:S(2)}) collective-permute-start(bf16[2,2,128,128]{3,2,1,0:T(8,128)(2,1)S(1)} %add_convert_fusion.2), channel_id=1, source_target_pairs={{4,0},{8,4},{12,8},{5,1},{9,5},{13,9},{6,2},{10,6},{14,10},{7,3},{... | collective-permute-start | bytes 393224 | tf_op jit(solution)/shard_map/ppermute | solution.py:27
  56.1 3.4 %collective-permute-start.10 = (f32[512]{0:T(512)S(1)}, f32[512]{0:T(512)S(1)}, u32[]{:S(2)}, u32[]{:S(2)}) collective-permute-start(f32[512]{0:T(512)S(1)} %bitcast.23), channel_id=1, source_target_pairs={{0,16},{16,0},{1,17},{17,1},{2,18},{18,2},{3,19},{19,3},{4,20},{20... | collective-permute-start | bytes 6152 | tf_op jit(solution)/shard_map/ppermute | solution.py:36
  56.2 12.2 %collective-permute-start.9 = (bf16[512,128]{1,0:T(8,128)(2,1)S(1)}, bf16[512,128]{1,0:T(8,128)(2,1)S(1)}, u32[]{:S(2)}, u32[]{:S(2)}) collective-permute-start(bf16[512,128]{1,0:T(8,128)(2,1)S(1)} %fusion.1), channel_id=1, source_target_pairs={{8,0},{9,1},{10,2},{11,3},{24,16},{25,17},{26,18},{27,19}} | collective-permute-start | bytes 393224 | tf_op jit(solution)/shard_map/ppermute | solution.py:325
  58.2 9.5 %collective-permute-start.7 = (bf16[512,128]{1,0:T(8,128)(2,1)S(1)}, bf16[512,128]{1,0:T(8,128)(2,1)S(1)}, u32[]{:S(2)}, u32[]{:S(2)}) collective-permute-start(bf16[512,128]{1,0:T(8,128)(2,1)S(1)} %fusion), channel_id=1, source_target_pairs={{8,0},{9,1},{10,2},{11,3},{24,16},{25,17},{26,18},{27,19}} | collective-permute-start | bytes 393224 | tf_op jit(solution)/shard_map/ppermute | solution.py:325
  59.5 3.7 %collective-permute-start.11 = (f32[512]{0:T(512)S(1)}, f32[512]{0:T(512)S(1)}, u32[]{:S(2)}, u32[]{:S(2)}) collective-permute-start(f32[512]{0:T(512)S(1)} %add.65), channel_id=1, source_target_pairs={{0,1},{1,0},{2,3},{3,2},{4,5},{5,4},{6,7},{7,6},{8,9},{9,8},{10,11... | collective-permute-start | bytes 6152 | tf_op jit(solution)/shard_map/ppermute | solution.py:36
  63.1 3.6 %collective-permute-start.12 = (f32[512]{0:T(512)S(1)}, f32[512]{0:T(512)S(1)}, u32[]{:S(2)}, u32[]{:S(2)}) collective-permute-start(f32[512]{0:T(512)S(1)} %add.66), channel_id=1, source_target_pairs={{0,2},{1,3},{2,0},{3,1},{4,6},{5,7},{6,4},{7,5},{8,10},{9,11},{10,... | collective-permute-start | bytes 6152 | tf_op jit(solution)/shard_map/ppermute | solution.py:36

commit v2 on v1

--- a/solution.py
+++ b/solution.py
@@ -14,6 +14,7 @@
 NGLOB = 4
 LEAD = WIN - 1
 FAN = 4
+CHUNK = 32
 LOG2E = math.log2(math.e)
 LN2 = math.log(2.0)
 NT = (((1,), (1,)), ((), ()))
@@ -54,7 +55,7 @@
     rest = rest[6:]
     if crossing:
         back_ref, rest = rest[0], rest[1:]
-    ds_scr, pb_scr = rest
+    ds_scr, pb_scr, s_scr, t_scr, u_scr = rest
     step = pl.program_id(0)
     block = first + step
     heads = q_ref.shape[1] // E
@@ -103,34 +104,56 @@
     low = jnp.float32(-1e9)
     loss = jnp.zeros((1, wide), F32)
 
-    def total(x):
+    def rows_pair(ref, pair):
+        ha, hb = 2 * pair, 2 * pair + 1
+        return jnp.concatenate([ref[:, ha * E:(ha + 1) * E], ref[:, hb * E:(hb + 1) * E]], axis=0)
+
+    def products(pair):
+        at = pair % 2
+        s_scr[at] = lax.dot_general(kcat, rows_pair(q_ref, pair), NT, preferred_element_type=F32)
+        u_scr[at] = lax.dot_general(vcat, rows_pair(g_ref, pair), NT, preferred_element_type=F32)
+
+    def fold(x, op):
+        return functools.reduce(op, [x[i:i + 8] for i in range(0, CHUNK, 8)])
+
+    def up(x):
         return jnp.sum(x, axis=0, keepdims=True)
 
+    products(0)
+    dk = dv = 0.0
     for pair in range(heads // 2):
+        at = pair % 2
+        if pair + 1 < heads // 2:
+            products(pair + 1)
         ha, hb = 2 * pair, 2 * pair + 1
-        q2 = jnp.concatenate([q_ref[:, ha * E:(ha + 1) * E], q_ref[:, hb * E:(hb + 1) * E]], axis=0)
-        g2 = jnp.concatenate([g_ref[:, ha * E:(ha + 1) * E], g_ref[:, hb * E:(hb + 1) * E]], axis=0)
-        s_all = lax.dot_general(kcat, q2, NT, preferred_element_type=F32)
-        pg_all = lax.dot_general(vcat, g2, NT, preferred_element_type=F32)
-        held, stats = [], []
+        stats = []
         for j in range(slots):
-            s = s_all[j * BLK:(j + 1) * BLK]
-            pg = pg_all[j * BLK:(j + 1) * BLK]
+            tile = slice(j * BLK, (j + 1) * BLK)
             t = jnp.concatenate([teacher_refs[j][0, 0, ha], teacher_refs[j][0, 0, hb]], axis=0)
             t = t.T.astype(F32)
             if j == 0:
-                s = jnp.where(causal, s, low)
                 t = jnp.where(causal, t, low)
-            m = jnp.max(s, axis=0, keepdims=True)
-            mt = jnp.max(t, axis=0, keepdims=True)
-            x = (s - m) * factor
-            y = (t - mt) * LOG2E
-            es = jnp.exp2(x)
-            et = jnp.exp2(y)
-            gap = y - x
-            u = pg + slope * gap
-            stats.append((m, mt, total(es), total(et), total(et * gap), total(es * gap), total(es * u)))
-            held.append((es, et, u))
+                s_scr[at, tile] = jnp.where(causal, s_scr[at, tile], low)
+            t_scr[at, tile] = t
+            chunks = [slice(k, k + CHUNK) for k in range(j * BLK, (j + 1) * BLK, CHUNK)]
+            m = functools.reduce(jnp.maximum, [fold(s_scr[at, c], jnp.maximum) for c in chunks])
+            mt = functools.reduce(jnp.maximum, [fold(t_scr[at, c], jnp.maximum) for c in chunks])
+            m = jnp.max(m, axis=0, keepdims=True)
+            mt = jnp.max(mt, axis=0, keepdims=True)
+            sums = None
+            for c in chunks:
+                x = (s_scr[at, c] - m) * factor
+                y = (t_scr[at, c] - mt) * LOG2E
+                es = jnp.exp2(x)
+                et = jnp.exp2(y)
+                gap = y - x
+                u = u_scr[at, c] + slope * gap
+                part = [fold(v, jnp.add) for v in (es, et, et * gap, es * gap, es * u)]
+                sums = part if sums is None else [v + w for v, w in zip(sums, part)]
+                s_scr[at, c] = es
+                t_scr[at, c] = et
+                u_scr[at, c] = u
+            stats.append((m, mt, *[up(v) for v in sums]))
         m = stats[0][0]
         mt = stats[0][1]
         for j in range(1, slots):
@@ -155,23 +178,29 @@
         )
         loss = loss + (w2 * LN2) * (rzt * fwd) + slope * (rz * rev)
         base = w2 - rz * mean_u
-        cols = pl.ds(pair * wide, wide)
+        cols = slice(pair * wide, (pair + 1) * wide)
         for j in range(slots):
-            es, et, u = held[j]
-            p = es * (fa[j] * rz)
-            ds = p * (u + (base + slope * off[j])) - et * (w2 * (fb[j] * rzt))
-            ds_scr[j * BLK:(j + 1) * BLK, cols] = ds.astype(BF)
-            pb_scr[j * BLK:(j + 1) * BLK, cols] = p.astype(BF)
+            to_p = fa[j] * rz
+            to_t = w2 * (fb[j] * rzt)
+            lift = base + slope * off[j]
+            for k in range(j * BLK, (j + 1) * BLK, CHUNK):
+                c = slice(k, k + CHUNK)
+                p = s_scr[at, c] * to_p
+                ds_scr[c, cols] = (p * (u_scr[at, c] + lift) - t_scr[at, c] * to_t).astype(BF)
+                pb_scr[c, cols] = p.astype(BF)
         dq_t = jnp.dot(kcat_t, ds_scr[:, cols], preferred_element_type=F32) * scale
         dq2 = dq_t.T.astype(BF)
         dq_ref[:, ha * E:(ha + 1) * E] = dq2[:BLK]
         dq_ref[:, hb * E:(hb + 1) * E] = dq2[BLK:]
+        if pair % 2 == 1 or pair + 1 == heads // 2:
+            first_pair = pair - pair % 2
+            cols = slice(first_pair * wide, (pair + 1) * wide)
+            q_part = jnp.concatenate([rows_pair(q_ref, n) for n in range(first_pair, pair + 1)], axis=0)
+            g_part = jnp.concatenate([rows_pair(g_ref, n) for n in range(first_pair, pair + 1)], axis=0)
+            dk = dk + jnp.dot(ds_scr[:, cols], q_part, preferred_element_type=F32)
+            dv = dv + jnp.dot(pb_scr[:, cols], g_part, preferred_element_type=F32)
     loss_ref[0] = loss[:, :BLK] + loss[:, BLK:]
-
-    q_all = jnp.concatenate([q_ref[:, h * E:(h + 1) * E] for h in range(heads)], axis=0)
-    g_all = jnp.concatenate([g_ref[:, h * E:(h + 1) * E] for h in range(heads)], axis=0)
-    dk = jnp.dot(ds_scr[...], q_all, preferred_element_type=F32) * scale
-    dv = jnp.dot(pb_scr[...], g_all, preferred_element_type=F32)
+    dk = dk * scale
     for d in range(WIN):
         part_k, part_v = dk[d * BLK:(d + 1) * BLK], dv[d * BLK:(d + 1) * BLK]
         if d in crossing:
@@ -247,7 +276,8 @@
             grid=(count,),
             in_specs=specs,
             out_specs=out_specs,
-            scratch_shapes=[pltpu.VMEM((slots * BLK, heads * BLK), BF)] * 2,
+            scratch_shapes=[pltpu.VMEM((slots * BLK, heads * BLK), BF)] * 2
+            + [pltpu.VMEM((2, slots * BLK, 2 * BLK), F32)] * 3,
         ),
         compiler_params=pltpu.CompilerParams(vmem_limit_bytes=48 * 1024 * 1024),
         cost_estimate=pl.CostEstimate(

time: 69.6 us -> 69.4 us (level)
  no operation moved by 1% of the time
where the time goes in v2:
time: 69.4 us; the launch traced here: 69 us
  starting transfers between devices  24.4 us (35%)
  Pallas kernels  21.5 us (31%)
  waiting for transfers between devices  14.1 us (20%)
  other arithmetic  5.94 us (9%)
  local copies, waits for them, and re-layouts  2.09 us (3%)
  between operations  0.91 us (1%)
    pallas_call x3, Pallas kernels, run_blocks(): pl.pallas_call(functools.partial(block_kernel, first, crossing, slots, ch...  21.5 us
    ppermute x4, starting transfers between devices, shift(): return lax.ppermute(block, axis, route)  8.96 us
    ppermute x2, starting transfers between devices, local(): more = lax.ppermute(known, 'seq', route)  7.16 us
    ppermute x2, waiting for transfers between devices, local(): more = lax.ppermute(known, 'seq', route)  5.69 us
    ppermute x4, starting transfers between devices, local(): came = [lax.ppermute(x, 'seq', route) for x in low]  5.17 us
    ppermute x4, waiting for transfers between devices, local(): came = [lax.ppermute(x, 'seq', route) for x in low]  4.34 us
    ppermute x3, waiting for transfers between devices, sum_over(): lax.ppermute(block, axis, [(i, i ^ step) for i in range(count)])  4.1 us
    ppermute x3, starting transfers between devices, sum_over(): lax.ppermute(block, axis, [(i, i ^ step) for i in range(count)])  3.14 us
  transfers between devices with their start and end apart: 13, of which 6 were waited for; matrix products, arithmetic and copies ran while one was open for 8% of the time, Pallas kernels for 23%

profile of v2, /device:TPU:0, one launch (start us, length us, event | category | flops | bytes accessed | tf_op | source)
XLA Modules:
  0.0 69.0 jit_solution(4973802411790402558)
XLA Ops:
  0.7 1.8 %pad_maximum_fusion.2 = bf16[2,512,128]{2,1,0:T(8,128)(2,1)} fusion(bf16[1,512,128]{2,1,0:T(8,128)(2,1)} %bitcast.16, bf16[1,512,128]{2,1,0:T(8,128)(2,1)} %bitcast.14), kind=kLoop, calls=%fused_computation.2 | loop fusion | flops 131072 | bytes 524288 | tf_op jit(solution)/shard_map/stack | solution.py:301
  2.4 5.1 %collective-permute-start.3 = (bf16[2,512,128]{2,1,0:T(8,128)(2,1)}, bf16[2,512,128]{2,1,0:T(8,128)(2,1)S(1)}, u32[]{:S(2)}, u32[]{:S(2)}) collective-permute-start(bf16[2,512,128]{2,1,0:T(8,128)(2,1)} %pad_maximum_fusion.2), channel_id=1, source_target_pairs={{0,4},{4,8},{8,12},{1,5},{5,9},{9,13},{2,6},{6,10},{10,14},{3,7},{... | collective-permute-start | bytes 786440 | tf_op jit(solution)/shard_map/ppermute | solution.py:28
  7.5 5.2 %collective-permute-start.2 = (bf16[2,512,128]{2,1,0:T(8,128)(2,1)}, bf16[2,512,128]{2,1,0:T(8,128)(2,1)}, u32[]{:S(2)}, u32[]{:S(2)}) collective-permute-start(bf16[2,512,128]{2,1,0:T(8,128)(2,1)} %pad_maximum_fusion.2), channel_id=1, source_target_pairs={{0,8},{1,9},{2,10},{3,11},{16,24},{17,25},{18,26},{19,27}} | collective-permute-start | bytes 786440 | tf_op jit(solution)/shard_map/ppermute | solution.py:312
  12.7 2.0 %collective-permute-start.1 = (bf16[2,512,128]{2,1,0:T(8,128)(2,1)}, bf16[2,512,128]{2,1,0:T(8,128)(2,1)}, u32[]{:S(2)}, u32[]{:S(2)}) collective-permute-start(bf16[2,512,128]{2,1,0:T(8,128)(2,1)} %pad_maximum_fusion.2), channel_id=1, source_target_pairs={{0,12},{1,13},{2,14},{3,15},{16,28},{17,29},{18,30},{19,31}} | collective-permute-start | bytes 786440 | tf_op jit(solution)/shard_map/ppermute | solution.py:312
  14.7 1.9 %fusion.2 = (bf16[1,1,8,128,128]{4,3,2,1,0:T(8,128)(2,1)S(1)}, bf16[1,1,8,128,128]{4,3,2,1,0:T(8,128)(2,1)}, bf16[1,1,8,128,128]{4,3,2,1,0:T(8,128)(2,1)S(1)}) fusion(bf16[4,3,8,128,128]{4,3,2,1,0:T(8,128)(2,1)} %rest_0_.5), kind=kLoop, calls=%fused_computation.18 | loop fusion | bytes 1572864 | tf_op jit(solution)/shard_map/slice | solution.py:321
  16.5 1.3 %collective-permute-start.4 = (bf16[1,1,8,128,128]{4,3,2,1,0:T(8,128)(2,1)}, bf16[1,1,8,128,128]{4,3,2,1,0:T(8,128)(2,1)S(1)}, u32[]{:S(2)}, u32[]{:S(2)}) collective-permute-start(bf16[1,1,8,128,128]{4,3,2,1,0:T(8,128)(2,1)} %get-tuple-element.113), channel_id=1, source_target_pairs={{0,4},{4,8},{8,12},{1,5},{5,9},{9,13},{2,6},{6,10},{10,14},{3,7},{... | collective-permute-start | bytes 786440 | tf_op jit(solution)/shard_map/ppermute | solution.py:28
  17.8 0.8 %pad_maximum_fusion.1 = bf16[2,1,8,128,128]{4,3,2,1,0:T(8,128)(2,1)} fusion(bf16[1,1,8,128,128]{4,3,2,1,0:T(8,128)(2,1)S(1)} %get-tuple-element.114, bf16[1,1,8,128,128]{4,3,2,1,0:T(8,128)(2,1)S(1)} %get-tuple-element.112), kind=kLoop, calls=%fused_computation.1 | loop fusion | flops 262144 | bytes 1048576 | tf_op jit(solution)/shard_map/concatenate | solution.py:320
  18.7 1.3 %collective-permute-start = (bf16[2,1,8,128,128]{4,3,2,1,0:T(8,128)(2,1)}, bf16[2,1,8,128,128]{4,3,2,1,0:T(8,128)(2,1)S(1)}, u32[]{:S(2)}, u32[]{:S(2)}) collective-permute-start(bf16[2,1,8,128,128]{4,3,2,1,0:T(8,128)(2,1)} %pad_maximum_fusion.1), channel_id=1, source_target_pairs={{0,4},{4,8},{8,12},{1,5},{5,9},{9,13},{2,6},{6,10},{10,14},{3,7},{... | collective-permute-start | bytes 1572872 | tf_op jit(solution)/shard_map/ppermute | solution.py:28
  20.0 0.1 copy.14.picks_ref
  20.1 0.0 collective-permute-done.2
  20.2 5.7 %collective-permute-done.1 = bf16[2,512,128]{2,1,0:T(8,128)(2,1)} collective-permute-done((bf16[2,512,128]{2,1,0:T(8,128)(2,1)}, bf16[2,512,128]{2,1,0:T(8,128)(2,1)}, u32[]{:S(2)}, u32[]{:S(2)}) %collective-permute-start.1) | collective-permute-done | bytes 262176 | tf_op jit(solution)/shard_map/ppermute | solution.py:312
  25.8 0.1 select_select_fusion
  26.0 10.0 %blocks_from_2.1 = (bf16[256,1024]{1,0:T(8,128)(2,1)S(1)}, f32[2,1,128]{2,1,0:T(1,128)S(1)}, f32[512,128]{1,0:T(8,128)S(1)}, f32[512,128]{1,0:T(8,128)S(1)}, f32...) custom-call(s32[1]{0:T(128)} %bitcast.base_ref, s32[4,2]{1,0:T(4,128)S(1)} %copy.14.picks_ref, bf16[512,1024]{1,0:T(8,128)(2,1)S(1)} %copy-done, ...), custom_call_target="tpu_custom_call" | custom-call | flops 1677721600 | bytes 3932160 | tf_op jit(solution)/shard_map/blocks_from_2/pallas_call | solution.py:271
  36.0 5.7 %blocks_from_1.1 = (bf16[128,1024]{1,0:T(8,128)(2,1)S(1)}, f32[1,1,128]{2,1,0:T(1,128)S(1)}, f32[512,128]{1,0:T(8,128)S(1)}, f32[512,128]{1,0:T(8,128)S(1)}, f32...) custom-call(s32[1]{0:T(128)} %bitcast.base_ref, s32[4,2]{1,0:T(4,128)S(1)} %copy.14.picks_ref, ...), custom_call_target="tpu_custom_call" | custom-call | flops 838860800 | bytes 1966080 | tf_op jit(solution)/shard_map/blocks_from_1/pallas_call | solution.py:271
  41.8 5.7 %blocks_from_0.1 = (bf16[128,1024]{1,0:T(8,128)(2,1)S(1)}, f32[1,1,128]{2,1,0:T(1,128)S(1)}, f32[512,128]{1,0:T(8,128)S(1)}, f32[512,128]{1,0:T(8,128)S(1)}, f32...) custom-call(s32[1]{0:T(128)} %bitcast.base_ref, s32[4,2]{1,0:T(4,128)S(1)} %copy.14.picks_ref, ...), custom_call_target="tpu_custom_call" | custom-call | flops 838860800 | bytes 1966080 | tf_op jit(solution)/shard_map/blocks_from_0/pallas_call | solution.py:271
  47.6 1.3 %collective-permute-start.8 = (bf16[512,128]{1,0:T(8,128)(2,1)S(1)}, bf16[512,128]{1,0:T(8,128)(2,1)S(1)}, u32[]{:S(2)}, u32[]{:S(2)}) collective-permute-start(bf16[512,128]{1,0:T(8,128)(2,1)S(1)} %convert_element_type.43), channel_id=1, source_target_pairs={{4,0},{12,8},{5,1},{13,9},{6,2},{14,10},{7,3},{15,11},{20,16},{28,... | collective-permute-start | bytes 393224 | tf_op jit(solution)/shard_map/ppermute | solution.py:355
  48.9 1.3 %collective-permute-start.6 = (bf16[512,128]{1,0:T(8,128)(2,1)S(1)}, bf16[512,128]{1,0:T(8,128)(2,1)S(1)}, u32[]{:S(2)}, u32[]{:S(2)}) collective-permute-start(bf16[512,128]{1,0:T(8,128)(2,1)S(1)} %convert_element_type.38), channel_id=1, source_target_pairs={{4,0},{12,8},{5,1},{13,9},{6,2},{14,10},{7,3},{15,11},{20,16},{28,... | collective-permute-start | bytes 393224 | tf_op jit(solution)/shard_map/ppermute | solution.py:355
  50.2 1.3 %collective-permute-start.5 = (bf16[2,2,128,128]{3,2,1,0:T(8,128)(2,1)S(1)}, bf16[2,2,128,128]{3,2,1,0:T(8,128)(2,1)S(1)}, u32[]{:S(2)}, u32[]{:S(2)}) collective-permute-start(bf16[2,2,128,128]{3,2,1,0:T(8,128)(2,1)S(1)} %add_convert_fusion.2), channel_id=1, source_target_pairs={{4,0},{8,4},{12,8},{5,1},{9,5},{13,9},{6,2},{10,6},{14,10},{7,3},{... | collective-permute-start | bytes 393224 | tf_op jit(solution)/shard_map/ppermute | solution.py:28
  51.5 1.0 %pad_maximum_fusion = bf16[512,1024]{1,0:T(8,128)(2,1)} fusion(bf16[256,1024]{1,0:T(8,128)(2,1)S(1)} %get-tuple-element.100, bf16[128,1024]{1,0:T(8,128)(2,1)S(1)} %get-tuple-element.99, bf16[128,1024]{1,0:T(8,128)(2,1)S(1)} %get-tuple-element.98), kind=kLoop, calls=%fused_computation | loop fusion | flops 3145728 | bytes 2097152 | tf_op jit(solution)/shard_map/concatenate | solution.py:340
  52.6 3.3 %collective-permute-done.8 = bf16[512,128]{1,0:T(8,128)(2,1)S(1)} collective-permute-done((bf16[512,128]{1,0:T(8,128)(2,1)S(1)}, bf16[512,128]{1,0:T(8,128)(2,1)S(1)}, u32[]{:S(2)}, u32[]{:S(2)}) %collective-permute-start.8) | collective-permute-done | bytes 131104 | tf_op jit(solution)/shard_map/ppermute | solution.py:355
  55.9 0.1 collective-permute-start.10
  56.0 1.3 %collective-permute-start.9 = (bf16[512,128]{1,0:T(8,128)(2,1)S(1)}, bf16[512,128]{1,0:T(8,128)(2,1)S(1)}, u32[]{:S(2)}, u32[]{:S(2)}) collective-permute-start(bf16[512,128]{1,0:T(8,128)(2,1)S(1)} %fusion.1), channel_id=1, source_target_pairs={{8,0},{9,1},{10,2},{11,3},{24,16},{25,17},{26,18},{27,19}} | collective-permute-start | bytes 393224 | tf_op jit(solution)/shard_map/ppermute | solution.py:355
  57.3 0.8 %collective-permute-done.6 = bf16[512,128]{1,0:T(8,128)(2,1)S(1)} collective-permute-done((bf16[512,128]{1,0:T(8,128)(2,1)S(1)}, bf16[512,128]{1,0:T(8,128)(2,1)S(1)}, u32[]{:S(2)}, u32[]{:S(2)}) %collective-permute-start.6) | collective-permute-done | bytes 131104 | tf_op jit(solution)/shard_map/ppermute | solution.py:355
  58.1 1.3 %collective-permute-start.7 = (bf16[512,128]{1,0:T(8,128)(2,1)S(1)}, bf16[512,128]{1,0:T(8,128)(2,1)S(1)}, u32[]{:S(2)}, u32[]{:S(2)}) collective-permute-start(bf16[512,128]{1,0:T(8,128)(2,1)S(1)} %fusion), channel_id=1, source_target_pairs={{8,0},{9,1},{10,2},{11,3},{24,16},{25,17},{26,18},{27,19}} | collective-permute-start | bytes 393224 | tf_op jit(solution)/shard_map/ppermute | solution.py:355
  59.5 1.6 %collective-permute-start.11 = (f32[512]{0:T(512)S(1)}, f32[512]{0:T(512)S(1)}, u32[]{:S(2)}, u32[]{:S(2)}) collective-permute-start(f32[512]{0:T(512)S(1)} %add.65), channel_id=1, source_target_pairs={{0,1},{1,0},{2,3},{3,2},{4,5},{5,4},{6,7},{7,6},{8,9},{9,8},{10,11... | collective-permute-start | bytes 6152 | tf_op jit(solution)/shard_map/ppermute | solution.py:37
  61.0 2.1 %collective-permute-done.11 = f32[512]{0:T(512)S(1)} collective-permute-done((f32[512]{0:T(512)S(1)}, f32[512]{0:T(512)S(1)}, u32[]{:S(2)}, u32[]{:S(2)}) %collective-permute-start.11) | collective-permute-done | bytes 2080 | tf_op jit(solution)/shard_map/ppermute | solution.py:37
  63.1 1.5 %collective-permute-start.12 = (f32[512]{0:T(512)S(1)}, f32[512]{0:T(512)S(1)}, u32[]{:S(2)}, u32[]{:S(2)}) collective-permute-start(f32[512]{0:T(512)S(1)} %add.66), channel_id=1, source_target_pairs={{0,2},{1,3},{2,0},{3,1},{4,6},{5,7},{6,4},{7,5},{8,10},{9,11},{10,... | collective-permute-start | bytes 6152 | tf_op jit(solution)/shard_map/ppermute | solution.py:37
  64.7 2.0 %collective-permute-done.12 = f32[512]{0:T(512)S(1)} collective-permute-done((f32[512]{0:T(512)S(1)}, f32[512]{0:T(512)S(1)}, u32[]{:S(2)}, u32[]{:S(2)}) %collective-permute-start.12) | collective-permute-done | bytes 2080 | tf_op jit(solution)/shard_map/ppermute | solution.py:37
  66.7 0.6 add.67
  67.3 0.2 collective-permute-done.7
  67.5 0.7 %add_convert_fusion.1 = bf16[512,128]{1,0:T(8,128)(2,1)} fusion(f32[512,128]{1,0:T(8,128)S(1)} %get-tuple-element.122, bf16[512,128]{1,0:T(8,128)(2,1)S(1)} %collective-permute-done.7, f32[512,128]{1,0:T(8,128)S(1)} %get-tuple-element.104, bf16[512,128]{1,0:T(8,128)(2,1)S(1)} %collective-permute-done.6, pred[]{:T(512)S(6)} %eq.2), kind=kLoop, calls=%fused_computation.5 | loop fusion | flops 458752 | bytes 917505 | tf_op jit(solution)/shard_map/convert_element_type | solution.py:364
  68.2 0.7 %add_convert_fusion = bf16[512,128]{1,0:T(8,128)(2,1)} fusion(f32[512,128]{1,0:T(8,128)S(1)} %get-tuple-element.121, bf16[512,128]{1,0:T(8,128)(2,1)S(1)} %collective-permute-done.9, f32[512,128]{1,0:T(8,128)S(1)} %get-tuple-element.106, bf16[512,128]{1,0:T(8,128)(2,1)S(1)} %collective-permute-done.8, pred[]{:T(512)S(6)} %eq.2), kind=kLoop, calls=%fused_computation.3 | loop fusion | flops 458752 | bytes 917505 | tf_op jit(solution)/shard_map/convert_element_type | solution.py:364
  (31 shorter events, 0.3 us)
Async XLA Ops:
  0.6 25.2 %copy-start.2 = (bf16[512,128]{1,0:T(8,128)(2,1)S(1)}, bf16[512,128]{1,0:T(8,128)(2,1)}, u32[]{:S(2)}) copy-start(bf16[512,128]{1,0:T(8,128)(2,1)} %rest_5_.5) | copy-start | bytes 393220
  0.6 25.2 %copy-start.3 = (bf16[512,128]{1,0:T(8,128)(2,1)S(1)}, bf16[512,128]{1,0:T(8,128)(2,1)}, u32[]{:S(2)}) copy-start(bf16[512,128]{1,0:T(8,128)(2,1)} %rest_6_.5) | copy-start | bytes 393220
  0.7 19.4 %copy-start.5 = (s32[4,2]{0,1:T(2,128)S(1)}, s32[4,2]{0,1:T(2,128)}, u32[]{:S(2)}) copy-start(s32[4,2]{0,1:T(2,128)} %param.26) | copy-start | bytes 100
  2.4 23.5 %copy-start = (bf16[512,1024]{1,0:T(8,128)(2,1)S(1)}, bf16[512,1024]{1,0:T(8,128)(2,1)}, u32[]{:S(2)}) copy-start(bf16[512,1024]{1,0:T(8,128)(2,1)} %q_ref.5) | copy-start | bytes 3145732
  2.4 23.5 %copy-start.1 = (bf16[512,1024]{1,0:T(8,128)(2,1)S(1)}, bf16[512,1024]{1,0:T(8,128)(2,1)}, u32[]{:S(2)}) copy-start(bf16[512,1024]{1,0:T(8,128)(2,1)} %g_ref.5) | copy-start | bytes 3145732
  2.4 23.5 %copy-start.4 = (f32[512]{0:T(512)S(1)}, f32[512]{0:T(512)}, u32[]{:S(2)}) copy-start(f32[512]{0:T(512)} %param.27) | copy-start | bytes 6148
  2.4 17.7 %collective-permute-start.3 = (bf16[2,512,128]{2,1,0:T(8,128)(2,1)}, bf16[2,512,128]{2,1,0:T(8,128)(2,1)S(1)}, u32[]{:S(2)}, u32[]{:S(2)}) collective-permute-start(bf16[2,512,128]{2,1,0:T(8,128)(2,1)} %pad_maximum_fusion.2), channel_id=1, source_target_pairs={{0,4},{4,8},{8,12},{1,5},{5,9},{9,13},{2,6},{6,10},{10,14},{3,7},{... | collective-permute-start | bytes 786440 | tf_op jit(solution)/shard_map/ppermute | solution.py:28
  7.5 12.7 %collective-permute-start.2 = (bf16[2,512,128]{2,1,0:T(8,128)(2,1)}, bf16[2,512,128]{2,1,0:T(8,128)(2,1)}, u32[]{:S(2)}, u32[]{:S(2)}) collective-permute-start(bf16[2,512,128]{2,1,0:T(8,128)(2,1)} %pad_maximum_fusion.2), channel_id=1, source_target_pairs={{0,8},{1,9},{2,10},{3,11},{16,24},{17,25},{18,26},{19,27}} | collective-permute-start | bytes 786440 | tf_op jit(solution)/shard_map/ppermute | solution.py:312
  12.7 13.1 %collective-permute-start.1 = (bf16[2,512,128]{2,1,0:T(8,128)(2,1)}, bf16[2,512,128]{2,1,0:T(8,128)(2,1)}, u32[]{:S(2)}, u32[]{:S(2)}) collective-permute-start(bf16[2,512,128]{2,1,0:T(8,128)(2,1)} %pad_maximum_fusion.2), channel_id=1, source_target_pairs={{0,12},{1,13},{2,14},{3,15},{16,28},{17,29},{18,30},{19,31}} | collective-permute-start | bytes 786440 | tf_op jit(solution)/shard_map/ppermute | solution.py:312
  16.5 19.5 %collective-permute-start.4 = (bf16[1,1,8,128,128]{4,3,2,1,0:T(8,128)(2,1)}, bf16[1,1,8,128,128]{4,3,2,1,0:T(8,128)(2,1)S(1)}, u32[]{:S(2)}, u32[]{:S(2)}) collective-permute-start(bf16[1,1,8,128,128]{4,3,2,1,0:T(8,128)(2,1)} %get-tuple-element.113), channel_id=1, source_target_pairs={{0,4},{4,8},{8,12},{1,5},{5,9},{9,13},{2,6},{6,10},{10,14},{3,7},{... | collective-permute-start | bytes 786440 | tf_op jit(solution)/shard_map/ppermute | solution.py:28
  18.7 23.1 %collective-permute-start = (bf16[2,1,8,128,128]{4,3,2,1,0:T(8,128)(2,1)}, bf16[2,1,8,128,128]{4,3,2,1,0:T(8,128)(2,1)S(1)}, u32[]{:S(2)}, u32[]{:S(2)}) collective-permute-start(bf16[2,1,8,128,128]{4,3,2,1,0:T(8,128)(2,1)} %pad_maximum_fusion.1), channel_id=1, source_target_pairs={{0,4},{4,8},{8,12},{1,5},{5,9},{9,13},{2,6},{6,10},{10,14},{3,7},{... | collective-permute-start | bytes 1572872 | tf_op jit(solution)/shard_map/ppermute | solution.py:28
  47.6 8.3 %collective-permute-start.8 = (bf16[512,128]{1,0:T(8,128)(2,1)S(1)}, bf16[512,128]{1,0:T(8,128)(2,1)S(1)}, u32[]{:S(2)}, u32[]{:S(2)}) collective-permute-start(bf16[512,128]{1,0:T(8,128)(2,1)S(1)} %convert_element_type.43), channel_id=1, source_target_pairs={{4,0},{12,8},{5,1},{13,9},{6,2},{14,10},{7,3},{15,11},{20,16},{28,... | collective-permute-start | bytes 393224 | tf_op jit(solution)/shard_map/ppermute | solution.py:355
  48.9 9.2 %collective-permute-start.6 = (bf16[512,128]{1,0:T(8,128)(2,1)S(1)}, bf16[512,128]{1,0:T(8,128)(2,1)S(1)}, u32[]{:S(2)}, u32[]{:S(2)}) collective-permute-start(bf16[512,128]{1,0:T(8,128)(2,1)S(1)} %convert_element_type.38), channel_id=1, source_target_pairs={{4,0},{12,8},{5,1},{13,9},{6,2},{14,10},{7,3},{15,11},{20,16},{28,... | collective-permute-start | bytes 393224 | tf_op jit(solution)/shard_map/ppermute | solution.py:355
  50.2 10.8 %collective-permute-start.5 = (bf16[2,2,128,128]{3,2,1,0:T(8,128)(2,1)S(1)}, bf16[2,2,128,128]{3,2,1,0:T(8,128)(2,1)S(1)}, u32[]{:S(2)}, u32[]{:S(2)}) collective-permute-start(bf16[2,2,128,128]{3,2,1,0:T(8,128)(2,1)S(1)} %add_convert_fusion.2), channel_id=1, source_target_pairs={{4,0},{8,4},{12,8},{5,1},{9,5},{13,9},{6,2},{10,6},{14,10},{7,3},{... | collective-permute-start | bytes 393224 | tf_op jit(solution)/shard_map/ppermute | solution.py:28
  55.9 3.5 %collective-permute-start.10 = (f32[512]{0:T(512)S(1)}, f32[512]{0:T(512)S(1)}, u32[]{:S(2)}, u32[]{:S(2)}) collective-permute-start(f32[512]{0:T(512)S(1)} %bitcast.23), channel_id=1, source_target_pairs={{0,16},{16,0},{1,17},{17,1},{2,18},{18,2},{3,19},{19,3},{4,20},{20... | collective-permute-start | bytes 6152 | tf_op jit(solution)/shard_map/ppermute | solution.py:37
  56.0 12.2 %collective-permute-start.9 = (bf16[512,128]{1,0:T(8,128)(2,1)S(1)}, bf16[512,128]{1,0:T(8,128)(2,1)S(1)}, u32[]{:S(2)}, u32[]{:S(2)}) collective-permute-start(bf16[512,128]{1,0:T(8,128)(2,1)S(1)} %fusion.1), channel_id=1, source_target_pairs={{8,0},{9,1},{10,2},{11,3},{24,16},{25,17},{26,18},{27,19}} | collective-permute-start | bytes 393224 | tf_op jit(solution)/shard_map/ppermute | solution.py:355
  58.1 9.4 %collective-permute-start.7 = (bf16[512,128]{1,0:T(8,128)(2,1)S(1)}, bf16[512,128]{1,0:T(8,128)(2,1)S(1)}, u32[]{:S(2)}, u32[]{:S(2)}) collective-permute-start(bf16[512,128]{1,0:T(8,128)(2,1)S(1)} %fusion), channel_id=1, source_target_pairs={{8,0},{9,1},{10,2},{11,3},{24,16},{25,17},{26,18},{27,19}} | collective-permute-start | bytes 393224 | tf_op jit(solution)/shard_map/ppermute | solution.py:355
  59.5 3.7 %collective-permute-start.11 = (f32[512]{0:T(512)S(1)}, f32[512]{0:T(512)S(1)}, u32[]{:S(2)}, u32[]{:S(2)}) collective-permute-start(f32[512]{0:T(512)S(1)} %add.65), channel_id=1, source_target_pairs={{0,1},{1,0},{2,3},{3,2},{4,5},{5,4},{6,7},{7,6},{8,9},{9,8},{10,11... | collective-permute-start | bytes 6152 | tf_op jit(solution)/shard_map/ppermute | solution.py:37
  63.1 3.6 %collective-permute-start.12 = (f32[512]{0:T(512)S(1)}, f32[512]{0:T(512)S(1)}, u32[]{:S(2)}, u32[]{:S(2)}) collective-permute-start(f32[512]{0:T(512)S(1)} %add.66), channel_id=1, source_target_pairs={{0,2},{1,3},{2,0},{3,1},{4,6},{5,7},{6,4},{7,5},{8,10},{9,11},{10,... | collective-permute-start | bytes 6152 | tf_op jit(solution)/shard_map/ppermute | solution.py:37

commit v3 on v2

--- a/solution.py
+++ b/solution.py
@@ -101,6 +101,8 @@
     key_id = lax.broadcasted_iota(jnp.int32, (BLK, wide), 0)
     row_id = lax.broadcasted_iota(jnp.int32, (BLK, wide), 1) & (BLK - 1)
     causal = key_id <= row_id
+    square = (BLK, BLK)
+    unit = (lax.broadcasted_iota(jnp.int32, square, 0) == lax.broadcasted_iota(jnp.int32, square, 1)).astype(F32).astype(BF)
     low = jnp.float32(-1e9)
     loss = jnp.zeros((1, wide), F32)
 
@@ -130,7 +132,7 @@
         for j in range(slots):
             tile = slice(j * BLK, (j + 1) * BLK)
             t = jnp.concatenate([teacher_refs[j][0, 0, ha], teacher_refs[j][0, 0, hb]], axis=0)
-            t = t.T.astype(F32)
+            t = lax.dot_general(unit, t, NT, preferred_element_type=F32)
             if j == 0:
                 t = jnp.where(causal, t, low)
                 s_scr[at, tile] = jnp.where(causal, s_scr[at, tile], low)
@@ -221,6 +223,53 @@
         dsv_ref[pl.ds(at, BLK), :] += dv[j * BLK:(j + 1) * BLK]
 
 
+def pack_kernel(*refs):
+    out = refs[-1]
+    for i, ref in enumerate(refs[:-1]):
+        out[i] = ref[...]
+
+
+def pack(arrays):
+    shape = arrays[0].shape
+    return pl.pallas_call(
+        pack_kernel,
+        out_shape=jax.ShapeDtypeStruct((len(arrays), *shape), arrays[0].dtype),
+        compiler_params=pltpu.CompilerParams(vmem_limit_bytes=16 * 1024 * 1024),
+        name="pack",
+    )(*arrays)
+
+
+def finish_kernel(root_ref, dk_ref, dv_ref, dsk_ref, dsv_ref, back_ref, *rest):
+    came, (kg_ref, vg_ref) = rest[:-2], rest[-2:]
+    root = root_ref[0] == 0
+    tokens = dk_ref.shape[0]
+    for which, (own, sink, out) in enumerate(((dk_ref, dsk_ref, kg_ref), (dv_ref, dsv_ref, vg_ref))):
+        for block in range(tokens // BLK):
+            rows = slice(block * BLK, (block + 1) * BLK)
+            value = own[rows]
+            late = block - (tokens // BLK - LEAD)
+            if late >= 0:
+                value = value + back_ref[which, late].astype(F32)
+            if block < NGLOB:
+                extra = sink[rows]
+                for arrived in came[which::2]:
+                    extra = extra + arrived[rows].astype(F32)
+                value = value + jnp.where(root, extra, 0.0)
+            out[rows] = value.astype(BF)
+
+
+def finish(root, dk, dv, dsk, dsv, back, came):
+    vmem = pl.BlockSpec(memory_space=pltpu.VMEM)
+    return pl.pallas_call(
+        finish_kernel,
+        out_shape=[jax.ShapeDtypeStruct(dk.shape, BF)] * 2,
+        in_specs=[pl.BlockSpec(memory_space=pltpu.SMEM)] + [vmem] * (5 + len(came)),
+        out_specs=[vmem] * 2,
+        compiler_params=pltpu.CompilerParams(vmem_limit_bytes=16 * 1024 * 1024),
+        name="finish",
+    )(root, dk, dv, dsk, dsv, back, *came)
+
+
 def run_blocks(first, count, base, picks, queries, out_grad, window, incoming, glob, own, sinks, weights,
                before, acc):
     crossing = [d for d in range(WIN) if d > first]
@@ -298,7 +347,7 @@
 
     tail = slice(tokens - LEAD * BLK, tokens)
     first_rows = slice(0, NGLOB * BLK)
-    pair = jnp.stack([key_rows, values])
+    pair = pack([key_rows, values])
     got = shift(pair, "seq", 1)
     before = got[:, tail].reshape(2, LEAD, BLK, E)
     sinks = jnp.where(where == 0, pair[:, first_rows], got[:, first_rows])
@@ -348,20 +397,18 @@
         steps.append([(i, i - reach) for i in range(reach, count, 2 * reach)])
         reach *= 2
     returned = None
+    arrived = []
     for number, route in enumerate(steps):
         low = [x.astype(BF) for x in sums]
-        if number == 1:
-            row_terms, low[1] = lax.optimization_barrier((row_terms, low[1]))
         came = [lax.ppermute(x, "seq", route) for x in low]
         if number == 0:
-            returned = shift(back.astype(BF), "seq", -1).astype(F32)
+            returned = shift(back.astype(BF), "seq", -1)
         sums = [x + y.astype(F32) for x, y in zip(sums, came)]
+        arrived += came
+    row_terms, returned = lax.optimization_barrier((row_terms, returned))
     row_loss = sum_over(sum_over(row_terms, "grp"), "head")
-    grads = []
-    for which, own_sum in enumerate((dk, dv)):
-        whole = own_sum.at[tail].add(returned[which].reshape(LEAD * BLK, E))
-        whole = whole.at[first_rows].add(jnp.where(where == 0, sums[which], 0.0))
-        grads.append(whole.astype(BF))
+    root = where.astype(jnp.int32).reshape(1)
+    grads = finish(root, dk, dv, dsk, dsv, returned, arrived)
     return (query_grad, grads[0], grads[1], row_loss)
 
 

time: 69.4 us -> 72.4 us (1.043)
  other arithmetic: 5.94 us -> 2.67 us
  Pallas kernels: 21.5 us -> 23.6 us
  local copies, waits for them, and re-layouts: 2.09 us -> 4.19 us
  waiting for transfers between devices: 14.1 us -> 15.4 us
  starting transfers between devices: 24.4 us -> 25.2 us
    ppermute x4, waiting for transfers between devices: 0.01 us -> 4.37 us  [shift(): return lax.ppermute(block, axis, route)]
    ppermute x3, waiting for transfers between devices: 4.1 us -> 1.78 us  [sum_over(): lax.ppermute(block, axis, [(i, i ^ step) for i in range(count)])]
    unnamed x13 -> x17, local copies, waits for them, and re-layouts: 0.12 us -> 1.93 us
    another operation x1 -> x0, other arithmetic: 1.75 us -> none  [local(): pair = jnp.stack([key_rows, values])]
    convert_element_type x3 -> x1, other arithmetic: 1.5 us -> 0.03 us  [local(): returned = shift(back.astype(BF), 'seq', -1)]
    pallas_call x3, Pallas kernels: 21.5 us -> 22.7 us  [run_blocks(): pl.pallas_call(functools.partial(block_kernel, first, crossing, slots, ch...]
    slice x1, local copies, waits for them, and re-layouts: 0.04 us -> 1.07 us  [local(): incoming[block] = {d: came[i:i + 1] for i, d in enumerate(offsets)}]
    pallas_call x0 -> x2, Pallas kernels: none -> 0.83 us  [the longest x1 0.81 us: finish(): pl.pallas_call(finish_kernel, out_shape=[jax.ShapeDtypeStruct(dk.shape, B...]
  transfers between devices with their start and end apart: 13 -> 13, of which waited for: 6 -> 7; matrix products, arithmetic and copies ran while one was open for 8% -> 5% of each run, Pallas kernels for 23% -> 23%
where the time goes in v3:
time: 72.4 us; the launch traced here: 71.9 us
  starting transfers between devices  25.2 us (35%)
  Pallas kernels  23.6 us (33%)
  waiting for transfers between devices  15.4 us (21%)
  local copies, waits for them, and re-layouts  4.19 us (6%)
  other arithmetic  2.67 us (4%)
  between operations  0.91 us (1%)
    pallas_call x3, Pallas kernels, run_blocks(): pl.pallas_call(functools.partial(block_kernel, first, crossing, slots, ch...  22.7 us
    ppermute x4, starting transfers between devices, shift(): return lax.ppermute(block, axis, route)  9.77 us
    ppermute x2, starting transfers between devices, local(): more = lax.ppermute(known, 'seq', route)  7.18 us
    ppermute x2, waiting for transfers between devices, local(): more = lax.ppermute(known, 'seq', route)  5.3 us
    ppermute x4, starting transfers between devices, local(): came = [lax.ppermute(x, 'seq', route) for x in low]  5.17 us
    ppermute x4, waiting for transfers between devices, shift(): return lax.ppermute(block, axis, route)  4.37 us
    ppermute x4, waiting for transfers between devices, local(): came = [lax.ppermute(x, 'seq', route) for x in low]  3.96 us
    ppermute x3, starting transfers between devices, sum_over(): lax.ppermute(block, axis, [(i, i ^ step) for i in range(count)])  3.08 us
  transfers between devices with their start and end apart: 13, of which 7 were waited for; matrix products, arithmetic and copies ran while one was open for 5% of the time, Pallas kernels for 23%

profile of v3, /device:TPU:0, one launch (start us, length us, event | category | flops | bytes accessed | tf_op | source)
XLA Modules:
  0.0 71.9 jit_solution(12351171785144784491)
XLA Ops:
  0.6 0.9 %copy-done.2 = bf16[512,128]{1,0:T(8,128)(2,1)S(1)} copy-done((bf16[512,128]{1,0:T(8,128)(2,1)S(1)}, bf16[512,128]{1,0:T(8,128)(2,1)}, u32[]{:S(2)}) %copy-start.2) | copy-done | bytes 131096
  1.5 0.9 %copy-done.4 = bf16[512,128]{1,0:T(8,128)(2,1)S(1)} copy-done((bf16[512,128]{1,0:T(8,128)(2,1)S(1)}, bf16[512,128]{1,0:T(8,128)(2,1)}, u32[]{:S(2)}) %copy-start.4) | copy-done | bytes 131096
  2.5 5.1 %collective-permute-start.3 = (bf16[2,512,128]{2,1,0:T(8,128)(2,1)S(1)}, bf16[2,512,128]{2,1,0:T(8,128)(2,1)S(1)}, u32[]{:S(2)}, u32[]{:S(2)}) collective-permute-start(bf16[2,512,128]{2,1,0:T(8,128)(2,1)S(1)} %pack.1), channel_id=1, source_target_pairs={{0,4},{4,8},{8,12},{1,5},{5,9},{9,13},{2,6},{6,10},{10,14},{3,7},{... | collective-permute-start | bytes 786440 | tf_op jit(solution)/shard_map/ppermute | solution.py:28
  7.6 5.2 %collective-permute-start.2 = (bf16[2,512,128]{2,1,0:T(8,128)(2,1)S(1)}, bf16[2,512,128]{2,1,0:T(8,128)(2,1)}, u32[]{:S(2)}, u32[]{:S(2)}) collective-permute-start(bf16[2,512,128]{2,1,0:T(8,128)(2,1)S(1)} %pack.1), channel_id=1, source_target_pairs={{0,8},{1,9},{2,10},{3,11},{16,24},{17,25},{18,26},{19,27}} | collective-permute-start | bytes 786440 | tf_op jit(solution)/shard_map/ppermute | solution.py:361
  12.8 2.0 %collective-permute-start.1 = (bf16[2,512,128]{2,1,0:T(8,128)(2,1)S(1)}, bf16[2,512,128]{2,1,0:T(8,128)(2,1)}, u32[]{:S(2)}, u32[]{:S(2)}) collective-permute-start(bf16[2,512,128]{2,1,0:T(8,128)(2,1)S(1)} %pack.1), channel_id=1, source_target_pairs={{0,12},{1,13},{2,14},{3,15},{16,28},{17,29},{18,30},{19,31}} | collective-permute-start | bytes 786440 | tf_op jit(solution)/shard_map/ppermute | solution.py:361
  14.8 1.2 %fusion = (bf16[1,1,8,128,128]{4,3,2,1,0:T(8,128)(2,1)S(1)}, bf16[1,1,8,128,128]{4,3,2,1,0:T(8,128)(2,1)S(1)}, bf16[1,1,8,128,128]{4,3,2,1,0:T(8,128)(2,1)S(1)}) fusion(bf16[4,3,8,128,128]{4,3,2,1,0:T(8,128)(2,1)} %rest_0_.5), kind=kLoop, calls=%fused_computation.9 | loop fusion | bytes 1572864 | tf_op jit(solution)/shard_map/slice | solution.py:370
  16.0 1.3 %collective-permute-start.4 = (bf16[1,1,8,128,128]{4,3,2,1,0:T(8,128)(2,1)S(1)}, bf16[1,1,8,128,128]{4,3,2,1,0:T(8,128)(2,1)S(1)}, u32[]{:S(2)}, u32[]{:S(2)}) collective-permute-start(bf16[1,1,8,128,128]{4,3,2,1,0:T(8,128)(2,1)S(1)} %get-tuple-element.53), channel_id=1, source_target_pairs={{0,4},{4,8},{8,12},{1,5},{5,9},{9,13},{2,6},{6,10},{10,14},{3,7},{... | collective-permute-start | bytes 786440 | tf_op jit(solution)/shard_map/ppermute | solution.py:28
  17.3 0.8 %pad_maximum_fusion.1 = bf16[2,1,8,128,128]{4,3,2,1,0:T(8,128)(2,1)} fusion(bf16[1,1,8,128,128]{4,3,2,1,0:T(8,128)(2,1)S(1)} %get-tuple-element.54, bf16[1,1,8,128,128]{4,3,2,1,0:T(8,128)(2,1)S(1)} %get-tuple-element.52), kind=kLoop, calls=%fused_computation.1 | loop fusion | flops 262144 | bytes 1048576 | tf_op jit(solution)/shard_map/concatenate | solution.py:369
  18.1 2.1 %collective-permute-start = (bf16[2,1,8,128,128]{4,3,2,1,0:T(8,128)(2,1)}, bf16[2,1,8,128,128]{4,3,2,1,0:T(8,128)(2,1)}, u32[]{:S(2)}, u32[]{:S(2)}) collective-permute-start(bf16[2,1,8,128,128]{4,3,2,1,0:T(8,128)(2,1)} %pad_maximum_fusion.1), channel_id=1, source_target_pairs={{0,4},{4,8},{8,12},{1,5},{5,9},{9,13},{2,6},{6,10},{10,14},{3,7},{... | collective-permute-start | bytes 1572872 | tf_op jit(solution)/shard_map/ppermute | solution.py:28
  20.2 0.1 copy.14.picks_ref
  20.3 5.3 %collective-permute-done.1 = bf16[2,512,128]{2,1,0:T(8,128)(2,1)} collective-permute-done((bf16[2,512,128]{2,1,0:T(8,128)(2,1)S(1)}, bf16[2,512,128]{2,1,0:T(8,128)(2,1)}, u32[]{:S(2)}, u32[]{:S(2)}) %collective-permute-start.1) | collective-permute-done | bytes 262176 | tf_op jit(solution)/shard_map/ppermute | solution.py:361
  25.6 0.1 select_select_fusion
  25.8 10.7 %blocks_from_2.1 = (bf16[256,1024]{1,0:T(8,128)(2,1)S(1)}, f32[2,1,128]{2,1,0:T(1,128)S(1)}, f32[512,128]{1,0:T(8,128)S(1)}, f32[512,128]{1,0:T(8,128)S(1)}, f32...) custom-call(s32[1]{0:T(128)} %bitcast.base_ref, s32[4,2]{1,0:T(4,128)S(1)} %copy.14.picks_ref, bf16[512,1024]{1,0:T(8,128)(2,1)S(1)} %copy-done, ...), custom_call_target="tpu_custom_call" | custom-call | flops 1677721600 | bytes 3932160 | tf_op jit(solution)/shard_map/blocks_from_2/pallas_call | solution.py:320
  36.5 6.1 %blocks_from_1.1 = (bf16[128,1024]{1,0:T(8,128)(2,1)S(1)}, f32[1,1,128]{2,1,0:T(1,128)S(1)}, f32[512,128]{1,0:T(8,128)S(1)}, f32[512,128]{1,0:T(8,128)S(1)}, f32...) custom-call(s32[1]{0:T(128)} %bitcast.base_ref, s32[4,2]{1,0:T(4,128)S(1)} %copy.14.picks_ref, ...), custom_call_target="tpu_custom_call" | custom-call | flops 838860800 | bytes 1966080 | tf_op jit(solution)/shard_map/blocks_from_1/pallas_call | solution.py:320
  42.6 1.1 %fusion.1 = (bf16[1,1,8,128,128]{4,3,2,1,0:T(8,128)(2,1)S(1)}, bf16[1,1,8,128,128]{4,3,2,1,0:T(8,128)(2,1)S(1)}) fusion(bf16[2,1,8,128,128]{4,3,2,1,0:T(8,128)(2,1)} %collective-permute-done), kind=kLoop, calls=%fused_computation.10 | loop fusion | bytes 1048576 | tf_op jit(solution)/shard_map/slice | solution.py:373
  43.6 6.0 %blocks_from_0.1 = (bf16[128,1024]{1,0:T(8,128)(2,1)S(1)}, f32[1,1,128]{2,1,0:T(1,128)S(1)}, f32[512,128]{1,0:T(8,128)S(1)}, f32[512,128]{1,0:T(8,128)S(1)}, f32...) custom-call(s32[1]{0:T(128)} %bitcast.base_ref, s32[4,2]{1,0:T(4,128)S(1)} %copy.14.picks_ref, ...), custom_call_target="tpu_custom_call" | custom-call | flops 838860800 | bytes 1966080 | tf_op jit(solution)/shard_map/blocks_from_0/pallas_call | solution.py:320
  49.7 1.3 %collective-permute-start.5 = (bf16[2,2,128,128]{3,2,1,0:T(8,128)(2,1)S(1)}, bf16[2,2,128,128]{3,2,1,0:T(8,128)(2,1)S(1)}, u32[]{:S(2)}, u32[]{:S(2)}) collective-permute-start(bf16[2,2,128,128]{3,2,1,0:T(8,128)(2,1)S(1)} %add_convert_fusion.2), channel_id=1, source_target_pairs={{4,0},{8,4},{12,8},{5,1},{9,5},{13,9},{6,2},{10,6},{14,10},{7,3},{... | collective-permute-start | bytes 393224 | tf_op jit(solution)/shard_map/ppermute | solution.py:28
  51.0 1.3 %collective-permute-start.7 = (bf16[512,128]{1,0:T(8,128)(2,1)S(1)}, bf16[512,128]{1,0:T(8,128)(2,1)S(1)}, u32[]{:S(2)}, u32[]{:S(2)}) collective-permute-start(bf16[512,128]{1,0:T(8,128)(2,1)S(1)} %convert_element_type.23), channel_id=1, source_target_pairs={{4,0},{12,8},{5,1},{13,9},{6,2},{14,10},{7,3},{15,11},{20,16},{28,... | collective-permute-start | bytes 393224 | tf_op jit(solution)/shard_map/ppermute | solution.py:403
  52.3 1.3 %collective-permute-start.6 = (bf16[512,128]{1,0:T(8,128)(2,1)S(1)}, bf16[512,128]{1,0:T(8,128)(2,1)S(1)}, u32[]{:S(2)}, u32[]{:S(2)}) collective-permute-start(bf16[512,128]{1,0:T(8,128)(2,1)S(1)} %convert_element_type.22), channel_id=1, source_target_pairs={{4,0},{12,8},{5,1},{13,9},{6,2},{14,10},{7,3},{15,11},{20,16},{28,... | collective-permute-start | bytes 393224 | tf_op jit(solution)/shard_map/ppermute | solution.py:403
  53.6 4.4 %collective-permute-done.5.back_ref = bf16[2,2,128,128]{3,2,1,0:T(8,128)(2,1)S(1)} collective-permute-done((bf16[2,2,128,128]{3,2,1,0:T(8,128)(2,1)S(1)}, bf16[2,2,128,128]{3,2,1,0:T(8,128)(2,1)S(1)}, u32[]{:S(2)}, u32[]{:S(2)}) %collective-permute-start.5) | collective-permute-done | bytes 131104 | tf_op jit(solution)/shard_map/ppermute | solution.py:28
  58.0 1.9 %collective-permute-done.7.rest_1_ = bf16[512,128]{1,0:T(8,128)(2,1)S(1)} collective-permute-done((bf16[512,128]{1,0:T(8,128)(2,1)S(1)}, bf16[512,128]{1,0:T(8,128)(2,1)S(1)}, u32[]{:S(2)}, u32[]{:S(2)}) %collective-permute-start.7) | collective-permute-done | bytes 131104 | tf_op jit(solution)/shard_map/ppermute | solution.py:403
  60.0 1.3 %collective-permute-start.9 = (bf16[512,128]{1,0:T(8,128)(2,1)S(1)}, bf16[512,128]{1,0:T(8,128)(2,1)S(1)}, u32[]{:S(2)}, u32[]{:S(2)}) collective-permute-start(bf16[512,128]{1,0:T(8,128)(2,1)S(1)} %add_convert_fusion), channel_id=1, source_target_pairs={{8,0},{9,1},{10,2},{11,3},{24,16},{25,17},{26,18},{27,19}} | collective-permute-start | bytes 393224 | tf_op jit(solution)/shard_map/ppermute | solution.py:403
  61.3 1.6 %collective-permute-start.11 = (f32[512]{0:T(512)S(1)}, f32[512]{0:T(512)S(1)}, u32[]{:S(2)}, u32[]{:S(2)}) collective-permute-start(f32[512]{0:T(512)S(1)} %add.21), channel_id=1, source_target_pairs={{0,1},{1,0},{2,3},{3,2},{4,5},{5,4},{6,7},{7,6},{8,9},{9,8},{10,11... | collective-permute-start | bytes 6152 | tf_op jit(solution)/shard_map/ppermute | solution.py:37
  62.9 1.3 %collective-permute-start.8 = (bf16[512,128]{1,0:T(8,128)(2,1)S(1)}, bf16[512,128]{1,0:T(8,128)(2,1)S(1)}, u32[]{:S(2)}, u32[]{:S(2)}) collective-permute-start(bf16[512,128]{1,0:T(8,128)(2,1)S(1)} %add_convert_fusion.1), channel_id=1, source_target_pairs={{8,0},{9,1},{10,2},{11,3},{24,16},{25,17},{26,18},{27,19}} | collective-permute-start | bytes 393224 | tf_op jit(solution)/shard_map/ppermute | solution.py:403
  64.2 0.8 %collective-permute-done.11 = f32[512]{0:T(512)S(1)} collective-permute-done((f32[512]{0:T(512)S(1)}, f32[512]{0:T(512)S(1)}, u32[]{:S(2)}, u32[]{:S(2)}) %collective-permute-start.11) | collective-permute-done | bytes 2080 | tf_op jit(solution)/shard_map/ppermute | solution.py:37
  65.0 1.5 %collective-permute-start.12 = (f32[512]{0:T(512)S(1)}, f32[512]{0:T(512)S(1)}, u32[]{:S(2)}, u32[]{:S(2)}) collective-permute-start(f32[512]{0:T(512)S(1)} %add.22), channel_id=1, source_target_pairs={{0,2},{1,3},{2,0},{3,1},{4,6},{5,7},{6,4},{7,5},{8,10},{9,11},{10,... | collective-permute-start | bytes 6152 | tf_op jit(solution)/shard_map/ppermute | solution.py:37
  66.5 1.0 %pad_maximum_fusion = bf16[512,1024]{1,0:T(8,128)(2,1)} fusion(bf16[256,1024]{1,0:T(8,128)(2,1)S(1)} %get-tuple-element.38, bf16[128,1024]{1,0:T(8,128)(2,1)S(1)} %get-tuple-element.37, bf16[128,1024]{1,0:T(8,128)(2,1)S(1)} %get-tuple-element.36), kind=kLoop, calls=%fused_computation | loop fusion | flops 3145728 | bytes 2097152 | tf_op jit(solution)/shard_map/concatenate | solution.py:389
  67.5 1.0 %collective-permute-done.12 = f32[512]{0:T(512)S(1)} collective-permute-done((f32[512]{0:T(512)S(1)}, f32[512]{0:T(512)S(1)}, u32[]{:S(2)}, u32[]{:S(2)}) %collective-permute-start.12) | collective-permute-done | bytes 2080 | tf_op jit(solution)/shard_map/ppermute | solution.py:37
  68.5 0.6 add.23
  69.1 0.2 collective-permute-done.9.rest_3_
  69.4 1.8 %collective-permute-done.8.rest_2_ = bf16[512,128]{1,0:T(8,128)(2,1)S(1)} collective-permute-done((bf16[512,128]{1,0:T(8,128)(2,1)S(1)}, bf16[512,128]{1,0:T(8,128)(2,1)S(1)}, u32[]{:S(2)}, u32[]{:S(2)}) %collective-permute-start.8) | collective-permute-done | bytes 131104 | tf_op jit(solution)/shard_map/ppermute | solution.py:403
  71.1 0.8 %finish.1 = (bf16[512,128]{1,0:T(8,128)(2,1)}, bf16[512,128]{1,0:T(8,128)(2,1)}) custom-call(s32[1]{0:T(128)} %bitcast.5.root_ref, f32[512,128]{1,0:T(8,128)S(1)} %get-tuple-element.39.dk_ref, f32[512,128]{1,0:T(8,128)S(1)} %get-tuple-element.40.dv_ref, f32[512,128]{1,0:T(8,128)S(1)} %get-tuple-element.41.dsk_ref, f32[512,128]{1,0:T(8,128)S(1)} %get-tuple-element.42.dsv_ref, ...), custom_call_target="tpu_custom_call" | custom-call | tf_op jit(solution)/shard_map/finish/pallas_call | solution.py:263
  (32 shorter events, 0.3 us)
Async XLA Ops:
  0.6 0.9 %copy-start.2 = (bf16[512,128]{1,0:T(8,128)(2,1)S(1)}, bf16[512,128]{1,0:T(8,128)(2,1)}, u32[]{:S(2)}) copy-start(bf16[512,128]{1,0:T(8,128)(2,1)} %rest_5_.5) | copy-start | bytes 393220
  1.5 0.9 %copy-start.4 = (bf16[512,128]{1,0:T(8,128)(2,1)S(1)}, bf16[512,128]{1,0:T(8,128)(2,1)}, u32[]{:S(2)}) copy-start(bf16[512,128]{1,0:T(8,128)(2,1)} %rest_6_.5) | copy-start | bytes 393220
  2.4 17.8 %copy-start.7 = (s32[4,2]{0,1:T(2,128)S(1)}, s32[4,2]{0,1:T(2,128)}, u32[]{:S(2)}) copy-start(s32[4,2]{0,1:T(2,128)} %param.14) | copy-start | bytes 100
  2.5 23.3 %copy-start = (bf16[512,1024]{1,0:T(8,128)(2,1)S(1)}, bf16[512,1024]{1,0:T(8,128)(2,1)}, u32[]{:S(2)}) copy-start(bf16[512,1024]{1,0:T(8,128)(2,1)} %q_ref.5) | copy-start | bytes 3145732
  2.5 23.3 %copy-start.1 = (bf16[512,1024]{1,0:T(8,128)(2,1)S(1)}, bf16[512,1024]{1,0:T(8,128)(2,1)}, u32[]{:S(2)}) copy-start(bf16[512,1024]{1,0:T(8,128)(2,1)} %g_ref.5) | copy-start | bytes 3145732
  2.5 23.3 %copy-start.3 = (bf16[512,128]{1,0:T(8,128)(2,1)S(1)}, bf16[512,128]{1,0:T(8,128)(2,1)}, u32[]{:S(2)}) copy-start(bf16[512,128]{1,0:T(8,128)(2,1)} %rest_5_.5) | copy-start | bytes 393220
  2.5 23.3 %copy-start.5 = (bf16[512,128]{1,0:T(8,128)(2,1)S(1)}, bf16[512,128]{1,0:T(8,128)(2,1)}, u32[]{:S(2)}) copy-start(bf16[512,128]{1,0:T(8,128)(2,1)} %rest_6_.5) | copy-start | bytes 393220
  2.5 23.3 %copy-start.6 = (f32[512]{0:T(512)S(1)}, f32[512]{0:T(512)}, u32[]{:S(2)}) copy-start(f32[512]{0:T(512)} %param.15) | copy-start | bytes 6148
  2.5 17.8 %collective-permute-start.3 = (bf16[2,512,128]{2,1,0:T(8,128)(2,1)S(1)}, bf16[2,512,128]{2,1,0:T(8,128)(2,1)S(1)}, u32[]{:S(2)}, u32[]{:S(2)}) collective-permute-start(bf16[2,512,128]{2,1,0:T(8,128)(2,1)S(1)} %pack.1), channel_id=1, source_target_pairs={{0,4},{4,8},{8,12},{1,5},{5,9},{9,13},{2,6},{6,10},{10,14},{3,7},{... | collective-permute-start | bytes 786440 | tf_op jit(solution)/shard_map/ppermute | solution.py:28
  7.6 12.7 %collective-permute-start.2 = (bf16[2,512,128]{2,1,0:T(8,128)(2,1)S(1)}, bf16[2,512,128]{2,1,0:T(8,128)(2,1)}, u32[]{:S(2)}, u32[]{:S(2)}) collective-permute-start(bf16[2,512,128]{2,1,0:T(8,128)(2,1)S(1)} %pack.1), channel_id=1, source_target_pairs={{0,8},{1,9},{2,10},{3,11},{16,24},{17,25},{18,26},{19,27}} | collective-permute-start | bytes 786440 | tf_op jit(solution)/shard_map/ppermute | solution.py:361
  12.8 12.8 %collective-permute-start.1 = (bf16[2,512,128]{2,1,0:T(8,128)(2,1)S(1)}, bf16[2,512,128]{2,1,0:T(8,128)(2,1)}, u32[]{:S(2)}, u32[]{:S(2)}) collective-permute-start(bf16[2,512,128]{2,1,0:T(8,128)(2,1)S(1)} %pack.1), channel_id=1, source_target_pairs={{0,12},{1,13},{2,14},{3,15},{16,28},{17,29},{18,30},{19,31}} | collective-permute-start | bytes 786440 | tf_op jit(solution)/shard_map/ppermute | solution.py:361
  16.0 20.5 %collective-permute-start.4 = (bf16[1,1,8,128,128]{4,3,2,1,0:T(8,128)(2,1)S(1)}, bf16[1,1,8,128,128]{4,3,2,1,0:T(8,128)(2,1)S(1)}, u32[]{:S(2)}, u32[]{:S(2)}) collective-permute-start(bf16[1,1,8,128,128]{4,3,2,1,0:T(8,128)(2,1)S(1)} %get-tuple-element.53), channel_id=1, source_target_pairs={{0,4},{4,8},{8,12},{1,5},{5,9},{9,13},{2,6},{6,10},{10,14},{3,7},{... | collective-permute-start | bytes 786440 | tf_op jit(solution)/shard_map/ppermute | solution.py:28
  18.1 24.4 %collective-permute-start = (bf16[2,1,8,128,128]{4,3,2,1,0:T(8,128)(2,1)}, bf16[2,1,8,128,128]{4,3,2,1,0:T(8,128)(2,1)}, u32[]{:S(2)}, u32[]{:S(2)}) collective-permute-start(bf16[2,1,8,128,128]{4,3,2,1,0:T(8,128)(2,1)} %pad_maximum_fusion.1), channel_id=1, source_target_pairs={{0,4},{4,8},{8,12},{1,5},{5,9},{9,13},{2,6},{6,10},{10,14},{3,7},{... | collective-permute-start | bytes 1572872 | tf_op jit(solution)/shard_map/ppermute | solution.py:28
  49.7 8.3 %collective-permute-start.5 = (bf16[2,2,128,128]{3,2,1,0:T(8,128)(2,1)S(1)}, bf16[2,2,128,128]{3,2,1,0:T(8,128)(2,1)S(1)}, u32[]{:S(2)}, u32[]{:S(2)}) collective-permute-start(bf16[2,2,128,128]{3,2,1,0:T(8,128)(2,1)S(1)} %add_convert_fusion.2), channel_id=1, source_target_pairs={{4,0},{8,4},{12,8},{5,1},{9,5},{13,9},{6,2},{10,6},{14,10},{7,3},{... | collective-permute-start | bytes 393224 | tf_op jit(solution)/shard_map/ppermute | solution.py:28
  51.0 9.0 %collective-permute-start.7 = (bf16[512,128]{1,0:T(8,128)(2,1)S(1)}, bf16[512,128]{1,0:T(8,128)(2,1)S(1)}, u32[]{:S(2)}, u32[]{:S(2)}) collective-permute-start(bf16[512,128]{1,0:T(8,128)(2,1)S(1)} %convert_element_type.23), channel_id=1, source_target_pairs={{4,0},{12,8},{5,1},{13,9},{6,2},{14,10},{7,3},{15,11},{20,16},{28,... | collective-permute-start | bytes 393224 | tf_op jit(solution)/shard_map/ppermute | solution.py:403
  52.3 10.6 %collective-permute-start.6 = (bf16[512,128]{1,0:T(8,128)(2,1)S(1)}, bf16[512,128]{1,0:T(8,128)(2,1)S(1)}, u32[]{:S(2)}, u32[]{:S(2)}) collective-permute-start(bf16[512,128]{1,0:T(8,128)(2,1)S(1)} %convert_element_type.22), channel_id=1, source_target_pairs={{4,0},{12,8},{5,1},{13,9},{6,2},{14,10},{7,3},{15,11},{20,16},{28,... | collective-permute-start | bytes 393224 | tf_op jit(solution)/shard_map/ppermute | solution.py:403
  58.0 3.3 %collective-permute-start.10 = (f32[512]{0:T(512)S(1)}, f32[512]{0:T(512)S(1)}, u32[]{:S(2)}, u32[]{:S(2)}) collective-permute-start(f32[512]{0:T(512)S(1)} %bitcast.14), channel_id=1, source_target_pairs={{0,16},{16,0},{1,17},{17,1},{2,18},{18,2},{3,19},{19,3},{4,20},{20... | collective-permute-start | bytes 6152 | tf_op jit(solution)/shard_map/ppermute | solution.py:37
  60.0 9.4 %collective-permute-start.9 = (bf16[512,128]{1,0:T(8,128)(2,1)S(1)}, bf16[512,128]{1,0:T(8,128)(2,1)S(1)}, u32[]{:S(2)}, u32[]{:S(2)}) collective-permute-start(bf16[512,128]{1,0:T(8,128)(2,1)S(1)} %add_convert_fusion), channel_id=1, source_target_pairs={{8,0},{9,1},{10,2},{11,3},{24,16},{25,17},{26,18},{27,19}} | collective-permute-start | bytes 393224 | tf_op jit(solution)/shard_map/ppermute | solution.py:403
  61.3 3.7 %collective-permute-start.11 = (f32[512]{0:T(512)S(1)}, f32[512]{0:T(512)S(1)}, u32[]{:S(2)}, u32[]{:S(2)}) collective-permute-start(f32[512]{0:T(512)S(1)} %add.21), channel_id=1, source_target_pairs={{0,1},{1,0},{2,3},{3,2},{4,5},{5,4},{6,7},{7,6},{8,9},{9,8},{10,11... | collective-permute-start | bytes 6152 | tf_op jit(solution)/shard_map/ppermute | solution.py:37
  62.9 8.2 %collective-permute-start.8 = (bf16[512,128]{1,0:T(8,128)(2,1)S(1)}, bf16[512,128]{1,0:T(8,128)(2,1)S(1)}, u32[]{:S(2)}, u32[]{:S(2)}) collective-permute-start(bf16[512,128]{1,0:T(8,128)(2,1)S(1)} %add_convert_fusion.1), channel_id=1, source_target_pairs={{8,0},{9,1},{10,2},{11,3},{24,16},{25,17},{26,18},{27,19}} | collective-permute-start | bytes 393224 | tf_op jit(solution)/shard_map/ppermute | solution.py:403
  65.0 3.6 %collective-permute-start.12 = (f32[512]{0:T(512)S(1)}, f32[512]{0:T(512)S(1)}, u32[]{:S(2)}, u32[]{:S(2)}) collective-permute-start(f32[512]{0:T(512)S(1)} %add.22), channel_id=1, source_target_pairs={{0,2},{1,3},{2,0},{3,1},{4,6},{5,7},{6,4},{7,5},{8,10},{9,11},{10,... | collective-permute-start | bytes 6152 | tf_op jit(solution)/shard_map/ppermute | solution.py:37

commit v4 on v3

--- a/solution.py
+++ b/solution.py
@@ -101,8 +101,6 @@
     key_id = lax.broadcasted_iota(jnp.int32, (BLK, wide), 0)
     row_id = lax.broadcasted_iota(jnp.int32, (BLK, wide), 1) & (BLK - 1)
     causal = key_id <= row_id
-    square = (BLK, BLK)
-    unit = (lax.broadcasted_iota(jnp.int32, square, 0) == lax.broadcasted_iota(jnp.int32, square, 1)).astype(F32).astype(BF)
     low = jnp.float32(-1e9)
     loss = jnp.zeros((1, wide), F32)
 
@@ -132,7 +130,7 @@
         for j in range(slots):
             tile = slice(j * BLK, (j + 1) * BLK)
             t = jnp.concatenate([teacher_refs[j][0, 0, ha], teacher_refs[j][0, 0, hb]], axis=0)
-            t = lax.dot_general(unit, t, NT, preferred_element_type=F32)
+            t = t.T.astype(F32)
             if j == 0:
                 t = jnp.where(causal, t, low)
                 s_scr[at, tile] = jnp.where(causal, s_scr[at, tile], low)
@@ -283,8 +281,8 @@
     specs = [pl.BlockSpec((BLK, columns), lambda i, *_: (first + i, 0))] * 2
     for d in range(WIN):
         if d in crossing:
-            args.append(incoming[d])
-            specs.append(pl.BlockSpec(tile, lambda i, *_: (0, 0, 0, 0, 0)))
+            args.append(incoming)
+            specs.append(pl.BlockSpec(tile, lambda i, *_, d=d: (crossing.index(d), 0, 0, 0, 0)))
         else:
             args.append(window)
             specs.append(pl.BlockSpec(tile, lambda i, *_, d=d: (first + i - d, d, 0, 0, 0)))
@@ -348,29 +346,34 @@
     tail = slice(tokens - LEAD * BLK, tokens)
     first_rows = slice(0, NGLOB * BLK)
     pair = pack([key_rows, values])
+    half = 1
+    while 2 * half < count:
+        half *= 2
+    sinks = pair[:, first_rows]
+    known, later = [0], None
+    while half > 1:
+        came = lax.ppermute(sinks, "seq", [(i, i + half) for i in known if i + half < count])
+        sinks = jnp.where(where % (2 * half) == half, came, sinks)
+        known = sorted(known + [i + half for i in known if i + half < count])
+        half //= 2
     got = shift(pair, "seq", 1)
     before = got[:, tail].reshape(2, LEAD, BLK, E)
-    sinks = jnp.where(where == 0, pair[:, first_rows], got[:, first_rows])
-    span, known = 1, pair[:, first_rows]
-    while span < count:
-        for times in range(1, FAN):
-            if span == 1 and times == 1:
-                continue
-            route = [(i, i + times * span) for i in range(span) if i + times * span < count]
-            if route:
-                more = lax.ppermute(known, "seq", route)
-                sinks = jnp.where((where >= times * span) & (where < (times + 1) * span), more, sinks)
-        span *= FAN
-        known = sinks
+    forward = [(i, i + 1) for i in known if i > 0 and i + 1 < count]
+    if forward:
+        came = lax.ppermute(sinks, "seq", forward)
+        later = sinks
+        sinks = jnp.where(where % 2 == 1, came, sinks)
+    sinks = jnp.where(where == 1, got[:, first_rows], sinks)
 
     incoming = {}
     for block in range(LEAD - 1, -1, -1):
-        offsets = list(range(block + 1, WIN))
         out = jnp.concatenate(
-            [teacher_window[blocks + block - d:blocks + block - d + 1, d:d + 1] for d in offsets], axis=0
+            [teacher_window[blocks + block - d:blocks + block - d + 1, d:d + 1] for d in range(block + 1, WIN)],
+            axis=0,
         )
-        came = shift(out, "seq", 1)
-        incoming[block] = {d: came[i:i + 1] for i, d in enumerate(offsets)}
+        if block == 0 and later is not None:
+            out, _ = lax.optimization_barrier((out, later))
+        incoming[block] = shift(out, "seq", 1)
 
     own = (key_rows, values)
     sink_arrays = (sinks[0], sinks[1])

time: 72.4 us -> 71.6 us (0.989)
  waiting for transfers between devices: 15.4 us -> 12.9 us
  starting transfers between devices: 25.2 us -> 27.4 us
  Pallas kernels: 23.6 us -> 22.2 us
    ppermute x4, starting transfers between devices: 9.77 us -> 11.7 us  [shift(): return lax.ppermute(block, axis, route)]
    pallas_call x3, Pallas kernels: 22.7 us -> 21.4 us  [run_blocks(): pl.pallas_call(functools.partial(block_kernel, first, crossing, slots, ch...]
    slice x1 -> x0, local copies, waits for them, and re-layouts: 1.07 us -> none  [local(): incoming[block] = {d: came[i:i + 1] for i, d in enumerate(offsets)}]
    ppermute x4, waiting for transfers between devices: 3.96 us -> 2.95 us  [local(): came = [lax.ppermute(x, 'seq', route) for x in low]]
    ppermute x4, waiting for transfers between devices: 4.37 us -> 3.42 us  [shift(): return lax.ppermute(block, axis, route)]
    slice x1, local copies, waits for them, and re-layouts: 0.01 us -> 0.92 us  [local(): before = got[:, tail].reshape(2, LEAD, BLK, E)]
    slice x1, local copies, waits for them, and re-layouts: 1.16 us -> 1.95 us  [local(): teacher_window[blocks + block - d:blocks + block - d + 1, d:d + 1]]
  transfers between devices with their start and end apart: 13 -> 13, of which waited for: 7 -> 6; matrix products, arithmetic and copies ran while one was open for 5% -> 8% of each run, Pallas kernels for 23% -> 22%
where the time goes in v4:
time: 71.6 us; the launch traced here: 71.1 us
  starting transfers between devices  27.4 us (38%)
  Pallas kernels  22.2 us (31%)
  waiting for transfers between devices  12.9 us (18%)
  local copies, waits for them, and re-layouts  4.82 us (7%)
  other arithmetic  2.86 us (4%)
  between operations  0.95 us (1%)
    pallas_call x3, Pallas kernels, run_blocks(): pl.pallas_call(functools.partial(block_kernel, first, crossing, slots, ch...  21.4 us
    ppermute x4, starting transfers between devices, shift(): return lax.ppermute(block, axis, route)  11.7 us
    ppermute x1, starting transfers between devices, local(): lax.ppermute(sinks, 'seq', [(i, i + half) for i in known if i + half < co...  5.96 us
    ppermute x4, starting transfers between devices, local(): came = [lax.ppermute(x, 'seq', route) for x in low]  5.17 us
    ppermute x1, waiting for transfers between devices, local(): lax.ppermute(sinks, 'seq', [(i, i + half) for i in known if i + half < co...  4.72 us
    ppermute x4, waiting for transfers between devices, shift(): return lax.ppermute(block, axis, route)  3.42 us
    ppermute x3, starting transfers between devices, sum_over(): lax.ppermute(block, axis, [(i, i ^ step) for i in range(count)])  3.08 us
    ppermute x4, waiting for transfers between devices, local(): came = [lax.ppermute(x, 'seq', route) for x in low]  2.95 us
  transfers between devices with their start and end apart: 13, of which 6 were waited for; matrix products, arithmetic and copies ran while one was open for 8% of the time, Pallas kernels for 22%

profile of v4, /device:TPU:0, one launch (start us, length us, event | category | flops | bytes accessed | tf_op | source)
XLA Modules:
  0.0 71.1 jit_solution(3237816848878628621)
XLA Ops:
  0.6 0.0 copy-start.2
  0.6 0.9 %copy-done.2 = bf16[512,128]{1,0:T(8,128)(2,1)S(1)} copy-done((bf16[512,128]{1,0:T(8,128)(2,1)S(1)}, bf16[512,128]{1,0:T(8,128)(2,1)}, u32[]{:S(2)}) %copy-start.2) | copy-done | bytes 131096
  1.5 0.9 %copy-done.4 = bf16[512,128]{1,0:T(8,128)(2,1)S(1)} copy-done((bf16[512,128]{1,0:T(8,128)(2,1)S(1)}, bf16[512,128]{1,0:T(8,128)(2,1)}, u32[]{:S(2)}) %copy-start.4) | copy-done | bytes 131096
  2.5 6.0 %collective-permute-start = (bf16[2,512,128]{2,1,0:T(8,128)(2,1)S(1)}, bf16[2,512,128]{2,1,0:T(8,128)(2,1)S(1)}, u32[]{:S(2)}, u32[]{:S(2)}) collective-permute-start(bf16[2,512,128]{2,1,0:T(8,128)(2,1)S(1)} %pack.1), channel_id=1, source_target_pairs={{0,8},{1,9},{2,10},{3,11},{16,24},{17,25},{18,26},{19,27}} | collective-permute-start | bytes 786440 | tf_op jit(solution)/shard_map/ppermute | solution.py:355
  8.4 2.0 %collective-permute-start.2 = (bf16[2,512,128]{2,1,0:T(8,128)(2,1)S(1)}, bf16[2,512,128]{2,1,0:T(8,128)(2,1)}, u32[]{:S(2)}, u32[]{:S(2)}) collective-permute-start(bf16[2,512,128]{2,1,0:T(8,128)(2,1)S(1)} %pack.1), channel_id=1, source_target_pairs={{0,4},{4,8},{8,12},{1,5},{5,9},{9,13},{2,6},{6,10},{10,14},{3,7},{... | collective-permute-start | bytes 786440 | tf_op jit(solution)/shard_map/ppermute | solution.py:28
  10.4 4.7 %collective-permute-done = bf16[2,512,128]{2,1,0:T(8,128)(2,1)S(1)} collective-permute-done((bf16[2,512,128]{2,1,0:T(8,128)(2,1)S(1)}, bf16[2,512,128]{2,1,0:T(8,128)(2,1)S(1)}, u32[]{:S(2)}, u32[]{:S(2)}) %collective-permute-start) | collective-permute-done | bytes 262176 | tf_op jit(solution)/shard_map/ppermute | solution.py:355
  15.2 1.5 %collective-permute-start.3 = (bf16[2,512,128]{2,1,0:T(8,128)(2,1)S(1)}, bf16[2,512,128]{2,1,0:T(8,128)(2,1)}, u32[]{:S(2)}, u32[]{:S(2)}) collective-permute-start(bf16[2,512,128]{2,1,0:T(8,128)(2,1)S(1)} %broadcast_select_fusion), channel_id=1, source_target_pairs={{8,12},{9,13},{10,14},{11,15},{24,28},{25,29},{26,30},{27,31}} | collective-permute-start | bytes 786440 | tf_op jit(solution)/shard_map/ppermute | solution.py:363
  16.7 1.9 %fusion = (bf16[1,1,8,128,128]{4,3,2,1,0:T(8,128)(2,1)S(1)}, bf16[1,1,8,128,128]{4,3,2,1,0:T(8,128)(2,1)}, bf16[1,1,8,128,128]{4,3,2,1,0:T(8,128)(2,1)}) fusion(bf16[4,3,8,128,128]{4,3,2,1,0:T(8,128)(2,1)} %rest_0_.5), kind=kLoop, calls=%fused_computation.10 | loop fusion | bytes 1572864 | tf_op jit(solution)/shard_map/slice | solution.py:371
  18.7 1.3 %collective-permute-start.4 = (bf16[1,1,8,128,128]{4,3,2,1,0:T(8,128)(2,1)}, bf16[1,1,8,128,128]{4,3,2,1,0:T(8,128)(2,1)S(1)}, u32[]{:S(2)}, u32[]{:S(2)}) collective-permute-start(bf16[1,1,8,128,128]{4,3,2,1,0:T(8,128)(2,1)} %get-tuple-element.55), channel_id=1, source_target_pairs={{0,4},{4,8},{8,12},{1,5},{5,9},{9,13},{2,6},{6,10},{10,14},{3,7},{... | collective-permute-start | bytes 786440 | tf_op jit(solution)/shard_map/ppermute | solution.py:28
  20.0 0.1 copy.14.picks_ref
  20.1 1.0 %pad_maximum_fusion.1 = bf16[2,1,8,128,128]{4,3,2,1,0:T(8,128)(2,1)S(1)} fusion(bf16[1,1,8,128,128]{4,3,2,1,0:T(8,128)(2,1)} %get-tuple-element.56, bf16[1,1,8,128,128]{4,3,2,1,0:T(8,128)(2,1)S(1)} %get-tuple-element.54), kind=kLoop, calls=%fused_computation.1 | loop fusion | flops 262144 | bytes 1048576 | tf_op jit(solution)/shard_map/concatenate | solution.py:370
  21.1 7.1 %collective-permute-start.1 = (bf16[2,1,8,128,128]{4,3,2,1,0:T(8,128)(2,1)S(1)}, bf16[2,1,8,128,128]{4,3,2,1,0:T(8,128)(2,1)S(1)}, u32[]{:S(2)}, u32[]{:S(2)}) collective-permute-start(bf16[2,1,8,128,128]{4,3,2,1,0:T(8,128)(2,1)S(1)} %pad_maximum_fusion.1), channel_id=1, source_target_pairs={{0,4},{4,8},{8,12},{1,5},{5,9},{9,13},{2,6},{6,10},{10,14},{3,7},{... | collective-permute-start | bytes 1572872 | tf_op jit(solution)/shard_map/ppermute | solution.py:28
  28.2 0.9 %slice.26 = bf16[2,256,128]{2,1,0:T(8,128)(2,1)S(1)} slice(bf16[2,512,128]{2,1,0:T(8,128)(2,1)} %collective-permute-done.2), slice={[0:2], [256:512], [0:128]} | slice | bytes 262144 | tf_op jit(solution)/shard_map/slice | solution.py:360
  29.2 0.1 select_select_fusion
  29.3 10.0 %blocks_from_2.1 = (bf16[256,1024]{1,0:T(8,128)(2,1)S(1)}, f32[2,1,128]{2,1,0:T(1,128)S(1)}, f32[512,128]{1,0:T(8,128)S(1)}, f32[512,128]{1,0:T(8,128)S(1)}, f32...) custom-call(s32[1]{0:T(128)} %bitcast.base_ref, s32[4,2]{1,0:T(4,128)S(1)} %copy.14.picks_ref, bf16[512,1024]{1,0:T(8,128)(2,1)S(1)} %copy-done, ...), custom_call_target="tpu_custom_call" | custom-call | flops 1677721600 | bytes 3932160 | tf_op jit(solution)/shard_map/blocks_from_2/pallas_call | solution.py:318
  39.3 5.7 %blocks_from_1.1 = (bf16[128,1024]{1,0:T(8,128)(2,1)S(1)}, f32[1,1,128]{2,1,0:T(1,128)S(1)}, f32[512,128]{1,0:T(8,128)S(1)}, f32[512,128]{1,0:T(8,128)S(1)}, f32...) custom-call(s32[1]{0:T(128)} %bitcast.base_ref, s32[4,2]{1,0:T(4,128)S(1)} %copy.14.picks_ref, ...), custom_call_target="tpu_custom_call" | custom-call | flops 838860800 | bytes 1966080 | tf_op jit(solution)/shard_map/blocks_from_1/pallas_call | solution.py:318
  45.1 5.7 %blocks_from_0.1 = (bf16[128,1024]{1,0:T(8,128)(2,1)S(1)}, f32[1,1,128]{2,1,0:T(1,128)S(1)}, f32[512,128]{1,0:T(8,128)S(1)}, f32[512,128]{1,0:T(8,128)S(1)}, f32...) custom-call(s32[1]{0:T(128)} %bitcast.base_ref, s32[4,2]{1,0:T(4,128)S(1)} %copy.14.picks_ref, ...), custom_call_target="tpu_custom_call" | custom-call | flops 838860800 | bytes 1966080 | tf_op jit(solution)/shard_map/blocks_from_0/pallas_call | solution.py:318
  50.8 1.3 %collective-permute-start.5 = (bf16[2,2,128,128]{3,2,1,0:T(8,128)(2,1)S(1)}, bf16[2,2,128,128]{3,2,1,0:T(8,128)(2,1)S(1)}, u32[]{:S(2)}, u32[]{:S(2)}) collective-permute-start(bf16[2,2,128,128]{3,2,1,0:T(8,128)(2,1)S(1)} %add_convert_fusion.2), channel_id=1, source_target_pairs={{4,0},{8,4},{12,8},{5,1},{9,5},{13,9},{6,2},{10,6},{14,10},{7,3},{... | collective-permute-start | bytes 393224 | tf_op jit(solution)/shard_map/ppermute | solution.py:28
  52.1 1.3 %collective-permute-start.7 = (bf16[512,128]{1,0:T(8,128)(2,1)S(1)}, bf16[512,128]{1,0:T(8,128)(2,1)S(1)}, u32[]{:S(2)}, u32[]{:S(2)}) collective-permute-start(bf16[512,128]{1,0:T(8,128)(2,1)S(1)} %convert_element_type.23), channel_id=1, source_target_pairs={{4,0},{12,8},{5,1},{13,9},{6,2},{14,10},{7,3},{15,11},{20,16},{28,... | collective-permute-start | bytes 393224 | tf_op jit(solution)/shard_map/ppermute | solution.py:406
  53.4 1.3 %collective-permute-start.6 = (bf16[512,128]{1,0:T(8,128)(2,1)S(1)}, bf16[512,128]{1,0:T(8,128)(2,1)S(1)}, u32[]{:S(2)}, u32[]{:S(2)}) collective-permute-start(bf16[512,128]{1,0:T(8,128)(2,1)S(1)} %convert_element_type.22), channel_id=1, source_target_pairs={{4,0},{12,8},{5,1},{13,9},{6,2},{14,10},{7,3},{15,11},{20,16},{28,... | collective-permute-start | bytes 393224 | tf_op jit(solution)/shard_map/ppermute | solution.py:406
  54.7 3.4 %collective-permute-done.5.back_ref = bf16[2,2,128,128]{3,2,1,0:T(8,128)(2,1)S(1)} collective-permute-done((bf16[2,2,128,128]{3,2,1,0:T(8,128)(2,1)S(1)}, bf16[2,2,128,128]{3,2,1,0:T(8,128)(2,1)S(1)}, u32[]{:S(2)}, u32[]{:S(2)}) %collective-permute-start.5) | collective-permute-done | bytes 131104 | tf_op jit(solution)/shard_map/ppermute | solution.py:28
  58.1 1.4 %collective-permute-done.7.rest_1_ = bf16[512,128]{1,0:T(8,128)(2,1)S(1)} collective-permute-done((bf16[512,128]{1,0:T(8,128)(2,1)S(1)}, bf16[512,128]{1,0:T(8,128)(2,1)S(1)}, u32[]{:S(2)}, u32[]{:S(2)}) %collective-permute-start.7) | collective-permute-done | bytes 131104 | tf_op jit(solution)/shard_map/ppermute | solution.py:406
  59.6 1.3 %collective-permute-start.9 = (bf16[512,128]{1,0:T(8,128)(2,1)S(1)}, bf16[512,128]{1,0:T(8,128)(2,1)S(1)}, u32[]{:S(2)}, u32[]{:S(2)}) collective-permute-start(bf16[512,128]{1,0:T(8,128)(2,1)S(1)} %add_convert_fusion), channel_id=1, source_target_pairs={{8,0},{9,1},{10,2},{11,3},{24,16},{25,17},{26,18},{27,19}} | collective-permute-start | bytes 393224 | tf_op jit(solution)/shard_map/ppermute | solution.py:406
  60.9 1.6 %collective-permute-start.11 = (f32[512]{0:T(512)S(1)}, f32[512]{0:T(512)S(1)}, u32[]{:S(2)}, u32[]{:S(2)}) collective-permute-start(f32[512]{0:T(512)S(1)} %add.30), channel_id=1, source_target_pairs={{0,1},{1,0},{2,3},{3,2},{4,5},{5,4},{6,7},{7,6},{8,9},{9,8},{10,11... | collective-permute-start | bytes 6152 | tf_op jit(solution)/shard_map/ppermute | solution.py:37
  62.5 1.3 %collective-permute-start.8 = (bf16[512,128]{1,0:T(8,128)(2,1)S(1)}, bf16[512,128]{1,0:T(8,128)(2,1)S(1)}, u32[]{:S(2)}, u32[]{:S(2)}) collective-permute-start(bf16[512,128]{1,0:T(8,128)(2,1)S(1)} %add_convert_fusion.1), channel_id=1, source_target_pairs={{8,0},{9,1},{10,2},{11,3},{24,16},{25,17},{26,18},{27,19}} | collective-permute-start | bytes 393224 | tf_op jit(solution)/shard_map/ppermute | solution.py:406
  63.8 0.7 %collective-permute-done.11 = f32[512]{0:T(512)S(1)} collective-permute-done((f32[512]{0:T(512)S(1)}, f32[512]{0:T(512)S(1)}, u32[]{:S(2)}, u32[]{:S(2)}) %collective-permute-start.11) | collective-permute-done | bytes 2080 | tf_op jit(solution)/shard_map/ppermute | solution.py:37
  64.6 1.5 %collective-permute-start.12 = (f32[512]{0:T(512)S(1)}, f32[512]{0:T(512)S(1)}, u32[]{:S(2)}, u32[]{:S(2)}) collective-permute-start(f32[512]{0:T(512)S(1)} %add.31), channel_id=1, source_target_pairs={{0,2},{1,3},{2,0},{3,1},{4,6},{5,7},{6,4},{7,5},{8,10},{9,11},{10,... | collective-permute-start | bytes 6152 | tf_op jit(solution)/shard_map/ppermute | solution.py:37
  66.1 1.0 %pad_maximum_fusion = bf16[512,1024]{1,0:T(8,128)(2,1)} fusion(bf16[256,1024]{1,0:T(8,128)(2,1)S(1)} %get-tuple-element.40, bf16[128,1024]{1,0:T(8,128)(2,1)S(1)} %get-tuple-element.39, bf16[128,1024]{1,0:T(8,128)(2,1)S(1)} %get-tuple-element.38), kind=kLoop, calls=%fused_computation | loop fusion | flops 3145728 | bytes 2097152 | tf_op jit(solution)/shard_map/concatenate | solution.py:392
  67.1 1.0 %collective-permute-done.12 = f32[512]{0:T(512)S(1)} collective-permute-done((f32[512]{0:T(512)S(1)}, f32[512]{0:T(512)S(1)}, u32[]{:S(2)}, u32[]{:S(2)}) %collective-permute-start.12) | collective-permute-done | bytes 2080 | tf_op jit(solution)/shard_map/ppermute | solution.py:37
  68.2 0.6 add.32
  68.7 1.5 %collective-permute-done.8.rest_2_ = bf16[512,128]{1,0:T(8,128)(2,1)S(1)} collective-permute-done((bf16[512,128]{1,0:T(8,128)(2,1)S(1)}, bf16[512,128]{1,0:T(8,128)(2,1)S(1)}, u32[]{:S(2)}, u32[]{:S(2)}) %collective-permute-start.8) | collective-permute-done | bytes 131104 | tf_op jit(solution)/shard_map/ppermute | solution.py:406
  70.3 0.8 %finish.1 = (bf16[512,128]{1,0:T(8,128)(2,1)}, bf16[512,128]{1,0:T(8,128)(2,1)}) custom-call(s32[1]{0:T(128)} %bitcast.5.root_ref, f32[512,128]{1,0:T(8,128)S(1)} %get-tuple-element.41.dk_ref, f32[512,128]{1,0:T(8,128)S(1)} %get-tuple-element.42.dv_ref, f32[512,128]{1,0:T(8,128)S(1)} %get-tuple-element.43.dsk_ref, f32[512,128]{1,0:T(8,128)S(1)} %get-tuple-element.44.dsv_ref, ...), custom_call_target="tpu_custom_call" | custom-call | tf_op jit(solution)/shard_map/finish/pallas_call | solution.py:261
  (32 shorter events, 0.3 us)
Async XLA Ops:
  0.6 0.9 %copy-start.2 = (bf16[512,128]{1,0:T(8,128)(2,1)S(1)}, bf16[512,128]{1,0:T(8,128)(2,1)}, u32[]{:S(2)}) copy-start(bf16[512,128]{1,0:T(8,128)(2,1)} %rest_5_.5) | copy-start | bytes 393220
  1.5 0.9 %copy-start.4 = (bf16[512,128]{1,0:T(8,128)(2,1)S(1)}, bf16[512,128]{1,0:T(8,128)(2,1)}, u32[]{:S(2)}) copy-start(bf16[512,128]{1,0:T(8,128)(2,1)} %rest_6_.5) | copy-start | bytes 393220
  2.4 17.6 %copy-start.7 = (s32[4,2]{0,1:T(2,128)S(1)}, s32[4,2]{0,1:T(2,128)}, u32[]{:S(2)}) copy-start(s32[4,2]{0,1:T(2,128)} %param.14) | copy-start | bytes 100
  2.5 12.7 %collective-permute-start = (bf16[2,512,128]{2,1,0:T(8,128)(2,1)S(1)}, bf16[2,512,128]{2,1,0:T(8,128)(2,1)S(1)}, u32[]{:S(2)}, u32[]{:S(2)}) collective-permute-start(bf16[2,512,128]{2,1,0:T(8,128)(2,1)S(1)} %pack.1), channel_id=1, source_target_pairs={{0,8},{1,9},{2,10},{3,11},{16,24},{17,25},{18,26},{19,27}} | collective-permute-start | bytes 786440 | tf_op jit(solution)/shard_map/ppermute | solution.py:355
  8.4 19.8 %collective-permute-start.2 = (bf16[2,512,128]{2,1,0:T(8,128)(2,1)S(1)}, bf16[2,512,128]{2,1,0:T(8,128)(2,1)}, u32[]{:S(2)}, u32[]{:S(2)}) collective-permute-start(bf16[2,512,128]{2,1,0:T(8,128)(2,1)S(1)} %pack.1), channel_id=1, source_target_pairs={{0,4},{4,8},{8,12},{1,5},{5,9},{9,13},{2,6},{6,10},{10,14},{3,7},{... | collective-permute-start | bytes 786440 | tf_op jit(solution)/shard_map/ppermute | solution.py:28
  15.2 14.1 %copy-start = (bf16[512,1024]{1,0:T(8,128)(2,1)S(1)}, bf16[512,1024]{1,0:T(8,128)(2,1)}, u32[]{:S(2)}) copy-start(bf16[512,1024]{1,0:T(8,128)(2,1)} %q_ref.5) | copy-start | bytes 3145732
  15.2 14.1 %copy-start.1 = (bf16[512,1024]{1,0:T(8,128)(2,1)S(1)}, bf16[512,1024]{1,0:T(8,128)(2,1)}, u32[]{:S(2)}) copy-start(bf16[512,1024]{1,0:T(8,128)(2,1)} %g_ref.5) | copy-start | bytes 3145732
  15.2 14.1 %copy-start.3 = (bf16[512,128]{1,0:T(8,128)(2,1)S(1)}, bf16[512,128]{1,0:T(8,128)(2,1)}, u32[]{:S(2)}) copy-start(bf16[512,128]{1,0:T(8,128)(2,1)} %rest_5_.5) | copy-start | bytes 393220
  15.2 14.1 %copy-start.5 = (bf16[512,128]{1,0:T(8,128)(2,1)S(1)}, bf16[512,128]{1,0:T(8,128)(2,1)}, u32[]{:S(2)}) copy-start(bf16[512,128]{1,0:T(8,128)(2,1)} %rest_6_.5) | copy-start | bytes 393220
  15.2 14.1 %copy-start.6 = (f32[512]{0:T(512)S(1)}, f32[512]{0:T(512)}, u32[]{:S(2)}) copy-start(f32[512]{0:T(512)} %param.15) | copy-start | bytes 6148
  15.2 13.9 %collective-permute-start.3 = (bf16[2,512,128]{2,1,0:T(8,128)(2,1)S(1)}, bf16[2,512,128]{2,1,0:T(8,128)(2,1)}, u32[]{:S(2)}, u32[]{:S(2)}) collective-permute-start(bf16[2,512,128]{2,1,0:T(8,128)(2,1)S(1)} %broadcast_select_fusion), channel_id=1, source_target_pairs={{8,12},{9,13},{10,14},{11,15},{24,28},{25,29},{26,30},{27,31}} | collective-permute-start | bytes 786440 | tf_op jit(solution)/shard_map/ppermute | solution.py:363
  18.7 20.6 %collective-permute-start.4 = (bf16[1,1,8,128,128]{4,3,2,1,0:T(8,128)(2,1)}, bf16[1,1,8,128,128]{4,3,2,1,0:T(8,128)(2,1)S(1)}, u32[]{:S(2)}, u32[]{:S(2)}) collective-permute-start(bf16[1,1,8,128,128]{4,3,2,1,0:T(8,128)(2,1)} %get-tuple-element.55), channel_id=1, source_target_pairs={{0,4},{4,8},{8,12},{1,5},{5,9},{9,13},{2,6},{6,10},{10,14},{3,7},{... | collective-permute-start | bytes 786440 | tf_op jit(solution)/shard_map/ppermute | solution.py:28
  21.1 24.0 %collective-permute-start.1 = (bf16[2,1,8,128,128]{4,3,2,1,0:T(8,128)(2,1)S(1)}, bf16[2,1,8,128,128]{4,3,2,1,0:T(8,128)(2,1)S(1)}, u32[]{:S(2)}, u32[]{:S(2)}) collective-permute-start(bf16[2,1,8,128,128]{4,3,2,1,0:T(8,128)(2,1)S(1)} %pad_maximum_fusion.1), channel_id=1, source_target_pairs={{0,4},{4,8},{8,12},{1,5},{5,9},{9,13},{2,6},{6,10},{10,14},{3,7},{... | collective-permute-start | bytes 1572872 | tf_op jit(solution)/shard_map/ppermute | solution.py:28
  50.8 7.4 %collective-permute-start.5 = (bf16[2,2,128,128]{3,2,1,0:T(8,128)(2,1)S(1)}, bf16[2,2,128,128]{3,2,1,0:T(8,128)(2,1)S(1)}, u32[]{:S(2)}, u32[]{:S(2)}) collective-permute-start(bf16[2,2,128,128]{3,2,1,0:T(8,128)(2,1)S(1)} %add_convert_fusion.2), channel_id=1, source_target_pairs={{4,0},{8,4},{12,8},{5,1},{9,5},{13,9},{6,2},{10,6},{14,10},{7,3},{... | collective-permute-start | bytes 393224 | tf_op jit(solution)/shard_map/ppermute | solution.py:28
  52.1 7.5 %collective-permute-start.7 = (bf16[512,128]{1,0:T(8,128)(2,1)S(1)}, bf16[512,128]{1,0:T(8,128)(2,1)S(1)}, u32[]{:S(2)}, u32[]{:S(2)}) collective-permute-start(bf16[512,128]{1,0:T(8,128)(2,1)S(1)} %convert_element_type.23), channel_id=1, source_target_pairs={{4,0},{12,8},{5,1},{13,9},{6,2},{14,10},{7,3},{15,11},{20,16},{28,... | collective-permute-start | bytes 393224 | tf_op jit(solution)/shard_map/ppermute | solution.py:406
  53.4 9.1 %collective-permute-start.6 = (bf16[512,128]{1,0:T(8,128)(2,1)S(1)}, bf16[512,128]{1,0:T(8,128)(2,1)S(1)}, u32[]{:S(2)}, u32[]{:S(2)}) collective-permute-start(bf16[512,128]{1,0:T(8,128)(2,1)S(1)} %convert_element_type.22), channel_id=1, source_target_pairs={{4,0},{12,8},{5,1},{13,9},{6,2},{14,10},{7,3},{15,11},{20,16},{28,... | collective-permute-start | bytes 393224 | tf_op jit(solution)/shard_map/ppermute | solution.py:406
  58.1 2.8 %collective-permute-start.10 = (f32[512]{0:T(512)S(1)}, f32[512]{0:T(512)S(1)}, u32[]{:S(2)}, u32[]{:S(2)}) collective-permute-start(f32[512]{0:T(512)S(1)} %bitcast.14), channel_id=1, source_target_pairs={{0,16},{16,0},{1,17},{17,1},{2,18},{18,2},{3,19},{19,3},{4,20},{20... | collective-permute-start | bytes 6152 | tf_op jit(solution)/shard_map/ppermute | solution.py:37
  59.6 9.1 %collective-permute-start.9 = (bf16[512,128]{1,0:T(8,128)(2,1)S(1)}, bf16[512,128]{1,0:T(8,128)(2,1)S(1)}, u32[]{:S(2)}, u32[]{:S(2)}) collective-permute-start(bf16[512,128]{1,0:T(8,128)(2,1)S(1)} %add_convert_fusion), channel_id=1, source_target_pairs={{8,0},{9,1},{10,2},{11,3},{24,16},{25,17},{26,18},{27,19}} | collective-permute-start | bytes 393224 | tf_op jit(solution)/shard_map/ppermute | solution.py:406
  60.9 3.7 %collective-permute-start.11 = (f32[512]{0:T(512)S(1)}, f32[512]{0:T(512)S(1)}, u32[]{:S(2)}, u32[]{:S(2)}) collective-permute-start(f32[512]{0:T(512)S(1)} %add.30), channel_id=1, source_target_pairs={{0,1},{1,0},{2,3},{3,2},{4,5},{5,4},{6,7},{7,6},{8,9},{9,8},{10,11... | collective-permute-start | bytes 6152 | tf_op jit(solution)/shard_map/ppermute | solution.py:37
  62.5 7.8 %collective-permute-start.8 = (bf16[512,128]{1,0:T(8,128)(2,1)S(1)}, bf16[512,128]{1,0:T(8,128)(2,1)S(1)}, u32[]{:S(2)}, u32[]{:S(2)}) collective-permute-start(bf16[512,128]{1,0:T(8,128)(2,1)S(1)} %add_convert_fusion.1), channel_id=1, source_target_pairs={{8,0},{9,1},{10,2},{11,3},{24,16},{25,17},{26,18},{27,19}} | collective-permute-start | bytes 393224 | tf_op jit(solution)/shard_map/ppermute | solution.py:406
  64.6 3.6 %collective-permute-start.12 = (f32[512]{0:T(512)S(1)}, f32[512]{0:T(512)S(1)}, u32[]{:S(2)}, u32[]{:S(2)}) collective-permute-start(f32[512]{0:T(512)S(1)} %add.31), channel_id=1, source_target_pairs={{0,2},{1,3},{2,0},{3,1},{4,6},{5,7},{6,4},{7,5},{8,10},{9,11},{10,... | collective-permute-start | bytes 6152 | tf_op jit(solution)/shard_map/ppermute | solution.py:37

commit v5 on v4

--- a/solution.py
+++ b/solution.py
@@ -221,20 +221,32 @@
         dsv_ref[pl.ds(at, BLK), :] += dv[j * BLK:(j + 1) * BLK]
 
 
-def pack_kernel(*refs):
-    out = refs[-1]
-    for i, ref in enumerate(refs[:-1]):
-        out[i] = ref[...]
-
-
-def pack(arrays):
-    shape = arrays[0].shape
+def pack_kernel(key_ref, value_ref, tile_ref, pair_ref, all_ref):
+    blocks = key_ref.shape[0] // BLK
+    pair_ref[0] = key_ref[...]
+    pair_ref[1] = value_ref[...]
+    for i in range(blocks):
+        rows = slice(i * BLK, (i + 1) * BLK)
+        all_ref[i] = key_ref[rows]
+        all_ref[blocks + i] = value_ref[rows]
+    for h in range(tile_ref.shape[2]):
+        all_ref[2 * blocks + h] = tile_ref[0, 0, h]
+
+
+def pack(keys, vals, window):
+    tokens = keys.shape[0]
+    blocks, heads = tokens // BLK, window.shape[2]
+    flat = pl.BlockSpec((tokens, E), lambda i: (0, 0))
+    shapes = [(2, tokens, E), (2 * blocks + heads, BLK, BLK)]
     return pl.pallas_call(
         pack_kernel,
-        out_shape=jax.ShapeDtypeStruct((len(arrays), *shape), arrays[0].dtype),
+        out_shape=[jax.ShapeDtypeStruct(x, BF) for x in shapes],
+        grid=(1,),
+        in_specs=[flat, flat, pl.BlockSpec((1, 1, heads, BLK, BLK), lambda i: (blocks - 1, WIN - 1, 0, 0, 0))],
+        out_specs=[pl.BlockSpec(x, lambda i: (0, 0, 0)) for x in shapes],
         compiler_params=pltpu.CompilerParams(vmem_limit_bytes=16 * 1024 * 1024),
         name="pack",
-    )(*arrays)
+    )(keys, vals, window)
 
 
 def finish_kernel(root_ref, dk_ref, dv_ref, dsk_ref, dsv_ref, back_ref, *rest):
@@ -281,8 +293,9 @@
     specs = [pl.BlockSpec((BLK, columns), lambda i, *_: (first + i, 0))] * 2
     for d in range(WIN):
         if d in crossing:
-            args.append(incoming)
-            specs.append(pl.BlockSpec(tile, lambda i, *_, d=d: (crossing.index(d), 0, 0, 0, 0)))
+            arrived, skip = incoming
+            args.append(arrived)
+            specs.append(pl.BlockSpec(tile, lambda i, *_, d=d: (skip + crossing.index(d), 0, 0, 0, 0)))
         else:
             args.append(window)
             specs.append(pl.BlockSpec(tile, lambda i, *_, d=d: (first + i - d, d, 0, 0, 0)))
@@ -345,7 +358,8 @@
 
     tail = slice(tokens - LEAD * BLK, tokens)
     first_rows = slice(0, NGLOB * BLK)
-    pair = pack([key_rows, values])
+    pair, packed = pack(key_rows, values, teacher_window)
+    heads = teacher_window.shape[2]
     half = 1
     while 2 * half < count:
         half *= 2
@@ -356,24 +370,29 @@
         sinks = jnp.where(where % (2 * half) == half, came, sinks)
         known = sorted(known + [i + half for i in known if i + half < count])
         half //= 2
-    got = shift(pair, "seq", 1)
-    before = got[:, tail].reshape(2, LEAD, BLK, E)
+    got = shift(packed, "seq", 1)
+    got_pair = got[:2 * blocks].reshape(2, tokens, E)
+    before = got_pair[:, tail].reshape(2, LEAD, BLK, E)
+    if 2 * blocks % heads == 0:
+        arrived = (got.reshape(-1, 1, heads, BLK, BLK), 2 * blocks // heads)
+    else:
+        arrived = (got[2 * blocks:].reshape(1, 1, heads, BLK, BLK), 0)
+    incoming = {LEAD - 1: arrived}
     forward = [(i, i + 1) for i in known if i > 0 and i + 1 < count]
     if forward:
         came = lax.ppermute(sinks, "seq", forward)
         later = sinks
         sinks = jnp.where(where % 2 == 1, came, sinks)
-    sinks = jnp.where(where == 1, got[:, first_rows], sinks)
-
-    incoming = {}
-    for block in range(LEAD - 1, -1, -1):
+    sinks = jnp.where(where == 1, got_pair[:, first_rows], sinks)
+
+    for block in range(LEAD - 2, -1, -1):
         out = jnp.concatenate(
             [teacher_window[blocks + block - d:blocks + block - d + 1, d:d + 1] for d in range(block + 1, WIN)],
             axis=0,
         )
         if block == 0 and later is not None:
             out, _ = lax.optimization_barrier((out, later))
-        incoming[block] = shift(out, "seq", 1)
+        incoming[block] = (shift(out, "seq", 1), 0)
 
     own = (key_rows, values)
     sink_arrays = (sinks[0], sinks[1])
@@ -405,11 +424,13 @@
         low = [x.astype(BF) for x in sums]
         came = [lax.ppermute(x, "seq", route) for x in low]
         if number == 0:
-            returned = shift(back.astype(BF), "seq", -1)
+            row_terms = sum_over(row_terms, "grp")
+            leaving, row_terms = lax.optimization_barrier((back.astype(BF), row_terms))
+            returned = shift(leaving, "seq", -1)
         sums = [x + y.astype(F32) for x, y in zip(sums, came)]
         arrived += came
     row_terms, returned = lax.optimization_barrier((row_terms, returned))
-    row_loss = sum_over(sum_over(row_terms, "grp"), "head")
+    row_loss = sum_over(row_terms, "head")
     root = where.astype(jnp.int32).reshape(1)
     grads = finish(root, dk, dv, dsk, dsv, returned, arrived)
     return (query_grad, grads[0], grads[1], row_loss)

time: 71.6 us -> 77.1 us (1.077)
  waiting for transfers between devices: 12.9 us -> 27.5 us
  starting transfers between devices: 27.4 us -> 18.9 us
  other arithmetic: 2.86 us -> 1.9 us
    ppermute x4 -> x3, waiting for transfers between devices: 3.42 us -> 14.7 us  [shift(): return lax.ppermute(block, axis, route)]
    ppermute x4 -> x3, starting transfers between devices: 11.7 us -> 3.94 us  [shift(): return lax.ppermute(block, axis, route)]
    ppermute x4, waiting for transfers between devices: 2.95 us -> 5.75 us  [local(): came = [lax.ppermute(x, 'seq', route) for x in low]]
    unnamed x17 -> x19, local copies, waits for them, and re-layouts: 1.93 us -> 3.82 us
    concatenate x1, other arithmetic: 1 us -> 0.05 us  [local(): jnp.concatenate([teacher_window[blocks + block - d:blocks + block - d + 1...]
    slice x1 -> x2, local copies, waits for them, and re-layouts: 0.92 us -> 0.03 us  [the longest x1 0.02 us: local(): got_pair = got[:2 * blocks].reshape(2, tokens, E)]
    slice x1, local copies, waits for them, and re-layouts: 1.95 us -> 1.07 us  [local(): teacher_window[blocks + block - d:blocks + block - d + 1, d:d + 1]]
  transfers between devices with their start and end apart: 13 -> 12, of which waited for: 6 -> 7; matrix products, arithmetic and copies ran while one was open for 8% -> 4% of each run, Pallas kernels for 22% -> 21%
where the time goes in v5:
time: 77.1 us; the launch traced here: 76.6 us
  waiting for transfers between devices  27.5 us (36%)
  Pallas kernels  22.4 us (29%)
  starting transfers between devices  18.9 us (25%)
  local copies, waits for them, and re-layouts  4.94 us (6%)
  other arithmetic  1.9 us (2%)
  between operations  0.97 us (1%)
    pallas_call x3, Pallas kernels, run_blocks(): pl.pallas_call(functools.partial(block_kernel, first, crossing, slots, ch...  21.5 us
    ppermute x3, waiting for transfers between devices, shift(): return lax.ppermute(block, axis, route)  14.7 us
    ppermute x1, starting transfers between devices, local(): lax.ppermute(sinks, 'seq', [(i, i + half) for i in known if i + half < co...  5.96 us
    ppermute x4, waiting for transfers between devices, local(): came = [lax.ppermute(x, 'seq', route) for x in low]  5.75 us
    ppermute x1, waiting for transfers between devices, local(): lax.ppermute(sinks, 'seq', [(i, i + half) for i in known if i + half < co...  5.26 us
    ppermute x4, starting transfers between devices, local(): came = [lax.ppermute(x, 'seq', route) for x in low]  5.17 us
    ppermute x3, starting transfers between devices, shift(): return lax.ppermute(block, axis, route)  3.94 us
    unnamed x19, local copies, waits for them, and re-layouts  3.82 us
  transfers between devices with their start and end apart: 12, of which 7 were waited for; matrix products, arithmetic and copies ran while one was open for 4% of the time, Pallas kernels for 21%

profile of v5, /device:TPU:0, one launch (start us, length us, event | category | flops | bytes accessed | tf_op | source)
XLA Modules:
  0.0 76.6 jit_solution(9146930250400438855)
XLA Ops:
  0.6 1.9 %copy-done = bf16[4,3,8,128,128]{4,3,2,1,0:T(8,128)(2,1)S(1)} copy-done((bf16[4,3,8,128,128]{4,3,2,1,0:T(8,128)(2,1)S(1)}, bf16[4,3,8,128,128]{4,3,2,1,0:T(8,128)(2,1)}, u32[]{:S(2)}) %copy-start) | copy-done | bytes 3145752
  2.5 0.9 %copy-done.3 = bf16[512,128]{1,0:T(8,128)(2,1)S(1)} copy-done((bf16[512,128]{1,0:T(8,128)(2,1)S(1)}, bf16[512,128]{1,0:T(8,128)(2,1)}, u32[]{:S(2)}) %copy-start.3) | copy-done | bytes 131096
  3.4 0.9 %copy-done.5 = bf16[512,128]{1,0:T(8,128)(2,1)S(1)} copy-done((bf16[512,128]{1,0:T(8,128)(2,1)S(1)}, bf16[512,128]{1,0:T(8,128)(2,1)}, u32[]{:S(2)}) %copy-start.5) | copy-done | bytes 131096
  4.3 0.1 pack.1
  4.4 6.0 %collective-permute-start = (bf16[2,512,128]{2,1,0:T(8,128)(2,1)S(1)}, bf16[2,512,128]{2,1,0:T(8,128)(2,1)S(1)}, u32[]{:S(2)}, u32[]{:S(2)}) collective-permute-start(bf16[2,512,128]{2,1,0:T(8,128)(2,1)S(1)} %get-tuple-element.33), channel_id=1, source_target_pairs={{0,8},{1,9},{2,10},{3,11},{16,24},{17,25},{18,26},{19,27}} | collective-permute-start | bytes 786440 | tf_op jit(solution)/shard_map/ppermute | solution.py:369
  10.4 1.3 %collective-permute-start.2 = (bf16[16,128,128]{2,1,0:T(8,128)(2,1)S(1)}, bf16[16,128,128]{2,1,0:T(8,128)(2,1)S(1)}, u32[]{:S(2)}, u32[]{:S(2)}) collective-permute-start(bf16[16,128,128]{2,1,0:T(8,128)(2,1)S(1)} %get-tuple-element.35), channel_id=1, source_target_pairs={{0,4},{4,8},{8,12},{1,5},{5,9},{9,13},{2,6},{6,10},{10,14},{3,7},{... | collective-permute-start | bytes 1572872 | tf_op jit(solution)/shard_map/ppermute | solution.py:28
  11.8 0.1 copy.14.picks_ref
  11.8 5.3 %collective-permute-done = bf16[2,512,128]{2,1,0:T(8,128)(2,1)S(1)} collective-permute-done((bf16[2,512,128]{2,1,0:T(8,128)(2,1)S(1)}, bf16[2,512,128]{2,1,0:T(8,128)(2,1)S(1)}, u32[]{:S(2)}, u32[]{:S(2)}) %collective-permute-start) | collective-permute-done | bytes 262176 | tf_op jit(solution)/shard_map/ppermute | solution.py:369
  17.2 0.8 %collective-permute-start.3 = (bf16[2,512,128]{2,1,0:T(8,128)(2,1)S(1)}, bf16[2,512,128]{2,1,0:T(8,128)(2,1)S(1)}, u32[]{:S(2)}, u32[]{:S(2)}) collective-permute-start(bf16[2,512,128]{2,1,0:T(8,128)(2,1)S(1)} %broadcast_select_fusion), channel_id=1, source_target_pairs={{8,12},{9,13},{10,14},{11,15},{24,28},{25,29},{26,30},{27,31}} | collective-permute-start | bytes 786440 | tf_op jit(solution)/shard_map/ppermute | solution.py:383
  18.0 1.1 %fusion = (bf16[1,1,8,128,128]{4,3,2,1,0:T(8,128)(2,1)S(1)}, bf16[1,1,8,128,128]{4,3,2,1,0:T(8,128)(2,1)S(1)}) fusion(bf16[4,3,8,128,128]{4,3,2,1,0:T(8,128)(2,1)} %rest_0_.5), kind=kLoop, calls=%fused_computation.10 | loop fusion | bytes 1048576 | tf_op jit(solution)/shard_map/slice | solution.py:390
  19.1 0.1 pad_maximum_fusion.1
  19.2 1.3 %collective-permute-start.1 = (bf16[2,1,8,128,128]{4,3,2,1,0:T(8,128)(2,1)S(1)}, bf16[2,1,8,128,128]{4,3,2,1,0:T(8,128)(2,1)S(1)}, u32[]{:S(2)}, u32[]{:S(2)}) collective-permute-start(bf16[2,1,8,128,128]{4,3,2,1,0:T(8,128)(2,1)S(1)} %pad_maximum_fusion.1), channel_id=1, source_target_pairs={{0,4},{4,8},{8,12},{1,5},{5,9},{9,13},{2,6},{6,10},{10,14},{3,7},{... | collective-permute-start | bytes 1572872 | tf_op jit(solution)/shard_map/ppermute | solution.py:28
  20.5 7.9 %collective-permute-done.2 = bf16[16,128,128]{2,1,0:T(8,128)(2,1)S(1)} collective-permute-done((bf16[16,128,128]{2,1,0:T(8,128)(2,1)S(1)}, bf16[16,128,128]{2,1,0:T(8,128)(2,1)S(1)}, u32[]{:S(2)}, u32[]{:S(2)}) %collective-permute-start.2) | collective-permute-done | bytes 524320 | tf_op jit(solution)/shard_map/ppermute | solution.py:28
  28.5 10.1 %blocks_from_2.1 = (bf16[256,1024]{1,0:T(8,128)(2,1)S(1)}, f32[2,1,128]{2,1,0:T(1,128)S(1)}, f32[512,128]{1,0:T(8,128)S(1)}, f32[512,128]{1,0:T(8,128)S(1)}, f32...) custom-call(s32[1]{0:T(128)} %bitcast.base_ref, s32[4,2]{1,0:T(4,128)S(1)} %copy.14.picks_ref, ...), custom_call_target="tpu_custom_call" | custom-call | flops 1677721600 | bytes 3932160 | tf_op jit(solution)/shard_map/blocks_from_2/pallas_call | solution.py:331
  38.6 5.7 %blocks_from_1.1 = (bf16[128,1024]{1,0:T(8,128)(2,1)S(1)}, f32[1,1,128]{2,1,0:T(1,128)S(1)}, f32[512,128]{1,0:T(8,128)S(1)}, f32[512,128]{1,0:T(8,128)S(1)}, f32...) custom-call(s32[1]{0:T(128)} %bitcast.base_ref, s32[4,2]{1,0:T(4,128)S(1)} %copy.14.picks_ref, ...), custom_call_target="tpu_custom_call" | custom-call | flops 838860800 | bytes 1966080 | tf_op jit(solution)/shard_map/blocks_from_1/pallas_call | solution.py:331
  44.4 5.7 %blocks_from_0.1 = (bf16[128,1024]{1,0:T(8,128)(2,1)S(1)}, f32[1,1,128]{2,1,0:T(1,128)S(1)}, f32[512,128]{1,0:T(8,128)S(1)}, f32[512,128]{1,0:T(8,128)S(1)}, f32...) custom-call(s32[1]{0:T(128)} %bitcast.base_ref, s32[4,2]{1,0:T(4,128)S(1)} %copy.14.picks_ref, ...), custom_call_target="tpu_custom_call" | custom-call | flops 838860800 | bytes 1966080 | tf_op jit(solution)/shard_map/blocks_from_0/pallas_call | solution.py:331
  50.1 0.1 collective-permute-start.4
  50.2 1.3 %collective-permute-start.7 = (bf16[512,128]{1,0:T(8,128)(2,1)S(1)}, bf16[512,128]{1,0:T(8,128)(2,1)S(1)}, u32[]{:S(2)}, u32[]{:S(2)}) collective-permute-start(bf16[512,128]{1,0:T(8,128)(2,1)S(1)} %convert_element_type.23), channel_id=1, source_target_pairs={{4,0},{12,8},{5,1},{13,9},{6,2},{14,10},{7,3},{15,11},{20,16},{28,... | collective-permute-start | bytes 393224 | tf_op jit(solution)/shard_map/ppermute | solution.py:425
  51.5 1.3 %collective-permute-start.6 = (bf16[512,128]{1,0:T(8,128)(2,1)S(1)}, bf16[512,128]{1,0:T(8,128)(2,1)S(1)}, u32[]{:S(2)}, u32[]{:S(2)}) collective-permute-start(bf16[512,128]{1,0:T(8,128)(2,1)S(1)} %convert_element_type.22), channel_id=1, source_target_pairs={{4,0},{12,8},{5,1},{13,9},{6,2},{14,10},{7,3},{15,11},{20,16},{28,... | collective-permute-start | bytes 393224 | tf_op jit(solution)/shard_map/ppermute | solution.py:425
  52.9 1.3 %collective-permute-start.5 = (bf16[2,2,128,128]{3,2,1,0:T(8,128)(2,1)S(1)}, bf16[2,2,128,128]{3,2,1,0:T(8,128)(2,1)S(1)}, u32[]{:S(2)}, u32[]{:S(2)}) collective-permute-start(bf16[2,2,128,128]{3,2,1,0:T(8,128)(2,1)S(1)} %add_convert_fusion.2), channel_id=1, source_target_pairs={{4,0},{8,4},{12,8},{5,1},{9,5},{13,9},{6,2},{10,6},{14,10},{7,3},{... | collective-permute-start | bytes 393224 | tf_op jit(solution)/shard_map/ppermute | solution.py:28
  54.2 4.2 %collective-permute-done.7.rest_1_ = bf16[512,128]{1,0:T(8,128)(2,1)S(1)} collective-permute-done((bf16[512,128]{1,0:T(8,128)(2,1)S(1)}, bf16[512,128]{1,0:T(8,128)(2,1)S(1)}, u32[]{:S(2)}, u32[]{:S(2)}) %collective-permute-start.7) | collective-permute-done | bytes 131104 | tf_op jit(solution)/shard_map/ppermute | solution.py:425
  58.4 1.3 %collective-permute-start.9 = (bf16[512,128]{1,0:T(8,128)(2,1)S(1)}, bf16[512,128]{1,0:T(8,128)(2,1)S(1)}, u32[]{:S(2)}, u32[]{:S(2)}) collective-permute-start(bf16[512,128]{1,0:T(8,128)(2,1)S(1)} %add_convert_fusion), channel_id=1, source_target_pairs={{8,0},{9,1},{10,2},{11,3},{24,16},{25,17},{26,18},{27,19}} | collective-permute-start | bytes 393224 | tf_op jit(solution)/shard_map/ppermute | solution.py:425
  59.7 6.8 %collective-permute-done.5.back_ref = bf16[2,2,128,128]{3,2,1,0:T(8,128)(2,1)S(1)} collective-permute-done((bf16[2,2,128,128]{3,2,1,0:T(8,128)(2,1)S(1)}, bf16[2,2,128,128]{3,2,1,0:T(8,128)(2,1)S(1)}, u32[]{:S(2)}, u32[]{:S(2)}) %collective-permute-start.5) | collective-permute-done | bytes 131104 | tf_op jit(solution)/shard_map/ppermute | solution.py:28
  66.5 1.5 %collective-permute-start.10 = (f32[512]{0:T(512)S(1)}, f32[512]{0:T(512)S(1)}, u32[]{:S(2)}, u32[]{:S(2)}) collective-permute-start(f32[512]{0:T(512)S(1)} %add.28), channel_id=1, source_target_pairs={{0,1},{1,0},{2,3},{3,2},{4,5},{5,4},{6,7},{7,6},{8,9},{9,8},{10,11... | collective-permute-start | bytes 6152 | tf_op jit(solution)/shard_map/ppermute | solution.py:37
  68.1 1.3 %collective-permute-start.8 = (bf16[512,128]{1,0:T(8,128)(2,1)S(1)}, bf16[512,128]{1,0:T(8,128)(2,1)S(1)}, u32[]{:S(2)}, u32[]{:S(2)}) collective-permute-start(bf16[512,128]{1,0:T(8,128)(2,1)S(1)} %add_convert_fusion.1), channel_id=1, source_target_pairs={{8,0},{9,1},{10,2},{11,3},{24,16},{25,17},{26,18},{27,19}} | collective-permute-start | bytes 393224 | tf_op jit(solution)/shard_map/ppermute | solution.py:425
  69.4 0.8 collective-permute-done.10
  70.1 1.5 %collective-permute-start.11 = (f32[512]{0:T(512)S(1)}, f32[512]{0:T(512)S(1)}, u32[]{:S(2)}, u32[]{:S(2)}) collective-permute-start(f32[512]{0:T(512)S(1)} %add.31), channel_id=1, source_target_pairs={{0,2},{1,3},{2,0},{3,1},{4,6},{5,7},{6,4},{7,5},{8,10},{9,11},{10,... | collective-permute-start | bytes 6152 | tf_op jit(solution)/shard_map/ppermute | solution.py:37
  71.7 1.0 %pad_maximum_fusion = bf16[512,1024]{1,0:T(8,128)(2,1)} fusion(bf16[256,1024]{1,0:T(8,128)(2,1)S(1)} %get-tuple-element.46, bf16[128,1024]{1,0:T(8,128)(2,1)S(1)} %get-tuple-element.45, bf16[128,1024]{1,0:T(8,128)(2,1)S(1)} %get-tuple-element.44), kind=kLoop, calls=%fused_computation | loop fusion | flops 3145728 | bytes 2097152 | tf_op jit(solution)/shard_map/concatenate | solution.py:411
  72.7 1.0 %collective-permute-done.11 = f32[512]{0:T(512)S(1)} collective-permute-done((f32[512]{0:T(512)S(1)}, f32[512]{0:T(512)S(1)}, u32[]{:S(2)}, u32[]{:S(2)}) %collective-permute-start.11) | collective-permute-done | bytes 2080 | tf_op jit(solution)/shard_map/ppermute | solution.py:37
  73.7 0.6 add.32
  74.3 1.5 %collective-permute-done.8.rest_2_ = bf16[512,128]{1,0:T(8,128)(2,1)S(1)} collective-permute-done((bf16[512,128]{1,0:T(8,128)(2,1)S(1)}, bf16[512,128]{1,0:T(8,128)(2,1)S(1)}, u32[]{:S(2)}, u32[]{:S(2)}) %collective-permute-start.8) | collective-permute-done | bytes 131104 | tf_op jit(solution)/shard_map/ppermute | solution.py:425
  75.8 0.8 %finish.1 = (bf16[512,128]{1,0:T(8,128)(2,1)}, bf16[512,128]{1,0:T(8,128)(2,1)}) custom-call(s32[1]{0:T(128)} %bitcast.7.root_ref, f32[512,128]{1,0:T(8,128)S(1)} %get-tuple-element.47.dk_ref, f32[512,128]{1,0:T(8,128)S(1)} %get-tuple-element.48.dv_ref, f32[512,128]{1,0:T(8,128)S(1)} %get-tuple-element.49.dsk_ref, f32[512,128]{1,0:T(8,128)S(1)} %get-tuple-element.50.dsv_ref, ...), custom_call_target="tpu_custom_call" | custom-call | tf_op jit(solution)/shard_map/finish/pallas_call | solution.py:273
  (33 shorter events, 0.3 us)
Async XLA Ops:
  0.6 1.9 %copy-start = (bf16[4,3,8,128,128]{4,3,2,1,0:T(8,128)(2,1)S(1)}, bf16[4,3,8,128,128]{4,3,2,1,0:T(8,128)(2,1)}, u32[]{:S(2)}) copy-start(bf16[4,3,8,128,128]{4,3,2,1,0:T(8,128)(2,1)} %rest_0_.5) | copy-start | bytes 9437188
  2.5 0.9 %copy-start.3 = (bf16[512,128]{1,0:T(8,128)(2,1)S(1)}, bf16[512,128]{1,0:T(8,128)(2,1)}, u32[]{:S(2)}) copy-start(bf16[512,128]{1,0:T(8,128)(2,1)} %rest_5_.5) | copy-start | bytes 393220
  3.4 0.9 %copy-start.5 = (bf16[512,128]{1,0:T(8,128)(2,1)S(1)}, bf16[512,128]{1,0:T(8,128)(2,1)}, u32[]{:S(2)}) copy-start(bf16[512,128]{1,0:T(8,128)(2,1)} %rest_6_.5) | copy-start | bytes 393220
  4.3 7.4 %copy-start.8 = (s32[4,2]{0,1:T(2,128)S(1)}, s32[4,2]{0,1:T(2,128)}, u32[]{:S(2)}) copy-start(s32[4,2]{0,1:T(2,128)} %param.14) | copy-start | bytes 100
  4.4 12.7 %collective-permute-start = (bf16[2,512,128]{2,1,0:T(8,128)(2,1)S(1)}, bf16[2,512,128]{2,1,0:T(8,128)(2,1)S(1)}, u32[]{:S(2)}, u32[]{:S(2)}) collective-permute-start(bf16[2,512,128]{2,1,0:T(8,128)(2,1)S(1)} %get-tuple-element.33), channel_id=1, source_target_pairs={{0,8},{1,9},{2,10},{3,11},{16,24},{17,25},{18,26},{19,27}} | collective-permute-start | bytes 786440 | tf_op jit(solution)/shard_map/ppermute | solution.py:369
  10.4 18.0 %collective-permute-start.2 = (bf16[16,128,128]{2,1,0:T(8,128)(2,1)S(1)}, bf16[16,128,128]{2,1,0:T(8,128)(2,1)S(1)}, u32[]{:S(2)}, u32[]{:S(2)}) collective-permute-start(bf16[16,128,128]{2,1,0:T(8,128)(2,1)S(1)} %get-tuple-element.35), channel_id=1, source_target_pairs={{0,4},{4,8},{8,12},{1,5},{5,9},{9,13},{2,6},{6,10},{10,14},{3,7},{... | collective-permute-start | bytes 1572872 | tf_op jit(solution)/shard_map/ppermute | solution.py:28
  17.1 11.3 %copy-start.1 = (bf16[512,1024]{1,0:T(8,128)(2,1)S(1)}, bf16[512,1024]{1,0:T(8,128)(2,1)}, u32[]{:S(2)}) copy-start(bf16[512,1024]{1,0:T(8,128)(2,1)} %q_ref.5) | copy-start | bytes 3145732
  17.2 11.3 %copy-start.2 = (bf16[512,1024]{1,0:T(8,128)(2,1)S(1)}, bf16[512,1024]{1,0:T(8,128)(2,1)}, u32[]{:S(2)}) copy-start(bf16[512,1024]{1,0:T(8,128)(2,1)} %g_ref.5) | copy-start | bytes 3145732
  17.2 11.3 %copy-start.4 = (bf16[512,128]{1,0:T(8,128)(2,1)S(1)}, bf16[512,128]{1,0:T(8,128)(2,1)}, u32[]{:S(2)}) copy-start(bf16[512,128]{1,0:T(8,128)(2,1)} %rest_5_.5) | copy-start | bytes 393220
  17.2 11.3 %copy-start.6 = (bf16[512,128]{1,0:T(8,128)(2,1)S(1)}, bf16[512,128]{1,0:T(8,128)(2,1)}, u32[]{:S(2)}) copy-start(bf16[512,128]{1,0:T(8,128)(2,1)} %rest_6_.5) | copy-start | bytes 393220
  17.2 11.3 %copy-start.7 = (f32[512]{0:T(512)S(1)}, f32[512]{0:T(512)}, u32[]{:S(2)}) copy-start(f32[512]{0:T(512)} %param.15) | copy-start | bytes 6148
  17.2 11.2 %collective-permute-start.3 = (bf16[2,512,128]{2,1,0:T(8,128)(2,1)S(1)}, bf16[2,512,128]{2,1,0:T(8,128)(2,1)S(1)}, u32[]{:S(2)}, u32[]{:S(2)}) collective-permute-start(bf16[2,512,128]{2,1,0:T(8,128)(2,1)S(1)} %broadcast_select_fusion), channel_id=1, source_target_pairs={{8,12},{9,13},{10,14},{11,15},{24,28},{25,29},{26,30},{27,31}} | collective-permute-start | bytes 786440 | tf_op jit(solution)/shard_map/ppermute | solution.py:383
  19.2 25.2 %collective-permute-start.1 = (bf16[2,1,8,128,128]{4,3,2,1,0:T(8,128)(2,1)S(1)}, bf16[2,1,8,128,128]{4,3,2,1,0:T(8,128)(2,1)S(1)}, u32[]{:S(2)}, u32[]{:S(2)}) collective-permute-start(bf16[2,1,8,128,128]{4,3,2,1,0:T(8,128)(2,1)S(1)} %pad_maximum_fusion.1), channel_id=1, source_target_pairs={{0,4},{4,8},{8,12},{1,5},{5,9},{9,13},{2,6},{6,10},{10,14},{3,7},{... | collective-permute-start | bytes 1572872 | tf_op jit(solution)/shard_map/ppermute | solution.py:28
  50.1 2.8 %collective-permute-start.4 = (f32[512]{0:T(512)S(1)}, f32[512]{0:T(512)S(1)}, u32[]{:S(2)}, u32[]{:S(2)}) collective-permute-start(f32[512]{0:T(512)S(1)} %bitcast.21), channel_id=1, source_target_pairs={{0,16},{16,0},{1,17},{17,1},{2,18},{18,2},{3,19},{19,3},{4,20},{20... | collective-permute-start | bytes 6152 | tf_op jit(solution)/shard_map/ppermute | solution.py:37
  50.2 8.2 %collective-permute-start.7 = (bf16[512,128]{1,0:T(8,128)(2,1)S(1)}, bf16[512,128]{1,0:T(8,128)(2,1)S(1)}, u32[]{:S(2)}, u32[]{:S(2)}) collective-permute-start(bf16[512,128]{1,0:T(8,128)(2,1)S(1)} %convert_element_type.23), channel_id=1, source_target_pairs={{4,0},{12,8},{5,1},{13,9},{6,2},{14,10},{7,3},{15,11},{20,16},{28,... | collective-permute-start | bytes 393224 | tf_op jit(solution)/shard_map/ppermute | solution.py:425
  51.5 16.5 %collective-permute-start.6 = (bf16[512,128]{1,0:T(8,128)(2,1)S(1)}, bf16[512,128]{1,0:T(8,128)(2,1)S(1)}, u32[]{:S(2)}, u32[]{:S(2)}) collective-permute-start(bf16[512,128]{1,0:T(8,128)(2,1)S(1)} %convert_element_type.22), channel_id=1, source_target_pairs={{4,0},{12,8},{5,1},{13,9},{6,2},{14,10},{7,3},{15,11},{20,16},{28,... | collective-permute-start | bytes 393224 | tf_op jit(solution)/shard_map/ppermute | solution.py:425
  52.9 13.7 %collective-permute-start.5 = (bf16[2,2,128,128]{3,2,1,0:T(8,128)(2,1)S(1)}, bf16[2,2,128,128]{3,2,1,0:T(8,128)(2,1)S(1)}, u32[]{:S(2)}, u32[]{:S(2)}) collective-permute-start(bf16[2,2,128,128]{3,2,1,0:T(8,128)(2,1)S(1)} %add_convert_fusion.2), channel_id=1, source_target_pairs={{4,0},{8,4},{12,8},{5,1},{9,5},{13,9},{6,2},{10,6},{14,10},{7,3},{... | collective-permute-start | bytes 393224 | tf_op jit(solution)/shard_map/ppermute | solution.py:28
  58.4 15.9 %collective-permute-start.9 = (bf16[512,128]{1,0:T(8,128)(2,1)S(1)}, bf16[512,128]{1,0:T(8,128)(2,1)S(1)}, u32[]{:S(2)}, u32[]{:S(2)}) collective-permute-start(bf16[512,128]{1,0:T(8,128)(2,1)S(1)} %add_convert_fusion), channel_id=1, source_target_pairs={{8,0},{9,1},{10,2},{11,3},{24,16},{25,17},{26,18},{27,19}} | collective-permute-start | bytes 393224 | tf_op jit(solution)/shard_map/ppermute | solution.py:425
  66.5 3.6 %collective-permute-start.10 = (f32[512]{0:T(512)S(1)}, f32[512]{0:T(512)S(1)}, u32[]{:S(2)}, u32[]{:S(2)}) collective-permute-start(f32[512]{0:T(512)S(1)} %add.28), channel_id=1, source_target_pairs={{0,1},{1,0},{2,3},{3,2},{4,5},{5,4},{6,7},{7,6},{8,9},{9,8},{10,11... | collective-permute-start | bytes 6152 | tf_op jit(solution)/shard_map/ppermute | solution.py:37
  68.1 7.8 %collective-permute-start.8 = (bf16[512,128]{1,0:T(8,128)(2,1)S(1)}, bf16[512,128]{1,0:T(8,128)(2,1)S(1)}, u32[]{:S(2)}, u32[]{:S(2)}) collective-permute-start(bf16[512,128]{1,0:T(8,128)(2,1)S(1)} %add_convert_fusion.1), channel_id=1, source_target_pairs={{8,0},{9,1},{10,2},{11,3},{24,16},{25,17},{26,18},{27,19}} | collective-permute-start | bytes 393224 | tf_op jit(solution)/shard_map/ppermute | solution.py:425
  70.1 3.6 %collective-permute-start.11 = (f32[512]{0:T(512)S(1)}, f32[512]{0:T(512)S(1)}, u32[]{:S(2)}, u32[]{:S(2)}) collective-permute-start(f32[512]{0:T(512)S(1)} %add.31), channel_id=1, source_target_pairs={{0,2},{1,3},{2,0},{3,1},{4,6},{5,7},{6,4},{7,5},{8,10},{9,11},{10,... | collective-permute-start | bytes 6152 | tf_op jit(solution)/shard_map/ppermute | solution.py:37

commit v6 on v2

--- a/solution.py
+++ b/solution.py
@@ -234,8 +234,8 @@
     specs = [pl.BlockSpec((BLK, columns), lambda i, *_: (first + i, 0))] * 2
     for d in range(WIN):
         if d in crossing:
-            args.append(incoming[d])
-            specs.append(pl.BlockSpec(tile, lambda i, *_: (0, 0, 0, 0, 0)))
+            args.append(incoming)
+            specs.append(pl.BlockSpec(tile, lambda i, *_, d=d: (crossing.index(d), 0, 0, 0, 0)))
         else:
             args.append(window)
             specs.append(pl.BlockSpec(tile, lambda i, *_, d=d: (first + i - d, d, 0, 0, 0)))
@@ -299,30 +299,35 @@
     tail = slice(tokens - LEAD * BLK, tokens)
     first_rows = slice(0, NGLOB * BLK)
     pair = jnp.stack([key_rows, values])
+    known = pair[:, first_rows]
+    far = {}
+    for times in range(min(FAN, count) - 1, 1, -1):
+        far[times] = lax.ppermute(known, "seq", [(0, times)])
+    tiles = [
+        jnp.concatenate(
+            [teacher_window[blocks + block - d:blocks + block - d + 1, d:d + 1] for d in range(block + 1, WIN)],
+            axis=0,
+        )
+        for block in range(LEAD)
+    ]
+    pair, *tiles = lax.optimization_barrier((pair, *tiles))
     got = shift(pair, "seq", 1)
     before = got[:, tail].reshape(2, LEAD, BLK, E)
-    sinks = jnp.where(where == 0, pair[:, first_rows], got[:, first_rows])
-    span, known = 1, pair[:, first_rows]
+    sinks = jnp.where(where == 0, known, got[:, first_rows])
+    for times, more in far.items():
+        sinks = jnp.where(where == times, more, sinks)
+    span = FAN
     while span < count:
-        for times in range(1, FAN):
-            if span == 1 and times == 1:
-                continue
+        more = sinks
+        for times in range(FAN - 1, 0, -1):
             route = [(i, i + times * span) for i in range(span) if i + times * span < count]
             if route:
-                more = lax.ppermute(known, "seq", route)
-                sinks = jnp.where((where >= times * span) & (where < (times + 1) * span), more, sinks)
+                came = lax.ppermute(sinks, "seq", route)
+                more = jnp.where((where >= times * span) & (where < (times + 1) * span), came, more)
+        sinks = more
         span *= FAN
-        known = sinks
-
-    incoming = {}
-    for block in range(LEAD - 1, -1, -1):
-        offsets = list(range(block + 1, WIN))
-        out = jnp.concatenate(
-            [teacher_window[blocks + block - d:blocks + block - d + 1, d:d + 1] for d in offsets], axis=0
-        )
-        came = shift(out, "seq", 1)
-        incoming[block] = {d: came[i:i + 1] for i, d in enumerate(offsets)}
-
+
+    incoming = {block: shift(tiles[block], "seq", 1) for block in range(LEAD - 1, -1, -1)}
     own = (key_rows, values)
     sink_arrays = (sinks[0], sinks[1])
     run = lambda first, n, acc: run_blocks(

time: 69.4 us -> 71.3 us (1.027)
  waiting for transfers between devices: 14.1 us -> 16.2 us
    ppermute x4, waiting for transfers between devices: 0.01 us -> 5.63 us  [shift(): return lax.ppermute(block, axis, route)]
    ppermute x2, waiting for transfers between devices: 5.69 us -> 2.18 us  [local(): far[times] = lax.ppermute(known, 'seq', [(0, times)])]
    ppermute x4, starting transfers between devices: 8.96 us -> 6.24 us  [shift(): return lax.ppermute(block, axis, route)]
    ppermute x2, starting transfers between devices: 7.16 us -> 9.77 us  [local(): far[times] = lax.ppermute(known, 'seq', [(0, times)])]
  transfers between devices with their start and end apart: 13 -> 13, of which waited for: 6 -> 7; matrix products, arithmetic and copies ran while one was open for 8% -> 8% of each run, Pallas kernels for 23% -> 22%
where the time goes in v6:
time: 71.3 us; the launch traced here: 70.9 us
  starting transfers between devices  24.3 us (34%)
  Pallas kernels  21.4 us (30%)
  waiting for transfers between devices  16.2 us (23%)
  other arithmetic  5.93 us (8%)
  local copies, waits for them, and re-layouts  2.04 us (3%)
  between operations  0.9 us (1%)
    pallas_call x3, Pallas kernels, run_blocks(): pl.pallas_call(functools.partial(block_kernel, first, crossing, slots, ch...  21.4 us
    ppermute x2, starting transfers between devices, local(): far[times] = lax.ppermute(known, 'seq', [(0, times)])  9.77 us
    ppermute x4, starting transfers between devices, shift(): return lax.ppermute(block, axis, route)  6.24 us
    ppermute x4, waiting for transfers between devices, shift(): return lax.ppermute(block, axis, route)  5.63 us
    ppermute x4, starting transfers between devices, local(): came = [lax.ppermute(x, 'seq', route) for x in low]  5.17 us
    ppermute x4, waiting for transfers between devices, local(): came = [lax.ppermute(x, 'seq', route) for x in low]  4.34 us
    ppermute x3, waiting for transfers between devices, sum_over(): lax.ppermute(block, axis, [(i, i ^ step) for i in range(count)])  4.09 us
    ppermute x3, starting transfers between devices, sum_over(): lax.ppermute(block, axis, [(i, i ^ step) for i in range(count)])  3.15 us
  transfers between devices with their start and end apart: 13, of which 7 were waited for; matrix products, arithmetic and copies ran while one was open for 8% of the time, Pallas kernels for 22%

profile of v6, /device:TPU:0, one launch (start us, length us, event | category | flops | bytes accessed | tf_op | source)
XLA Modules:
  0.0 70.9 jit_solution(6570242411745806673)
XLA Ops:
  0.7 1.8 %pad_maximum_fusion.2 = bf16[2,512,128]{2,1,0:T(8,128)(2,1)} fusion(bf16[1,512,128]{2,1,0:T(8,128)(2,1)} %bitcast.16, bf16[1,512,128]{2,1,0:T(8,128)(2,1)} %bitcast.14), kind=kLoop, calls=%fused_computation.2 | loop fusion | flops 131072 | bytes 524288 | tf_op jit(solution)/shard_map/stack | solution.py:301
  2.4 7.8 %collective-permute-start.2 = (bf16[2,512,128]{2,1,0:T(8,128)(2,1)}, bf16[2,512,128]{2,1,0:T(8,128)(2,1)}, u32[]{:S(2)}, u32[]{:S(2)}) collective-permute-start(bf16[2,512,128]{2,1,0:T(8,128)(2,1)} %pad_maximum_fusion.2), channel_id=1, source_target_pairs={{0,12},{1,13},{2,14},{3,15},{16,28},{17,29},{18,30},{19,31}} | collective-permute-start | bytes 786440 | tf_op jit(solution)/shard_map/ppermute | solution.py:305
  10.2 2.0 %collective-permute-start.1 = (bf16[2,512,128]{2,1,0:T(8,128)(2,1)}, bf16[2,512,128]{2,1,0:T(8,128)(2,1)}, u32[]{:S(2)}, u32[]{:S(2)}) collective-permute-start(bf16[2,512,128]{2,1,0:T(8,128)(2,1)} %pad_maximum_fusion.2), channel_id=1, source_target_pairs={{0,8},{1,9},{2,10},{3,11},{16,24},{17,25},{18,26},{19,27}} | collective-permute-start | bytes 786440 | tf_op jit(solution)/shard_map/ppermute | solution.py:305
  12.2 1.9 %fusion.2 = (bf16[1,1,8,128,128]{4,3,2,1,0:T(8,128)(2,1)}, bf16[1,1,8,128,128]{4,3,2,1,0:T(8,128)(2,1)S(1)}, bf16[1,1,8,128,128]{4,3,2,1,0:T(8,128)(2,1)S(1)}) fusion(bf16[4,3,8,128,128]{4,3,2,1,0:T(8,128)(2,1)} %rest_0_.5), kind=kLoop, calls=%fused_computation.18 | loop fusion | bytes 1572864 | tf_op jit(solution)/shard_map/slice | solution.py:308
  14.1 0.8 %pad_maximum_fusion.1 = bf16[2,1,8,128,128]{4,3,2,1,0:T(8,128)(2,1)} fusion(bf16[1,1,8,128,128]{4,3,2,1,0:T(8,128)(2,1)S(1)} %get-tuple-element.119, bf16[1,1,8,128,128]{4,3,2,1,0:T(8,128)(2,1)S(1)} %get-tuple-element.120), kind=kLoop, calls=%fused_computation.1 | loop fusion | flops 262144 | bytes 1048576 | tf_op jit(solution)/shard_map/concatenate | solution.py:307
  14.9 1.3 %collective-permute-start.3 = (bf16[2,512,128]{2,1,0:T(8,128)(2,1)}, bf16[2,512,128]{2,1,0:T(8,128)(2,1)S(1)}, u32[]{:S(2)}, u32[]{:S(2)}) collective-permute-start(bf16[2,512,128]{2,1,0:T(8,128)(2,1)} %pad_maximum_fusion.2), channel_id=1, source_target_pairs={{0,4},{4,8},{8,12},{1,5},{5,9},{9,13},{2,6},{6,10},{10,14},{3,7},{... | collective-permute-start | bytes 786440 | tf_op jit(solution)/shard_map/ppermute | solution.py:28
  16.2 1.3 %collective-permute-start.4 = (bf16[1,1,8,128,128]{4,3,2,1,0:T(8,128)(2,1)}, bf16[1,1,8,128,128]{4,3,2,1,0:T(8,128)(2,1)S(1)}, u32[]{:S(2)}, u32[]{:S(2)}) collective-permute-start(bf16[1,1,8,128,128]{4,3,2,1,0:T(8,128)(2,1)} %get-tuple-element.95), channel_id=1, source_target_pairs={{0,4},{4,8},{8,12},{1,5},{5,9},{9,13},{2,6},{6,10},{10,14},{3,7},{... | collective-permute-start | bytes 786440 | tf_op jit(solution)/shard_map/ppermute | solution.py:28
  17.5 2.3 %collective-permute-start = (bf16[2,1,8,128,128]{4,3,2,1,0:T(8,128)(2,1)}, bf16[2,1,8,128,128]{4,3,2,1,0:T(8,128)(2,1)S(1)}, u32[]{:S(2)}, u32[]{:S(2)}) collective-permute-start(bf16[2,1,8,128,128]{4,3,2,1,0:T(8,128)(2,1)} %pad_maximum_fusion.1), channel_id=1, source_target_pairs={{0,4},{4,8},{8,12},{1,5},{5,9},{9,13},{2,6},{6,10},{10,14},{3,7},{... | collective-permute-start | bytes 1572872 | tf_op jit(solution)/shard_map/ppermute | solution.py:28
  19.9 0.1 copy.14.picks_ref
  20.0 2.2 %collective-permute-done.1 = bf16[2,512,128]{2,1,0:T(8,128)(2,1)} collective-permute-done((bf16[2,512,128]{2,1,0:T(8,128)(2,1)}, bf16[2,512,128]{2,1,0:T(8,128)(2,1)}, u32[]{:S(2)}, u32[]{:S(2)}) %collective-permute-start.1) | collective-permute-done | bytes 262176 | tf_op jit(solution)/shard_map/ppermute | solution.py:305
  22.2 5.6 %collective-permute-done.3 = bf16[2,512,128]{2,1,0:T(8,128)(2,1)S(1)} collective-permute-done((bf16[2,512,128]{2,1,0:T(8,128)(2,1)}, bf16[2,512,128]{2,1,0:T(8,128)(2,1)S(1)}, u32[]{:S(2)}, u32[]{:S(2)}) %collective-permute-start.3) | collective-permute-done | bytes 262176 | tf_op jit(solution)/shard_map/ppermute | solution.py:28
  27.8 0.1 select_select_fusion
  27.9 10.0 %blocks_from_2.1 = (bf16[256,1024]{1,0:T(8,128)(2,1)S(1)}, f32[2,1,128]{2,1,0:T(1,128)S(1)}, f32[512,128]{1,0:T(8,128)S(1)}, f32[512,128]{1,0:T(8,128)S(1)}, f32...) custom-call(s32[1]{0:T(128)} %bitcast.base_ref, s32[4,2]{1,0:T(4,128)S(1)} %copy.14.picks_ref, bf16[512,1024]{1,0:T(8,128)(2,1)S(1)} %copy-done, ...), custom_call_target="tpu_custom_call" | custom-call | flops 1677721600 | bytes 3932160 | tf_op jit(solution)/shard_map/blocks_from_2/pallas_call | solution.py:271
  38.0 5.7 %blocks_from_1.1 = (bf16[128,1024]{1,0:T(8,128)(2,1)S(1)}, f32[1,1,128]{2,1,0:T(1,128)S(1)}, f32[512,128]{1,0:T(8,128)S(1)}, f32[512,128]{1,0:T(8,128)S(1)}, f32...) custom-call(s32[1]{0:T(128)} %bitcast.base_ref, s32[4,2]{1,0:T(4,128)S(1)} %copy.14.picks_ref, ...), custom_call_target="tpu_custom_call" | custom-call | flops 838860800 | bytes 1966080 | tf_op jit(solution)/shard_map/blocks_from_1/pallas_call | solution.py:271
  43.7 5.7 %blocks_from_0.1 = (bf16[128,1024]{1,0:T(8,128)(2,1)S(1)}, f32[1,1,128]{2,1,0:T(1,128)S(1)}, f32[512,128]{1,0:T(8,128)S(1)}, f32[512,128]{1,0:T(8,128)S(1)}, f32...) custom-call(s32[1]{0:T(128)} %bitcast.base_ref, s32[4,2]{1,0:T(4,128)S(1)} %copy.14.picks_ref, ...), custom_call_target="tpu_custom_call" | custom-call | flops 838860800 | bytes 1966080 | tf_op jit(solution)/shard_map/blocks_from_0/pallas_call | solution.py:271
  49.5 1.3 %collective-permute-start.8 = (bf16[512,128]{1,0:T(8,128)(2,1)S(1)}, bf16[512,128]{1,0:T(8,128)(2,1)S(1)}, u32[]{:S(2)}, u32[]{:S(2)}) collective-permute-start(bf16[512,128]{1,0:T(8,128)(2,1)S(1)} %convert_element_type.43), channel_id=1, source_target_pairs={{4,0},{12,8},{5,1},{13,9},{6,2},{14,10},{7,3},{15,11},{20,16},{28,... | collective-permute-start | bytes 393224 | tf_op jit(solution)/shard_map/ppermute | solution.py:360
  50.8 1.3 %collective-permute-start.6 = (bf16[512,128]{1,0:T(8,128)(2,1)S(1)}, bf16[512,128]{1,0:T(8,128)(2,1)S(1)}, u32[]{:S(2)}, u32[]{:S(2)}) collective-permute-start(bf16[512,128]{1,0:T(8,128)(2,1)S(1)} %convert_element_type.38), channel_id=1, source_target_pairs={{4,0},{12,8},{5,1},{13,9},{6,2},{14,10},{7,3},{15,11},{20,16},{28,... | collective-permute-start | bytes 393224 | tf_op jit(solution)/shard_map/ppermute | solution.py:360
  52.1 1.3 %collective-permute-start.5 = (bf16[2,2,128,128]{3,2,1,0:T(8,128)(2,1)S(1)}, bf16[2,2,128,128]{3,2,1,0:T(8,128)(2,1)S(1)}, u32[]{:S(2)}, u32[]{:S(2)}) collective-permute-start(bf16[2,2,128,128]{3,2,1,0:T(8,128)(2,1)S(1)} %add_convert_fusion.2), channel_id=1, source_target_pairs={{4,0},{8,4},{12,8},{5,1},{9,5},{13,9},{6,2},{10,6},{14,10},{7,3},{... | collective-permute-start | bytes 393224 | tf_op jit(solution)/shard_map/ppermute | solution.py:28
  53.4 1.0 %pad_maximum_fusion = bf16[512,1024]{1,0:T(8,128)(2,1)} fusion(bf16[256,1024]{1,0:T(8,128)(2,1)S(1)} %get-tuple-element.106, bf16[128,1024]{1,0:T(8,128)(2,1)S(1)} %get-tuple-element.105, bf16[128,1024]{1,0:T(8,128)(2,1)S(1)} %get-tuple-element.104), kind=kLoop, calls=%fused_computation | loop fusion | flops 3145728 | bytes 2097152 | tf_op jit(solution)/shard_map/concatenate | solution.py:345
  54.5 3.3 %collective-permute-done.8 = bf16[512,128]{1,0:T(8,128)(2,1)S(1)} collective-permute-done((bf16[512,128]{1,0:T(8,128)(2,1)S(1)}, bf16[512,128]{1,0:T(8,128)(2,1)S(1)}, u32[]{:S(2)}, u32[]{:S(2)}) %collective-permute-start.8) | collective-permute-done | bytes 131104 | tf_op jit(solution)/shard_map/ppermute | solution.py:360
  57.8 0.1 collective-permute-start.10
  57.9 1.3 %collective-permute-start.9 = (bf16[512,128]{1,0:T(8,128)(2,1)S(1)}, bf16[512,128]{1,0:T(8,128)(2,1)S(1)}, u32[]{:S(2)}, u32[]{:S(2)}) collective-permute-start(bf16[512,128]{1,0:T(8,128)(2,1)S(1)} %fusion.1), channel_id=1, source_target_pairs={{8,0},{9,1},{10,2},{11,3},{24,16},{25,17},{26,18},{27,19}} | collective-permute-start | bytes 393224 | tf_op jit(solution)/shard_map/ppermute | solution.py:360
  59.2 0.6 collective-permute-done.6
  59.8 1.3 %collective-permute-start.7 = (bf16[512,128]{1,0:T(8,128)(2,1)S(1)}, bf16[512,128]{1,0:T(8,128)(2,1)S(1)}, u32[]{:S(2)}, u32[]{:S(2)}) collective-permute-start(bf16[512,128]{1,0:T(8,128)(2,1)S(1)} %fusion), channel_id=1, source_target_pairs={{8,0},{9,1},{10,2},{11,3},{24,16},{25,17},{26,18},{27,19}} | collective-permute-start | bytes 393224 | tf_op jit(solution)/shard_map/ppermute | solution.py:360
  61.2 1.6 %collective-permute-start.11 = (f32[512]{0:T(512)S(1)}, f32[512]{0:T(512)S(1)}, u32[]{:S(2)}, u32[]{:S(2)}) collective-permute-start(f32[512]{0:T(512)S(1)} %add.65), channel_id=1, source_target_pairs={{0,1},{1,0},{2,3},{3,2},{4,5},{5,4},{6,7},{7,6},{8,9},{9,8},{10,11... | collective-permute-start | bytes 6152 | tf_op jit(solution)/shard_map/ppermute | solution.py:37
  62.7 2.1 %collective-permute-done.11 = f32[512]{0:T(512)S(1)} collective-permute-done((f32[512]{0:T(512)S(1)}, f32[512]{0:T(512)S(1)}, u32[]{:S(2)}, u32[]{:S(2)}) %collective-permute-start.11) | collective-permute-done | bytes 2080 | tf_op jit(solution)/shard_map/ppermute | solution.py:37
  64.8 1.5 %collective-permute-start.12 = (f32[512]{0:T(512)S(1)}, f32[512]{0:T(512)S(1)}, u32[]{:S(2)}, u32[]{:S(2)}) collective-permute-start(f32[512]{0:T(512)S(1)} %add.66), channel_id=1, source_target_pairs={{0,2},{1,3},{2,0},{3,1},{4,6},{5,7},{6,4},{7,5},{8,10},{9,11},{10,... | collective-permute-start | bytes 6152 | tf_op jit(solution)/shard_map/ppermute | solution.py:37
  66.4 2.0 %collective-permute-done.12 = f32[512]{0:T(512)S(1)} collective-permute-done((f32[512]{0:T(512)S(1)}, f32[512]{0:T(512)S(1)}, u32[]{:S(2)}, u32[]{:S(2)}) %collective-permute-start.12) | collective-permute-done | bytes 2080 | tf_op jit(solution)/shard_map/ppermute | solution.py:37
  68.4 0.6 add.67
  69.0 0.4 collective-permute-done.7
  69.4 0.7 %add_convert_fusion.1 = bf16[512,128]{1,0:T(8,128)(2,1)} fusion(f32[512,128]{1,0:T(8,128)S(1)} %get-tuple-element.126, bf16[512,128]{1,0:T(8,128)(2,1)S(1)} %collective-permute-done.7, f32[512,128]{1,0:T(8,128)S(1)} %get-tuple-element.110, bf16[512,128]{1,0:T(8,128)(2,1)S(1)} %collective-permute-done.6, pred[]{:T(512)S(6)} %eq.13), kind=kLoop, calls=%fused_computation.5 | loop fusion | flops 458752 | bytes 917505 | tf_op jit(solution)/shard_map/convert_element_type | solution.py:369
  70.1 0.7 %add_convert_fusion = bf16[512,128]{1,0:T(8,128)(2,1)} fusion(f32[512,128]{1,0:T(8,128)S(1)} %get-tuple-element.125, bf16[512,128]{1,0:T(8,128)(2,1)S(1)} %collective-permute-done.9, f32[512,128]{1,0:T(8,128)S(1)} %get-tuple-element.112, bf16[512,128]{1,0:T(8,128)(2,1)S(1)} %collective-permute-done.8, pred[]{:T(512)S(6)} %eq.13), kind=kLoop, calls=%fused_computation.3 | loop fusion | flops 458752 | bytes 917505 | tf_op jit(solution)/shard_map/convert_element_type | solution.py:369
  (30 shorter events, 0.3 us)
Async XLA Ops:
  0.6 27.2 %copy-start.2 = (bf16[512,128]{1,0:T(8,128)(2,1)S(1)}, bf16[512,128]{1,0:T(8,128)(2,1)}, u32[]{:S(2)}) copy-start(bf16[512,128]{1,0:T(8,128)(2,1)} %rest_5_.5) | copy-start | bytes 393220
  0.6 27.2 %copy-start.3 = (bf16[512,128]{1,0:T(8,128)(2,1)S(1)}, bf16[512,128]{1,0:T(8,128)(2,1)}, u32[]{:S(2)}) copy-start(bf16[512,128]{1,0:T(8,128)(2,1)} %rest_6_.5) | copy-start | bytes 393220
  0.7 19.2 %copy-start.5 = (s32[4,2]{0,1:T(2,128)S(1)}, s32[4,2]{0,1:T(2,128)}, u32[]{:S(2)}) copy-start(s32[4,2]{0,1:T(2,128)} %param.26) | copy-start | bytes 100
  2.4 25.5 %copy-start = (bf16[512,1024]{1,0:T(8,128)(2,1)S(1)}, bf16[512,1024]{1,0:T(8,128)(2,1)}, u32[]{:S(2)}) copy-start(bf16[512,1024]{1,0:T(8,128)(2,1)} %q_ref.5) | copy-start | bytes 3145732
  2.4 25.5 %copy-start.1 = (bf16[512,1024]{1,0:T(8,128)(2,1)S(1)}, bf16[512,1024]{1,0:T(8,128)(2,1)}, u32[]{:S(2)}) copy-start(bf16[512,1024]{1,0:T(8,128)(2,1)} %g_ref.5) | copy-start | bytes 3145732
  2.4 25.5 %copy-start.4 = (f32[512]{0:T(512)S(1)}, f32[512]{0:T(512)}, u32[]{:S(2)}) copy-start(f32[512]{0:T(512)} %param.27) | copy-start | bytes 6148
  2.4 17.6 %collective-permute-start.2 = (bf16[2,512,128]{2,1,0:T(8,128)(2,1)}, bf16[2,512,128]{2,1,0:T(8,128)(2,1)}, u32[]{:S(2)}, u32[]{:S(2)}) collective-permute-start(bf16[2,512,128]{2,1,0:T(8,128)(2,1)} %pad_maximum_fusion.2), channel_id=1, source_target_pairs={{0,12},{1,13},{2,14},{3,15},{16,28},{17,29},{18,30},{19,31}} | collective-permute-start | bytes 786440 | tf_op jit(solution)/shard_map/ppermute | solution.py:305
  10.2 12.0 %collective-permute-start.1 = (bf16[2,512,128]{2,1,0:T(8,128)(2,1)}, bf16[2,512,128]{2,1,0:T(8,128)(2,1)}, u32[]{:S(2)}, u32[]{:S(2)}) collective-permute-start(bf16[2,512,128]{2,1,0:T(8,128)(2,1)} %pad_maximum_fusion.2), channel_id=1, source_target_pairs={{0,8},{1,9},{2,10},{3,11},{16,24},{17,25},{18,26},{19,27}} | collective-permute-start | bytes 786440 | tf_op jit(solution)/shard_map/ppermute | solution.py:305
  14.9 12.9 %collective-permute-start.3 = (bf16[2,512,128]{2,1,0:T(8,128)(2,1)}, bf16[2,512,128]{2,1,0:T(8,128)(2,1)S(1)}, u32[]{:S(2)}, u32[]{:S(2)}) collective-permute-start(bf16[2,512,128]{2,1,0:T(8,128)(2,1)} %pad_maximum_fusion.2), channel_id=1, source_target_pairs={{0,4},{4,8},{8,12},{1,5},{5,9},{9,13},{2,6},{6,10},{10,14},{3,7},{... | collective-permute-start | bytes 786440 | tf_op jit(solution)/shard_map/ppermute | solution.py:28
  16.2 21.8 %collective-permute-start.4 = (bf16[1,1,8,128,128]{4,3,2,1,0:T(8,128)(2,1)}, bf16[1,1,8,128,128]{4,3,2,1,0:T(8,128)(2,1)S(1)}, u32[]{:S(2)}, u32[]{:S(2)}) collective-permute-start(bf16[1,1,8,128,128]{4,3,2,1,0:T(8,128)(2,1)} %get-tuple-element.95), channel_id=1, source_target_pairs={{0,4},{4,8},{8,12},{1,5},{5,9},{9,13},{2,6},{6,10},{10,14},{3,7},{... | collective-permute-start | bytes 786440 | tf_op jit(solution)/shard_map/ppermute | solution.py:28
  17.5 26.2 %collective-permute-start = (bf16[2,1,8,128,128]{4,3,2,1,0:T(8,128)(2,1)}, bf16[2,1,8,128,128]{4,3,2,1,0:T(8,128)(2,1)S(1)}, u32[]{:S(2)}, u32[]{:S(2)}) collective-permute-start(bf16[2,1,8,128,128]{4,3,2,1,0:T(8,128)(2,1)} %pad_maximum_fusion.1), channel_id=1, source_target_pairs={{0,4},{4,8},{8,12},{1,5},{5,9},{9,13},{2,6},{6,10},{10,14},{3,7},{... | collective-permute-start | bytes 1572872 | tf_op jit(solution)/shard_map/ppermute | solution.py:28
  49.5 8.3 %collective-permute-start.8 = (bf16[512,128]{1,0:T(8,128)(2,1)S(1)}, bf16[512,128]{1,0:T(8,128)(2,1)S(1)}, u32[]{:S(2)}, u32[]{:S(2)}) collective-permute-start(bf16[512,128]{1,0:T(8,128)(2,1)S(1)} %convert_element_type.43), channel_id=1, source_target_pairs={{4,0},{12,8},{5,1},{13,9},{6,2},{14,10},{7,3},{15,11},{20,16},{28,... | collective-permute-start | bytes 393224 | tf_op jit(solution)/shard_map/ppermute | solution.py:360
  50.8 9.0 %collective-permute-start.6 = (bf16[512,128]{1,0:T(8,128)(2,1)S(1)}, bf16[512,128]{1,0:T(8,128)(2,1)S(1)}, u32[]{:S(2)}, u32[]{:S(2)}) collective-permute-start(bf16[512,128]{1,0:T(8,128)(2,1)S(1)} %convert_element_type.38), channel_id=1, source_target_pairs={{4,0},{12,8},{5,1},{13,9},{6,2},{14,10},{7,3},{15,11},{20,16},{28,... | collective-permute-start | bytes 393224 | tf_op jit(solution)/shard_map/ppermute | solution.py:360
  52.1 10.6 %collective-permute-start.5 = (bf16[2,2,128,128]{3,2,1,0:T(8,128)(2,1)S(1)}, bf16[2,2,128,128]{3,2,1,0:T(8,128)(2,1)S(1)}, u32[]{:S(2)}, u32[]{:S(2)}) collective-permute-start(bf16[2,2,128,128]{3,2,1,0:T(8,128)(2,1)S(1)} %add_convert_fusion.2), channel_id=1, source_target_pairs={{4,0},{8,4},{12,8},{5,1},{9,5},{13,9},{6,2},{10,6},{14,10},{7,3},{... | collective-permute-start | bytes 393224 | tf_op jit(solution)/shard_map/ppermute | solution.py:28
  57.8 3.3 %collective-permute-start.10 = (f32[512]{0:T(512)S(1)}, f32[512]{0:T(512)S(1)}, u32[]{:S(2)}, u32[]{:S(2)}) collective-permute-start(f32[512]{0:T(512)S(1)} %bitcast.23), channel_id=1, source_target_pairs={{0,16},{16,0},{1,17},{17,1},{2,18},{18,2},{3,19},{19,3},{4,20},{20... | collective-permute-start | bytes 6152 | tf_op jit(solution)/shard_map/ppermute | solution.py:37
  57.9 12.2 %collective-permute-start.9 = (bf16[512,128]{1,0:T(8,128)(2,1)S(1)}, bf16[512,128]{1,0:T(8,128)(2,1)S(1)}, u32[]{:S(2)}, u32[]{:S(2)}) collective-permute-start(bf16[512,128]{1,0:T(8,128)(2,1)S(1)} %fusion.1), channel_id=1, source_target_pairs={{8,0},{9,1},{10,2},{11,3},{24,16},{25,17},{26,18},{27,19}} | collective-permute-start | bytes 393224 | tf_op jit(solution)/shard_map/ppermute | solution.py:360
  59.8 9.6 %collective-permute-start.7 = (bf16[512,128]{1,0:T(8,128)(2,1)S(1)}, bf16[512,128]{1,0:T(8,128)(2,1)S(1)}, u32[]{:S(2)}, u32[]{:S(2)}) collective-permute-start(bf16[512,128]{1,0:T(8,128)(2,1)S(1)} %fusion), channel_id=1, source_target_pairs={{8,0},{9,1},{10,2},{11,3},{24,16},{25,17},{26,18},{27,19}} | collective-permute-start | bytes 393224 | tf_op jit(solution)/shard_map/ppermute | solution.py:360
  61.2 3.7 %collective-permute-start.11 = (f32[512]{0:T(512)S(1)}, f32[512]{0:T(512)S(1)}, u32[]{:S(2)}, u32[]{:S(2)}) collective-permute-start(f32[512]{0:T(512)S(1)} %add.65), channel_id=1, source_target_pairs={{0,1},{1,0},{2,3},{3,2},{4,5},{5,4},{6,7},{7,6},{8,9},{9,8},{10,11... | collective-permute-start | bytes 6152 | tf_op jit(solution)/shard_map/ppermute | solution.py:37
  64.8 3.6 %collective-permute-start.12 = (f32[512]{0:T(512)S(1)}, f32[512]{0:T(512)S(1)}, u32[]{:S(2)}, u32[]{:S(2)}) collective-permute-start(f32[512]{0:T(512)S(1)} %add.66), channel_id=1, source_target_pairs={{0,2},{1,3},{2,0},{3,1},{4,6},{5,7},{6,4},{7,5},{8,10},{9,11},{10,... | collective-permute-start | bytes 6152 | tf_op jit(solution)/shard_map/ppermute | solution.py:37

commit v7 on v2

--- a/solution.py
+++ b/solution.py
@@ -130,16 +130,19 @@
         for j in range(slots):
             tile = slice(j * BLK, (j + 1) * BLK)
             t = jnp.concatenate([teacher_refs[j][0, 0, ha], teacher_refs[j][0, 0, hb]], axis=0)
-            t = t.T.astype(F32)
+            t = t.T
+            mt = jnp.max(t, axis=0, keepdims=True).astype(F32)
+            t = t.astype(F32)
             if j == 0:
                 t = jnp.where(causal, t, low)
                 s_scr[at, tile] = jnp.where(causal, s_scr[at, tile], low)
             t_scr[at, tile] = t
             chunks = [slice(k, k + CHUNK) for k in range(j * BLK, (j + 1) * BLK, CHUNK)]
             m = functools.reduce(jnp.maximum, [fold(s_scr[at, c], jnp.maximum) for c in chunks])
-            mt = functools.reduce(jnp.maximum, [fold(t_scr[at, c], jnp.maximum) for c in chunks])
             m = jnp.max(m, axis=0, keepdims=True)
-            mt = jnp.max(mt, axis=0, keepdims=True)
+            if j == 0:
+                mt = functools.reduce(jnp.maximum, [fold(t_scr[at, c], jnp.maximum) for c in chunks])
+                mt = jnp.max(mt, axis=0, keepdims=True)
             sums = None
             for c in chunks:
                 x = (s_scr[at, c] - m) * factor
@@ -279,7 +282,7 @@
             scratch_shapes=[pltpu.VMEM((slots * BLK, heads * BLK), BF)] * 2
             + [pltpu.VMEM((2, slots * BLK, 2 * BLK), F32)] * 3,
         ),
-        compiler_params=pltpu.CompilerParams(vmem_limit_bytes=48 * 1024 * 1024),
+        compiler_params=pltpu.CompilerParams(vmem_limit_bytes=(28 if crossing else 48) * 1024 * 1024),
         cost_estimate=pl.CostEstimate(
             flops=elements * E * 10, bytes_accessed=elements * 3, transcendentals=2 * elements
         ),

time: 69.4 us -> 67.9 us (0.978)
  Pallas kernels: 21.5 us -> 19 us
  waiting for transfers between devices: 14.1 us -> 15.1 us
    pallas_call x3, Pallas kernels: 21.5 us -> 19 us  [run_blocks(): pl.pallas_call(functools.partial(block_kernel, first, crossing, slots, ch...]
    ppermute x4, waiting for transfers between devices: 0.01 us -> 0.98 us  [shift(): return lax.ppermute(block, axis, route)]
  transfers between devices with their start and end apart: 13 -> 13, of which waited for: 6 -> 6; matrix products, arithmetic and copies ran while one was open for 8% -> 8% of each run, Pallas kernels for 23% -> 21%
where the time goes in v7:
time: 67.9 us; the launch traced here: 67.6 us
  starting transfers between devices  24.5 us (36%)
  Pallas kernels  19 us (28%)
  waiting for transfers between devices  15.1 us (22%)
  other arithmetic  5.94 us (9%)
  local copies, waits for them, and re-layouts  2.11 us (3%)
  between operations  0.92 us (1%)
    pallas_call x3, Pallas kernels, run_blocks(): pl.pallas_call(functools.partial(block_kernel, first, crossing, slots, ch...  19 us
    ppermute x4, starting transfers between devices, shift(): return lax.ppermute(block, axis, route)  8.96 us
    ppermute x2, starting transfers between devices, local(): more = lax.ppermute(known, 'seq', route)  7.18 us
    ppermute x2, waiting for transfers between devices, local(): more = lax.ppermute(known, 'seq', route)  5.66 us
    ppermute x4, starting transfers between devices, local(): came = [lax.ppermute(x, 'seq', route) for x in low]  5.17 us
    ppermute x4, waiting for transfers between devices, local(): came = [lax.ppermute(x, 'seq', route) for x in low]  4.39 us
    ppermute x3, waiting for transfers between devices, sum_over(): lax.ppermute(block, axis, [(i, i ^ step) for i in range(count)])  4.08 us
    ppermute x3, starting transfers between devices, sum_over(): lax.ppermute(block, axis, [(i, i ^ step) for i in range(count)])  3.15 us
  transfers between devices with their start and end apart: 13, of which 6 were waited for; matrix products, arithmetic and copies ran while one was open for 8% of the time, Pallas kernels for 21%

profile of v7, /device:TPU:0, one launch (start us, length us, event | category | flops | bytes accessed | tf_op | source)
XLA Modules:
  0.0 67.6 jit_solution(14902169629895823763)
XLA Ops:
  0.7 1.8 %pad_maximum_fusion.2 = bf16[2,512,128]{2,1,0:T(8,128)(2,1)} fusion(bf16[1,512,128]{2,1,0:T(8,128)(2,1)} %bitcast.16, bf16[1,512,128]{2,1,0:T(8,128)(2,1)} %bitcast.14), kind=kLoop, calls=%fused_computation.2 | loop fusion | flops 131072 | bytes 524288 | tf_op jit(solution)/shard_map/stack | solution.py:304
  2.4 5.1 %collective-permute-start.3 = (bf16[2,512,128]{2,1,0:T(8,128)(2,1)}, bf16[2,512,128]{2,1,0:T(8,128)(2,1)S(1)}, u32[]{:S(2)}, u32[]{:S(2)}) collective-permute-start(bf16[2,512,128]{2,1,0:T(8,128)(2,1)} %pad_maximum_fusion.2), channel_id=1, source_target_pairs={{0,4},{4,8},{8,12},{1,5},{5,9},{9,13},{2,6},{6,10},{10,14},{3,7},{... | collective-permute-start | bytes 786440 | tf_op jit(solution)/shard_map/ppermute | solution.py:28
  7.5 5.2 %collective-permute-start.2 = (bf16[2,512,128]{2,1,0:T(8,128)(2,1)}, bf16[2,512,128]{2,1,0:T(8,128)(2,1)}, u32[]{:S(2)}, u32[]{:S(2)}) collective-permute-start(bf16[2,512,128]{2,1,0:T(8,128)(2,1)} %pad_maximum_fusion.2), channel_id=1, source_target_pairs={{0,8},{1,9},{2,10},{3,11},{16,24},{17,25},{18,26},{19,27}} | collective-permute-start | bytes 786440 | tf_op jit(solution)/shard_map/ppermute | solution.py:315
  12.7 2.0 %collective-permute-start.1 = (bf16[2,512,128]{2,1,0:T(8,128)(2,1)}, bf16[2,512,128]{2,1,0:T(8,128)(2,1)}, u32[]{:S(2)}, u32[]{:S(2)}) collective-permute-start(bf16[2,512,128]{2,1,0:T(8,128)(2,1)} %pad_maximum_fusion.2), channel_id=1, source_target_pairs={{0,12},{1,13},{2,14},{3,15},{16,28},{17,29},{18,30},{19,31}} | collective-permute-start | bytes 786440 | tf_op jit(solution)/shard_map/ppermute | solution.py:315
  14.7 1.9 %fusion.2 = (bf16[1,1,8,128,128]{4,3,2,1,0:T(8,128)(2,1)S(1)}, bf16[1,1,8,128,128]{4,3,2,1,0:T(8,128)(2,1)}, bf16[1,1,8,128,128]{4,3,2,1,0:T(8,128)(2,1)S(1)}) fusion(bf16[4,3,8,128,128]{4,3,2,1,0:T(8,128)(2,1)} %rest_0_.5), kind=kLoop, calls=%fused_computation.18 | loop fusion | bytes 1572864 | tf_op jit(solution)/shard_map/slice | solution.py:324
  16.6 1.3 %collective-permute-start.4 = (bf16[1,1,8,128,128]{4,3,2,1,0:T(8,128)(2,1)}, bf16[1,1,8,128,128]{4,3,2,1,0:T(8,128)(2,1)S(1)}, u32[]{:S(2)}, u32[]{:S(2)}) collective-permute-start(bf16[1,1,8,128,128]{4,3,2,1,0:T(8,128)(2,1)} %get-tuple-element.113), channel_id=1, source_target_pairs={{0,4},{4,8},{8,12},{1,5},{5,9},{9,13},{2,6},{6,10},{10,14},{3,7},{... | collective-permute-start | bytes 786440 | tf_op jit(solution)/shard_map/ppermute | solution.py:28
  17.9 0.8 %pad_maximum_fusion.1 = bf16[2,1,8,128,128]{4,3,2,1,0:T(8,128)(2,1)} fusion(bf16[1,1,8,128,128]{4,3,2,1,0:T(8,128)(2,1)S(1)} %get-tuple-element.114, bf16[1,1,8,128,128]{4,3,2,1,0:T(8,128)(2,1)S(1)} %get-tuple-element.112), kind=kLoop, calls=%fused_computation.1 | loop fusion | flops 262144 | bytes 1048576 | tf_op jit(solution)/shard_map/concatenate | solution.py:323
  18.7 1.3 %collective-permute-start = (bf16[2,1,8,128,128]{4,3,2,1,0:T(8,128)(2,1)}, bf16[2,1,8,128,128]{4,3,2,1,0:T(8,128)(2,1)S(1)}, u32[]{:S(2)}, u32[]{:S(2)}) collective-permute-start(bf16[2,1,8,128,128]{4,3,2,1,0:T(8,128)(2,1)} %pad_maximum_fusion.1), channel_id=1, source_target_pairs={{0,4},{4,8},{8,12},{1,5},{5,9},{9,13},{2,6},{6,10},{10,14},{3,7},{... | collective-permute-start | bytes 1572872 | tf_op jit(solution)/shard_map/ppermute | solution.py:28
  20.1 0.1 copy.14.picks_ref
  20.2 5.7 %collective-permute-done.1 = bf16[2,512,128]{2,1,0:T(8,128)(2,1)} collective-permute-done((bf16[2,512,128]{2,1,0:T(8,128)(2,1)}, bf16[2,512,128]{2,1,0:T(8,128)(2,1)}, u32[]{:S(2)}, u32[]{:S(2)}) %collective-permute-start.1) | collective-permute-done | bytes 262176 | tf_op jit(solution)/shard_map/ppermute | solution.py:315
  25.8 0.1 select_select_fusion
  26.0 0.0 copy-start.1
  26.0 10.0 %blocks_from_2.1 = (bf16[256,1024]{1,0:T(8,128)(2,1)S(1)}, f32[2,1,128]{2,1,0:T(1,128)S(1)}, f32[512,128]{1,0:T(8,128)S(1)}, f32[512,128]{1,0:T(8,128)S(1)}, f32...) custom-call(s32[1]{0:T(128)} %bitcast.base_ref, s32[4,2]{1,0:T(4,128)S(1)} %copy.14.picks_ref, ...), custom_call_target="tpu_custom_call" | custom-call | flops 1677721600 | bytes 3932160 | tf_op jit(solution)/shard_map/blocks_from_2/pallas_call | solution.py:274
  36.1 4.5 %blocks_from_1.1 = (bf16[128,1024]{1,0:T(8,128)(2,1)S(1)}, f32[1,1,128]{2,1,0:T(1,128)S(1)}, f32[512,128]{1,0:T(8,128)S(1)}, f32[512,128]{1,0:T(8,128)S(1)}, f32...) custom-call(s32[1]{0:T(128)} %bitcast.base_ref, s32[4,2]{1,0:T(4,128)S(1)} %copy.14.picks_ref, ...), custom_call_target="tpu_custom_call" | custom-call | flops 838860800 | bytes 1966080 | tf_op jit(solution)/shard_map/blocks_from_1/pallas_call | solution.py:274
  40.6 1.0 %collective-permute-done = bf16[2,1,8,128,128]{4,3,2,1,0:T(8,128)(2,1)S(1)} collective-permute-done((bf16[2,1,8,128,128]{4,3,2,1,0:T(8,128)(2,1)}, bf16[2,1,8,128,128]{4,3,2,1,0:T(8,128)(2,1)S(1)}, u32[]{:S(2)}, u32[]{:S(2)}) %collective-permute-start) | collective-permute-done | bytes 524320 | tf_op jit(solution)/shard_map/ppermute | solution.py:28
  41.6 4.5 %blocks_from_0.1 = (bf16[128,1024]{1,0:T(8,128)(2,1)S(1)}, f32[1,1,128]{2,1,0:T(1,128)S(1)}, f32[512,128]{1,0:T(8,128)S(1)}, f32[512,128]{1,0:T(8,128)S(1)}, f32...) custom-call(s32[1]{0:T(128)} %bitcast.base_ref, s32[4,2]{1,0:T(4,128)S(1)} %copy.14.picks_ref, ...), custom_call_target="tpu_custom_call" | custom-call | flops 838860800 | bytes 1966080 | tf_op jit(solution)/shard_map/blocks_from_0/pallas_call | solution.py:274
  46.1 1.3 %collective-permute-start.8 = (bf16[512,128]{1,0:T(8,128)(2,1)S(1)}, bf16[512,128]{1,0:T(8,128)(2,1)S(1)}, u32[]{:S(2)}, u32[]{:S(2)}) collective-permute-start(bf16[512,128]{1,0:T(8,128)(2,1)S(1)} %convert_element_type.43), channel_id=1, source_target_pairs={{4,0},{12,8},{5,1},{13,9},{6,2},{14,10},{7,3},{15,11},{20,16},{28,... | collective-permute-start | bytes 393224 | tf_op jit(solution)/shard_map/ppermute | solution.py:358
  47.4 1.3 %collective-permute-start.6 = (bf16[512,128]{1,0:T(8,128)(2,1)S(1)}, bf16[512,128]{1,0:T(8,128)(2,1)S(1)}, u32[]{:S(2)}, u32[]{:S(2)}) collective-permute-start(bf16[512,128]{1,0:T(8,128)(2,1)S(1)} %convert_element_type.38), channel_id=1, source_target_pairs={{4,0},{12,8},{5,1},{13,9},{6,2},{14,10},{7,3},{15,11},{20,16},{28,... | collective-permute-start | bytes 393224 | tf_op jit(solution)/shard_map/ppermute | solution.py:358
  48.8 1.3 %collective-permute-start.5 = (bf16[2,2,128,128]{3,2,1,0:T(8,128)(2,1)S(1)}, bf16[2,2,128,128]{3,2,1,0:T(8,128)(2,1)S(1)}, u32[]{:S(2)}, u32[]{:S(2)}) collective-permute-start(bf16[2,2,128,128]{3,2,1,0:T(8,128)(2,1)S(1)} %add_convert_fusion.2), channel_id=1, source_target_pairs={{4,0},{8,4},{12,8},{5,1},{9,5},{13,9},{6,2},{10,6},{14,10},{7,3},{... | collective-permute-start | bytes 393224 | tf_op jit(solution)/shard_map/ppermute | solution.py:28
  50.1 1.0 %pad_maximum_fusion = bf16[512,1024]{1,0:T(8,128)(2,1)} fusion(bf16[256,1024]{1,0:T(8,128)(2,1)S(1)} %get-tuple-element.100, bf16[128,1024]{1,0:T(8,128)(2,1)S(1)} %get-tuple-element.99, bf16[128,1024]{1,0:T(8,128)(2,1)S(1)} %get-tuple-element.98), kind=kLoop, calls=%fused_computation | loop fusion | flops 3145728 | bytes 2097152 | tf_op jit(solution)/shard_map/concatenate | solution.py:343
  51.1 3.3 %collective-permute-done.8 = bf16[512,128]{1,0:T(8,128)(2,1)S(1)} collective-permute-done((bf16[512,128]{1,0:T(8,128)(2,1)S(1)}, bf16[512,128]{1,0:T(8,128)(2,1)S(1)}, u32[]{:S(2)}, u32[]{:S(2)}) %collective-permute-start.8) | collective-permute-done | bytes 131104 | tf_op jit(solution)/shard_map/ppermute | solution.py:358
  54.5 0.1 collective-permute-start.10
  54.6 1.3 %collective-permute-start.9 = (bf16[512,128]{1,0:T(8,128)(2,1)S(1)}, bf16[512,128]{1,0:T(8,128)(2,1)S(1)}, u32[]{:S(2)}, u32[]{:S(2)}) collective-permute-start(bf16[512,128]{1,0:T(8,128)(2,1)S(1)} %fusion.1), channel_id=1, source_target_pairs={{8,0},{9,1},{10,2},{11,3},{24,16},{25,17},{26,18},{27,19}} | collective-permute-start | bytes 393224 | tf_op jit(solution)/shard_map/ppermute | solution.py:358
  55.9 1.0 %collective-permute-done.6 = bf16[512,128]{1,0:T(8,128)(2,1)S(1)} collective-permute-done((bf16[512,128]{1,0:T(8,128)(2,1)S(1)}, bf16[512,128]{1,0:T(8,128)(2,1)S(1)}, u32[]{:S(2)}, u32[]{:S(2)}) %collective-permute-start.6) | collective-permute-done | bytes 131104 | tf_op jit(solution)/shard_map/ppermute | solution.py:358
  57.0 1.3 %collective-permute-start.7 = (bf16[512,128]{1,0:T(8,128)(2,1)S(1)}, bf16[512,128]{1,0:T(8,128)(2,1)S(1)}, u32[]{:S(2)}, u32[]{:S(2)}) collective-permute-start(bf16[512,128]{1,0:T(8,128)(2,1)S(1)} %fusion), channel_id=1, source_target_pairs={{8,0},{9,1},{10,2},{11,3},{24,16},{25,17},{26,18},{27,19}} | collective-permute-start | bytes 393224 | tf_op jit(solution)/shard_map/ppermute | solution.py:358
  58.3 1.6 %collective-permute-start.11 = (f32[512]{0:T(512)S(1)}, f32[512]{0:T(512)S(1)}, u32[]{:S(2)}, u32[]{:S(2)}) collective-permute-start(f32[512]{0:T(512)S(1)} %add.65), channel_id=1, source_target_pairs={{0,1},{1,0},{2,3},{3,2},{4,5},{5,4},{6,7},{7,6},{8,9},{9,8},{10,11... | collective-permute-start | bytes 6152 | tf_op jit(solution)/shard_map/ppermute | solution.py:37
  59.9 2.1 %collective-permute-done.11 = f32[512]{0:T(512)S(1)} collective-permute-done((f32[512]{0:T(512)S(1)}, f32[512]{0:T(512)S(1)}, u32[]{:S(2)}, u32[]{:S(2)}) %collective-permute-start.11) | collective-permute-done | bytes 2080 | tf_op jit(solution)/shard_map/ppermute | solution.py:37
  61.9 1.5 %collective-permute-start.12 = (f32[512]{0:T(512)S(1)}, f32[512]{0:T(512)S(1)}, u32[]{:S(2)}, u32[]{:S(2)}) collective-permute-start(f32[512]{0:T(512)S(1)} %add.66), channel_id=1, source_target_pairs={{0,2},{1,3},{2,0},{3,1},{4,6},{5,7},{6,4},{7,5},{8,10},{9,11},{10,... | collective-permute-start | bytes 6152 | tf_op jit(solution)/shard_map/ppermute | solution.py:37
  63.5 2.0 %collective-permute-done.12 = f32[512]{0:T(512)S(1)} collective-permute-done((f32[512]{0:T(512)S(1)}, f32[512]{0:T(512)S(1)}, u32[]{:S(2)}, u32[]{:S(2)}) %collective-permute-start.12) | collective-permute-done | bytes 2080 | tf_op jit(solution)/shard_map/ppermute | solution.py:37
  65.5 0.6 add.67
  66.1 0.7 %add_convert_fusion.1 = bf16[512,128]{1,0:T(8,128)(2,1)} fusion(f32[512,128]{1,0:T(8,128)S(1)} %get-tuple-element.122, bf16[512,128]{1,0:T(8,128)(2,1)S(1)} %collective-permute-done.7, f32[512,128]{1,0:T(8,128)S(1)} %get-tuple-element.104, bf16[512,128]{1,0:T(8,128)(2,1)S(1)} %collective-permute-done.6, pred[]{:T(512)S(6)} %eq.2), kind=kLoop, calls=%fused_computation.5 | loop fusion | flops 458752 | bytes 917505 | tf_op jit(solution)/shard_map/convert_element_type | solution.py:367
  66.9 0.7 %add_convert_fusion = bf16[512,128]{1,0:T(8,128)(2,1)} fusion(f32[512,128]{1,0:T(8,128)S(1)} %get-tuple-element.121, bf16[512,128]{1,0:T(8,128)(2,1)S(1)} %collective-permute-done.9, f32[512,128]{1,0:T(8,128)S(1)} %get-tuple-element.106, bf16[512,128]{1,0:T(8,128)(2,1)S(1)} %collective-permute-done.8, pred[]{:T(512)S(6)} %eq.2), kind=kLoop, calls=%fused_computation.3 | loop fusion | flops 458752 | bytes 917505 | tf_op jit(solution)/shard_map/convert_element_type | solution.py:367
  (35 shorter events, 0.3 us)
Async XLA Ops:
  0.6 25.2 %copy-start.4 = (bf16[512,128]{1,0:T(8,128)(2,1)S(1)}, bf16[512,128]{1,0:T(8,128)(2,1)}, u32[]{:S(2)}) copy-start(bf16[512,128]{1,0:T(8,128)(2,1)} %rest_5_.5) | copy-start | bytes 393220
  0.6 25.2 %copy-start.5 = (bf16[512,128]{1,0:T(8,128)(2,1)S(1)}, bf16[512,128]{1,0:T(8,128)(2,1)}, u32[]{:S(2)}) copy-start(bf16[512,128]{1,0:T(8,128)(2,1)} %rest_6_.5) | copy-start | bytes 393220
  0.7 19.4 %copy-start.7 = (s32[4,2]{0,1:T(2,128)S(1)}, s32[4,2]{0,1:T(2,128)}, u32[]{:S(2)}) copy-start(s32[4,2]{0,1:T(2,128)} %param.26) | copy-start | bytes 100
  2.4 23.5 %copy-start.2 = (bf16[512,1024]{1,0:T(8,128)(2,1)S(1)}, bf16[512,1024]{1,0:T(8,128)(2,1)}, u32[]{:S(2)}) copy-start(bf16[512,1024]{1,0:T(8,128)(2,1)} %q_ref.5) | copy-start | bytes 3145732
  2.4 23.5 %copy-start.3 = (bf16[512,1024]{1,0:T(8,128)(2,1)S(1)}, bf16[512,1024]{1,0:T(8,128)(2,1)}, u32[]{:S(2)}) copy-start(bf16[512,1024]{1,0:T(8,128)(2,1)} %g_ref.5) | copy-start | bytes 3145732
  2.4 23.5 %copy-start.6 = (f32[512]{0:T(512)S(1)}, f32[512]{0:T(512)}, u32[]{:S(2)}) copy-start(f32[512]{0:T(512)} %param.27) | copy-start | bytes 6148
  2.4 17.7 %collective-permute-start.3 = (bf16[2,512,128]{2,1,0:T(8,128)(2,1)}, bf16[2,512,128]{2,1,0:T(8,128)(2,1)S(1)}, u32[]{:S(2)}, u32[]{:S(2)}) collective-permute-start(bf16[2,512,128]{2,1,0:T(8,128)(2,1)} %pad_maximum_fusion.2), channel_id=1, source_target_pairs={{0,4},{4,8},{8,12},{1,5},{5,9},{9,13},{2,6},{6,10},{10,14},{3,7},{... | collective-permute-start | bytes 786440 | tf_op jit(solution)/shard_map/ppermute | solution.py:28
  7.5 12.7 %collective-permute-start.2 = (bf16[2,512,128]{2,1,0:T(8,128)(2,1)}, bf16[2,512,128]{2,1,0:T(8,128)(2,1)}, u32[]{:S(2)}, u32[]{:S(2)}) collective-permute-start(bf16[2,512,128]{2,1,0:T(8,128)(2,1)} %pad_maximum_fusion.2), channel_id=1, source_target_pairs={{0,8},{1,9},{2,10},{3,11},{16,24},{17,25},{18,26},{19,27}} | collective-permute-start | bytes 786440 | tf_op jit(solution)/shard_map/ppermute | solution.py:315
  12.7 13.1 %collective-permute-start.1 = (bf16[2,512,128]{2,1,0:T(8,128)(2,1)}, bf16[2,512,128]{2,1,0:T(8,128)(2,1)}, u32[]{:S(2)}, u32[]{:S(2)}) collective-permute-start(bf16[2,512,128]{2,1,0:T(8,128)(2,1)} %pad_maximum_fusion.2), channel_id=1, source_target_pairs={{0,12},{1,13},{2,14},{3,15},{16,28},{17,29},{18,30},{19,31}} | collective-permute-start | bytes 786440 | tf_op jit(solution)/shard_map/ppermute | solution.py:315
  16.6 19.5 %collective-permute-start.4 = (bf16[1,1,8,128,128]{4,3,2,1,0:T(8,128)(2,1)}, bf16[1,1,8,128,128]{4,3,2,1,0:T(8,128)(2,1)S(1)}, u32[]{:S(2)}, u32[]{:S(2)}) collective-permute-start(bf16[1,1,8,128,128]{4,3,2,1,0:T(8,128)(2,1)} %get-tuple-element.113), channel_id=1, source_target_pairs={{0,4},{4,8},{8,12},{1,5},{5,9},{9,13},{2,6},{6,10},{10,14},{3,7},{... | collective-permute-start | bytes 786440 | tf_op jit(solution)/shard_map/ppermute | solution.py:28
  18.7 22.8 %collective-permute-start = (bf16[2,1,8,128,128]{4,3,2,1,0:T(8,128)(2,1)}, bf16[2,1,8,128,128]{4,3,2,1,0:T(8,128)(2,1)S(1)}, u32[]{:S(2)}, u32[]{:S(2)}) collective-permute-start(bf16[2,1,8,128,128]{4,3,2,1,0:T(8,128)(2,1)} %pad_maximum_fusion.1), channel_id=1, source_target_pairs={{0,4},{4,8},{8,12},{1,5},{5,9},{9,13},{2,6},{6,10},{10,14},{3,7},{... | collective-permute-start | bytes 1572872 | tf_op jit(solution)/shard_map/ppermute | solution.py:28
  26.0 10.1 %copy-start = (bf16[4,3,8,128,128]{4,3,2,1,0:T(8,128)(2,1)S(1)}, bf16[4,3,8,128,128]{4,3,2,1,0:T(8,128)(2,1)}, u32[]{:S(2)}) copy-start(bf16[4,3,8,128,128]{4,3,2,1,0:T(8,128)(2,1)} %rest_0_.5) | copy-start | bytes 9437188
  26.0 10.1 %copy-start.1 = (bf16[4,2,8,128,128]{4,3,2,1,0:T(8,128)(2,1)S(1)}, bf16[4,2,8,128,128]{4,3,2,1,0:T(8,128)(2,1)}, u32[]{:S(2)}) copy-start(bf16[4,2,8,128,128]{4,3,2,1,0:T(8,128)(2,1)} %rest_4_.5) | copy-start | bytes 6291460
  46.1 8.3 %collective-permute-start.8 = (bf16[512,128]{1,0:T(8,128)(2,1)S(1)}, bf16[512,128]{1,0:T(8,128)(2,1)S(1)}, u32[]{:S(2)}, u32[]{:S(2)}) collective-permute-start(bf16[512,128]{1,0:T(8,128)(2,1)S(1)} %convert_element_type.43), channel_id=1, source_target_pairs={{4,0},{12,8},{5,1},{13,9},{6,2},{14,10},{7,3},{15,11},{20,16},{28,... | collective-permute-start | bytes 393224 | tf_op jit(solution)/shard_map/ppermute | solution.py:358
  47.4 9.5 %collective-permute-start.6 = (bf16[512,128]{1,0:T(8,128)(2,1)S(1)}, bf16[512,128]{1,0:T(8,128)(2,1)S(1)}, u32[]{:S(2)}, u32[]{:S(2)}) collective-permute-start(bf16[512,128]{1,0:T(8,128)(2,1)S(1)} %convert_element_type.38), channel_id=1, source_target_pairs={{4,0},{12,8},{5,1},{13,9},{6,2},{14,10},{7,3},{15,11},{20,16},{28,... | collective-permute-start | bytes 393224 | tf_op jit(solution)/shard_map/ppermute | solution.py:358
  48.8 11.1 %collective-permute-start.5 = (bf16[2,2,128,128]{3,2,1,0:T(8,128)(2,1)S(1)}, bf16[2,2,128,128]{3,2,1,0:T(8,128)(2,1)S(1)}, u32[]{:S(2)}, u32[]{:S(2)}) collective-permute-start(bf16[2,2,128,128]{3,2,1,0:T(8,128)(2,1)S(1)} %add_convert_fusion.2), channel_id=1, source_target_pairs={{4,0},{8,4},{12,8},{5,1},{9,5},{13,9},{6,2},{10,6},{14,10},{7,3},{... | collective-permute-start | bytes 393224 | tf_op jit(solution)/shard_map/ppermute | solution.py:28
  54.5 3.8 %collective-permute-start.10 = (f32[512]{0:T(512)S(1)}, f32[512]{0:T(512)S(1)}, u32[]{:S(2)}, u32[]{:S(2)}) collective-permute-start(f32[512]{0:T(512)S(1)} %bitcast.23), channel_id=1, source_target_pairs={{0,16},{16,0},{1,17},{17,1},{2,18},{18,2},{3,19},{19,3},{4,20},{20... | collective-permute-start | bytes 6152 | tf_op jit(solution)/shard_map/ppermute | solution.py:37
  54.6 12.3 %collective-permute-start.9 = (bf16[512,128]{1,0:T(8,128)(2,1)S(1)}, bf16[512,128]{1,0:T(8,128)(2,1)S(1)}, u32[]{:S(2)}, u32[]{:S(2)}) collective-permute-start(bf16[512,128]{1,0:T(8,128)(2,1)S(1)} %fusion.1), channel_id=1, source_target_pairs={{8,0},{9,1},{10,2},{11,3},{24,16},{25,17},{26,18},{27,19}} | collective-permute-start | bytes 393224 | tf_op jit(solution)/shard_map/ppermute | solution.py:358
  57.0 9.1 %collective-permute-start.7 = (bf16[512,128]{1,0:T(8,128)(2,1)S(1)}, bf16[512,128]{1,0:T(8,128)(2,1)S(1)}, u32[]{:S(2)}, u32[]{:S(2)}) collective-permute-start(bf16[512,128]{1,0:T(8,128)(2,1)S(1)} %fusion), channel_id=1, source_target_pairs={{8,0},{9,1},{10,2},{11,3},{24,16},{25,17},{26,18},{27,19}} | collective-permute-start | bytes 393224 | tf_op jit(solution)/shard_map/ppermute | solution.py:358
  58.3 3.7 %collective-permute-start.11 = (f32[512]{0:T(512)S(1)}, f32[512]{0:T(512)S(1)}, u32[]{:S(2)}, u32[]{:S(2)}) collective-permute-start(f32[512]{0:T(512)S(1)} %add.65), channel_id=1, source_target_pairs={{0,1},{1,0},{2,3},{3,2},{4,5},{5,4},{6,7},{7,6},{8,9},{9,8},{10,11... | collective-permute-start | bytes 6152 | tf_op jit(solution)/shard_map/ppermute | solution.py:37
  61.9 3.6 %collective-permute-start.12 = (f32[512]{0:T(512)S(1)}, f32[512]{0:T(512)S(1)}, u32[]{:S(2)}, u32[]{:S(2)}) collective-permute-start(f32[512]{0:T(512)S(1)} %add.66), channel_id=1, source_target_pairs={{0,2},{1,3},{2,0},{3,1},{4,6},{5,7},{6,4},{7,5},{8,10},{9,11},{10,... | collective-permute-start | bytes 6152 | tf_op jit(solution)/shard_map/ppermute | solution.py:37

commit v8 on v3

--- a/solution.py
+++ b/solution.py
@@ -28,15 +28,16 @@
     return lax.ppermute(block, axis, route)
 
 
-def sum_over(block, axis):
+def exchange_sum(block, axis, steps):
+    for step in steps:
+        block = block + lax.ppermute(block, axis, [(i, i ^ step) for i in range(lax.axis_size(axis))])
+    return block
+
+
+def distances(axis):
     count = lax.axis_size(axis)
-    if count & (count - 1):
-        return lax.psum(block, axis)
-    step = 1
-    while step < count:
-        block = block + lax.ppermute(block, axis, [(i, i ^ step) for i in range(count)])
-        step *= 2
-    return block
+    assert count & (count - 1) == 0
+    return [1 << n for n in range(count.bit_length() - 1)]
 
 
 def block_kernel(
@@ -101,8 +102,6 @@
     key_id = lax.broadcasted_iota(jnp.int32, (BLK, wide), 0)
     row_id = lax.broadcasted_iota(jnp.int32, (BLK, wide), 1) & (BLK - 1)
     causal = key_id <= row_id
-    square = (BLK, BLK)
-    unit = (lax.broadcasted_iota(jnp.int32, square, 0) == lax.broadcasted_iota(jnp.int32, square, 1)).astype(F32).astype(BF)
     low = jnp.float32(-1e9)
     loss = jnp.zeros((1, wide), F32)
 
@@ -132,16 +131,19 @@
         for j in range(slots):
             tile = slice(j * BLK, (j + 1) * BLK)
             t = jnp.concatenate([teacher_refs[j][0, 0, ha], teacher_refs[j][0, 0, hb]], axis=0)
-            t = lax.dot_general(unit, t, NT, preferred_element_type=F32)
+            t = t.T
+            mt = jnp.max(t, axis=0, keepdims=True).astype(F32)
+            t = t.astype(F32)
             if j == 0:
                 t = jnp.where(causal, t, low)
                 s_scr[at, tile] = jnp.where(causal, s_scr[at, tile], low)
             t_scr[at, tile] = t
             chunks = [slice(k, k + CHUNK) for k in range(j * BLK, (j + 1) * BLK, CHUNK)]
             m = functools.reduce(jnp.maximum, [fold(s_scr[at, c], jnp.maximum) for c in chunks])
-            mt = functools.reduce(jnp.maximum, [fold(t_scr[at, c], jnp.maximum) for c in chunks])
             m = jnp.max(m, axis=0, keepdims=True)
-            mt = jnp.max(mt, axis=0, keepdims=True)
+            if j == 0:
+                mt = functools.reduce(jnp.maximum, [fold(t_scr[at, c], jnp.maximum) for c in chunks])
+                mt = jnp.max(mt, axis=0, keepdims=True)
             sums = None
             for c in chunks:
                 x = (s_scr[at, c] - m) * factor
@@ -223,22 +225,6 @@
         dsv_ref[pl.ds(at, BLK), :] += dv[j * BLK:(j + 1) * BLK]
 
 
-def pack_kernel(*refs):
-    out = refs[-1]
-    for i, ref in enumerate(refs[:-1]):
-        out[i] = ref[...]
-
-
-def pack(arrays):
-    shape = arrays[0].shape
-    return pl.pallas_call(
-        pack_kernel,
-        out_shape=jax.ShapeDtypeStruct((len(arrays), *shape), arrays[0].dtype),
-        compiler_params=pltpu.CompilerParams(vmem_limit_bytes=16 * 1024 * 1024),
-        name="pack",
-    )(*arrays)
-
-
 def finish_kernel(root_ref, dk_ref, dv_ref, dsk_ref, dsv_ref, back_ref, *rest):
     came, (kg_ref, vg_ref) = rest[:-2], rest[-2:]
     root = root_ref[0] == 0
@@ -266,6 +252,7 @@
         in_specs=[pl.BlockSpec(memory_space=pltpu.SMEM)] + [vmem] * (5 + len(came)),
         out_specs=[vmem] * 2,
         compiler_params=pltpu.CompilerParams(vmem_limit_bytes=16 * 1024 * 1024),
+        cost_estimate=pl.CostEstimate(flops=4 * dk.size, bytes_accessed=14 * dk.size, transcendentals=0),
         name="finish",
     )(root, dk, dv, dsk, dsv, back, *came)
 
@@ -328,7 +315,7 @@
             scratch_shapes=[pltpu.VMEM((slots * BLK, heads * BLK), BF)] * 2
             + [pltpu.VMEM((2, slots * BLK, 2 * BLK), F32)] * 3,
         ),
-        compiler_params=pltpu.CompilerParams(vmem_limit_bytes=48 * 1024 * 1024),
+        compiler_params=pltpu.CompilerParams(vmem_limit_bytes=(28 if crossing else 48) * 1024 * 1024),
         cost_estimate=pl.CostEstimate(
             flops=elements * E * 10, bytes_accessed=elements * 3, transcendentals=2 * elements
         ),
@@ -347,7 +334,7 @@
 
     tail = slice(tokens - LEAD * BLK, tokens)
     first_rows = slice(0, NGLOB * BLK)
-    pair = pack([key_rows, values])
+    pair = jnp.stack([key_rows, values])
     got = shift(pair, "seq", 1)
     before = got[:, tail].reshape(2, LEAD, BLK, E)
     sinks = jnp.where(where == 0, pair[:, first_rows], got[:, first_rows])
@@ -397,6 +384,8 @@
         steps.append([(i, i - reach) for i in range(reach, count, 2 * reach)])
         reach *= 2
     returned = None
+    early, late = distances("head")[:-1], distances("head")[-1:]
+    row_terms = exchange_sum(exchange_sum(row_terms, "grp", distances("grp")), "head", early)
     arrived = []
     for number, route in enumerate(steps):
         low = [x.astype(BF) for x in sums]
@@ -406,7 +395,7 @@
         sums = [x + y.astype(F32) for x, y in zip(sums, came)]
         arrived += came
     row_terms, returned = lax.optimization_barrier((row_terms, returned))
-    row_loss = sum_over(sum_over(row_terms, "grp"), "head")
+    row_loss = exchange_sum(row_terms, "head", late)
     root = where.astype(jnp.int32).reshape(1)
     grads = finish(root, dk, dv, dsk, dsv, returned, arrived)
     return (query_grad, grads[0], grads[1], row_loss)

time: 72.4 us -> 69.1 us (0.954)
  the two profiles are of different devices: /device:TPU:0 before, /device:TPU:2 now
where the time goes in v8:
time: 69.1 us; the launch traced here: 68.8 us
  starting transfers between devices  22 us (32%)
  Pallas kernels  19.8 us (29%)
  waiting for transfers between devices  19.5 us (28%)
  other arithmetic  4.43 us (6%)
  local copies, waits for them, and re-layouts  2.08 us (3%)
  between operations  0.92 us (1%)
    pallas_call x3, Pallas kernels, run_blocks(): pl.pallas_call(functools.partial(block_kernel, first, crossing, slots, ch...  19 us
    ppermute x4, waiting for transfers between devices, shift(): return lax.ppermute(block, axis, route)  7.68 us
    ppermute x4, starting transfers between devices, shift(): return lax.ppermute(block, axis, route)  7.51 us
    ppermute x2, starting transfers between devices, local(): more = lax.ppermute(known, 'seq', route)  7.18 us
    ppermute x2, waiting for transfers between devices, local(): more = lax.ppermute(known, 'seq', route)  5.67 us
    ppermute x4, starting transfers between devices, local(): came = [lax.ppermute(x, 'seq', route) for x in low]  5.17 us
    ppermute x4, waiting for transfers between devices, local(): came = [lax.ppermute(x, 'seq', route) for x in low]  3.38 us
    ppermute x3, waiting for transfers between devices, exchange_sum(): lax.ppermute(block, axis, [(i, i ^ step) for i in range(lax.axis_size(axi...  2.74 us
  transfers between devices with their start and end apart: 13, of which 7 were waited for; matrix products, arithmetic and copies ran while one was open for 7% of the time, Pallas kernels for 21%

profile of v8, /device:TPU:2, one launch (start us, length us, event | category | flops | bytes accessed | tf_op | source)
XLA Modules:
  0.0 68.8 jit_solution(10890696277718055325)
XLA Ops:
  0.7 1.7 %pad_maximum_fusion.2 = bf16[2,512,128]{2,1,0:T(8,128)(2,1)} fusion(bf16[1,512,128]{2,1,0:T(8,128)(2,1)} %bitcast.13, bf16[1,512,128]{2,1,0:T(8,128)(2,1)} %bitcast.11), kind=kLoop, calls=%fused_computation.2 | loop fusion | flops 131072 | bytes 524288 | tf_op jit(solution)/shard_map/stack | solution.py:337
  2.4 3.6 %collective-permute-start.3 = (bf16[2,512,128]{2,1,0:T(8,128)(2,1)}, bf16[2,512,128]{2,1,0:T(8,128)(2,1)S(1)}, u32[]{:S(2)}, u32[]{:S(2)}) collective-permute-start(bf16[2,512,128]{2,1,0:T(8,128)(2,1)} %pad_maximum_fusion.2), channel_id=1, source_target_pairs={{0,4},{4,8},{8,12},{1,5},{5,9},{9,13},{2,6},{6,10},{10,14},{3,7},{... | collective-permute-start | bytes 786440 | tf_op jit(solution)/shard_map/ppermute | solution.py:28
  6.0 5.2 %collective-permute-start.2 = (bf16[2,512,128]{2,1,0:T(8,128)(2,1)}, bf16[2,512,128]{2,1,0:T(8,128)(2,1)}, u32[]{:S(2)}, u32[]{:S(2)}) collective-permute-start(bf16[2,512,128]{2,1,0:T(8,128)(2,1)} %pad_maximum_fusion.2), channel_id=1, source_target_pairs={{0,8},{1,9},{2,10},{3,11},{16,24},{17,25},{18,26},{19,27}} | collective-permute-start | bytes 786440 | tf_op jit(solution)/shard_map/ppermute | solution.py:348
  11.2 2.0 %collective-permute-start.1 = (bf16[2,512,128]{2,1,0:T(8,128)(2,1)}, bf16[2,512,128]{2,1,0:T(8,128)(2,1)}, u32[]{:S(2)}, u32[]{:S(2)}) collective-permute-start(bf16[2,512,128]{2,1,0:T(8,128)(2,1)} %pad_maximum_fusion.2), channel_id=1, source_target_pairs={{0,12},{1,13},{2,14},{3,15},{16,28},{17,29},{18,30},{19,31}} | collective-permute-start | bytes 786440 | tf_op jit(solution)/shard_map/ppermute | solution.py:348
  13.2 1.9 %fusion = (bf16[1,1,8,128,128]{4,3,2,1,0:T(8,128)(2,1)S(1)}, bf16[1,1,8,128,128]{4,3,2,1,0:T(8,128)(2,1)}, bf16[1,1,8,128,128]{4,3,2,1,0:T(8,128)(2,1)S(1)}) fusion(bf16[4,3,8,128,128]{4,3,2,1,0:T(8,128)(2,1)} %rest_0_.5), kind=kLoop, calls=%fused_computation.10 | loop fusion | bytes 1572864 | tf_op jit(solution)/shard_map/slice | solution.py:357
  15.1 1.3 %collective-permute-start.4 = (bf16[1,1,8,128,128]{4,3,2,1,0:T(8,128)(2,1)}, bf16[1,1,8,128,128]{4,3,2,1,0:T(8,128)(2,1)S(1)}, u32[]{:S(2)}, u32[]{:S(2)}) collective-permute-start(bf16[1,1,8,128,128]{4,3,2,1,0:T(8,128)(2,1)} %get-tuple-element.53), channel_id=1, source_target_pairs={{0,4},{4,8},{8,12},{1,5},{5,9},{9,13},{2,6},{6,10},{10,14},{3,7},{... | collective-permute-start | bytes 786440 | tf_op jit(solution)/shard_map/ppermute | solution.py:28
  16.4 0.8 %pad_maximum_fusion.1 = bf16[2,1,8,128,128]{4,3,2,1,0:T(8,128)(2,1)} fusion(bf16[1,1,8,128,128]{4,3,2,1,0:T(8,128)(2,1)S(1)} %get-tuple-element.54, bf16[1,1,8,128,128]{4,3,2,1,0:T(8,128)(2,1)S(1)} %get-tuple-element.52), kind=kLoop, calls=%fused_computation.1 | loop fusion | flops 262144 | bytes 1048576 | tf_op jit(solution)/shard_map/concatenate | solution.py:356
  17.2 1.3 %collective-permute-start = (bf16[2,1,8,128,128]{4,3,2,1,0:T(8,128)(2,1)}, bf16[2,1,8,128,128]{4,3,2,1,0:T(8,128)(2,1)S(1)}, u32[]{:S(2)}, u32[]{:S(2)}) collective-permute-start(bf16[2,1,8,128,128]{4,3,2,1,0:T(8,128)(2,1)} %pad_maximum_fusion.1), channel_id=1, source_target_pairs={{0,4},{4,8},{8,12},{1,5},{5,9},{9,13},{2,6},{6,10},{10,14},{3,7},{... | collective-permute-start | bytes 1572872 | tf_op jit(solution)/shard_map/ppermute | solution.py:28
  18.6 0.1 copy.14.picks_ref
  18.7 0.0 collective-permute-done.2
  18.7 5.7 %collective-permute-done.1 = bf16[2,512,128]{2,1,0:T(8,128)(2,1)} collective-permute-done((bf16[2,512,128]{2,1,0:T(8,128)(2,1)}, bf16[2,512,128]{2,1,0:T(8,128)(2,1)}, u32[]{:S(2)}, u32[]{:S(2)}) %collective-permute-start.1) | collective-permute-done | bytes 262176 | tf_op jit(solution)/shard_map/ppermute | solution.py:348
  24.4 0.1 select_select_fusion
  24.5 10.0 %blocks_from_2.1 = (bf16[256,1024]{1,0:T(8,128)(2,1)S(1)}, f32[2,1,128]{2,1,0:T(1,128)S(1)}, f32[512,128]{1,0:T(8,128)S(1)}, f32[512,128]{1,0:T(8,128)S(1)}, f32...) custom-call(s32[1]{0:T(128)} %bitcast.base_ref, s32[4,2]{1,0:T(4,128)S(1)} %copy.14.picks_ref, ...), custom_call_target="tpu_custom_call" | custom-call | flops 1677721600 | bytes 3932160 | tf_op jit(solution)/shard_map/blocks_from_2/pallas_call | solution.py:307
  34.6 4.5 %blocks_from_1.1 = (bf16[128,1024]{1,0:T(8,128)(2,1)S(1)}, f32[1,1,128]{2,1,0:T(1,128)S(1)}, f32[512,128]{1,0:T(8,128)S(1)}, f32[512,128]{1,0:T(8,128)S(1)}, f32...) custom-call(s32[1]{0:T(128)} %bitcast.base_ref, s32[4,2]{1,0:T(4,128)S(1)} %copy.14.picks_ref, ...), custom_call_target="tpu_custom_call" | custom-call | flops 838860800 | bytes 1966080 | tf_op jit(solution)/shard_map/blocks_from_1/pallas_call | solution.py:307
  39.1 1.0 %collective-permute-done = bf16[2,1,8,128,128]{4,3,2,1,0:T(8,128)(2,1)S(1)} collective-permute-done((bf16[2,1,8,128,128]{4,3,2,1,0:T(8,128)(2,1)}, bf16[2,1,8,128,128]{4,3,2,1,0:T(8,128)(2,1)S(1)}, u32[]{:S(2)}, u32[]{:S(2)}) %collective-permute-start) | collective-permute-done | bytes 524320 | tf_op jit(solution)/shard_map/ppermute | solution.py:28
  40.1 4.5 %blocks_from_0.1 = (bf16[128,1024]{1,0:T(8,128)(2,1)S(1)}, f32[1,1,128]{2,1,0:T(1,128)S(1)}, f32[512,128]{1,0:T(8,128)S(1)}, f32[512,128]{1,0:T(8,128)S(1)}, f32...) custom-call(s32[1]{0:T(128)} %bitcast.base_ref, s32[4,2]{1,0:T(4,128)S(1)} %copy.14.picks_ref, ...), custom_call_target="tpu_custom_call" | custom-call | flops 838860800 | bytes 1966080 | tf_op jit(solution)/shard_map/blocks_from_0/pallas_call | solution.py:307
  44.6 0.1 collective-permute-start.5
  44.8 1.3 %collective-permute-start.9 = (bf16[512,128]{1,0:T(8,128)(2,1)S(1)}, bf16[512,128]{1,0:T(8,128)(2,1)S(1)}, u32[]{:S(2)}, u32[]{:S(2)}) collective-permute-start(bf16[512,128]{1,0:T(8,128)(2,1)S(1)} %convert_element_type.23), channel_id=1, source_target_pairs={{4,0},{12,8},{5,1},{13,9},{6,2},{14,10},{7,3},{15,11},{20,16},{28,... | collective-permute-start | bytes 393224 | tf_op jit(solution)/shard_map/ppermute | solution.py:392
  46.1 1.3 %collective-permute-start.8 = (bf16[512,128]{1,0:T(8,128)(2,1)S(1)}, bf16[512,128]{1,0:T(8,128)(2,1)S(1)}, u32[]{:S(2)}, u32[]{:S(2)}) collective-permute-start(bf16[512,128]{1,0:T(8,128)(2,1)S(1)} %convert_element_type.22), channel_id=1, source_target_pairs={{4,0},{12,8},{5,1},{13,9},{6,2},{14,10},{7,3},{15,11},{20,16},{28,... | collective-permute-start | bytes 393224 | tf_op jit(solution)/shard_map/ppermute | solution.py:392
  47.4 0.6 collective-permute-start.6
  48.0 1.3 %collective-permute-start.7 = (bf16[2,2,128,128]{3,2,1,0:T(8,128)(2,1)S(1)}, bf16[2,2,128,128]{3,2,1,0:T(8,128)(2,1)S(1)}, u32[]{:S(2)}, u32[]{:S(2)}) collective-permute-start(bf16[2,2,128,128]{3,2,1,0:T(8,128)(2,1)S(1)} %add_convert_fusion.2), channel_id=1, source_target_pairs={{4,0},{8,4},{12,8},{5,1},{9,5},{13,9},{6,2},{10,6},{14,10},{7,3},{... | collective-permute-start | bytes 393224 | tf_op jit(solution)/shard_map/ppermute | solution.py:28
  49.3 1.7 %collective-permute-done.6 = f32[512]{0:T(512)S(1)} collective-permute-done((f32[512]{0:T(512)S(1)}, f32[512]{0:T(512)S(1)}, u32[]{:S(2)}, u32[]{:S(2)}) %collective-permute-start.6) | collective-permute-done | bytes 2080 | tf_op jit(solution)/shard_map/ppermute | solution.py:33
  51.0 1.9 %collective-permute-done.9.rest_1_ = bf16[512,128]{1,0:T(8,128)(2,1)S(1)} collective-permute-done((bf16[512,128]{1,0:T(8,128)(2,1)S(1)}, bf16[512,128]{1,0:T(8,128)(2,1)S(1)}, u32[]{:S(2)}, u32[]{:S(2)}) %collective-permute-start.9) | collective-permute-done | bytes 131104 | tf_op jit(solution)/shard_map/ppermute | solution.py:392
  53.0 1.3 %collective-permute-start.11 = (bf16[512,128]{1,0:T(8,128)(2,1)S(1)}, bf16[512,128]{1,0:T(8,128)(2,1)S(1)}, u32[]{:S(2)}, u32[]{:S(2)}) collective-permute-start(bf16[512,128]{1,0:T(8,128)(2,1)S(1)} %add_convert_fusion), channel_id=1, source_target_pairs={{8,0},{9,1},{10,2},{11,3},{24,16},{25,17},{26,18},{27,19}} | collective-permute-start | bytes 393224 | tf_op jit(solution)/shard_map/ppermute | solution.py:392
  54.3 1.5 %collective-permute-done.8.rest_0_ = bf16[512,128]{1,0:T(8,128)(2,1)S(1)} collective-permute-done((bf16[512,128]{1,0:T(8,128)(2,1)S(1)}, bf16[512,128]{1,0:T(8,128)(2,1)S(1)}, u32[]{:S(2)}, u32[]{:S(2)}) %collective-permute-start.8) | collective-permute-done | bytes 131104 | tf_op jit(solution)/shard_map/ppermute | solution.py:392
  55.8 1.3 %collective-permute-start.10 = (bf16[512,128]{1,0:T(8,128)(2,1)S(1)}, bf16[512,128]{1,0:T(8,128)(2,1)S(1)}, u32[]{:S(2)}, u32[]{:S(2)}) collective-permute-start(bf16[512,128]{1,0:T(8,128)(2,1)S(1)} %add_convert_fusion.1), channel_id=1, source_target_pairs={{8,0},{9,1},{10,2},{11,3},{24,16},{25,17},{26,18},{27,19}} | collective-permute-start | bytes 393224 | tf_op jit(solution)/shard_map/ppermute | solution.py:392
  57.1 6.7 %collective-permute-done.7.back_ref = bf16[2,2,128,128]{3,2,1,0:T(8,128)(2,1)S(1)} collective-permute-done((bf16[2,2,128,128]{3,2,1,0:T(8,128)(2,1)S(1)}, bf16[2,2,128,128]{3,2,1,0:T(8,128)(2,1)S(1)}, u32[]{:S(2)}, u32[]{:S(2)}) %collective-permute-start.7) | collective-permute-done | bytes 131104 | tf_op jit(solution)/shard_map/ppermute | solution.py:28
  63.8 1.5 %collective-permute-start.12 = (f32[512]{0:T(512)S(1)}, f32[512]{0:T(512)S(1)}, u32[]{:S(2)}, u32[]{:S(2)}) collective-permute-start(f32[512]{0:T(512)S(1)} %add.19), channel_id=1, source_target_pairs={{0,2},{1,3},{2,0},{3,1},{4,6},{5,7},{6,4},{7,5},{8,10},{9,11},{10,... | collective-permute-start | bytes 6152 | tf_op jit(solution)/shard_map/ppermute | solution.py:33
  65.3 1.0 %pad_maximum_fusion = bf16[512,1024]{1,0:T(8,128)(2,1)} fusion(bf16[256,1024]{1,0:T(8,128)(2,1)S(1)} %get-tuple-element.38, bf16[128,1024]{1,0:T(8,128)(2,1)S(1)} %get-tuple-element.37, bf16[128,1024]{1,0:T(8,128)(2,1)S(1)} %get-tuple-element.36), kind=kLoop, calls=%fused_computation | loop fusion | flops 3145728 | bytes 2097152 | tf_op jit(solution)/shard_map/concatenate | solution.py:376
  66.4 1.0 %collective-permute-done.12 = f32[512]{0:T(512)S(1)} collective-permute-done((f32[512]{0:T(512)S(1)}, f32[512]{0:T(512)S(1)}, u32[]{:S(2)}, u32[]{:S(2)}) %collective-permute-start.12) | collective-permute-done | bytes 2080 | tf_op jit(solution)/shard_map/ppermute | solution.py:33
  67.4 0.6 add.23
  68.0 0.8 %finish.1 = (bf16[512,128]{1,0:T(8,128)(2,1)}, bf16[512,128]{1,0:T(8,128)(2,1)}) custom-call(s32[1]{0:T(128)} %bitcast.7.root_ref, f32[512,128]{1,0:T(8,128)S(1)} %get-tuple-element.39.dk_ref, f32[512,128]{1,0:T(8,128)S(1)} %get-tuple-element.40.dv_ref, f32[512,128]{1,0:T(8,128)S(1)} %get-tuple-element.41.dsk_ref, f32[512,128]{1,0:T(8,128)S(1)} %get-tuple-element.42.dsv_ref, ...), custom_call_target="tpu_custom_call" | custom-call | flops 262144 | bytes 917504 | tf_op jit(solution)/shard_map/finish/pallas_call | solution.py:249
  (32 shorter events, 0.3 us)
Async XLA Ops:
  0.6 23.7 %copy-start.4 = (bf16[512,128]{1,0:T(8,128)(2,1)S(1)}, bf16[512,128]{1,0:T(8,128)(2,1)}, u32[]{:S(2)}) copy-start(bf16[512,128]{1,0:T(8,128)(2,1)} %rest_5_.5) | copy-start | bytes 393220
  0.6 23.7 %copy-start.5 = (bf16[512,128]{1,0:T(8,128)(2,1)S(1)}, bf16[512,128]{1,0:T(8,128)(2,1)}, u32[]{:S(2)}) copy-start(bf16[512,128]{1,0:T(8,128)(2,1)} %rest_6_.5) | copy-start | bytes 393220
  0.7 17.9 %copy-start.7 = (s32[4,2]{0,1:T(2,128)S(1)}, s32[4,2]{0,1:T(2,128)}, u32[]{:S(2)}) copy-start(s32[4,2]{0,1:T(2,128)} %param.14) | copy-start | bytes 100
  2.4 22.1 %copy-start.2 = (bf16[512,1024]{1,0:T(8,128)(2,1)S(1)}, bf16[512,1024]{1,0:T(8,128)(2,1)}, u32[]{:S(2)}) copy-start(bf16[512,1024]{1,0:T(8,128)(2,1)} %q_ref.5) | copy-start | bytes 3145732
  2.4 22.1 %copy-start.3 = (bf16[512,1024]{1,0:T(8,128)(2,1)S(1)}, bf16[512,1024]{1,0:T(8,128)(2,1)}, u32[]{:S(2)}) copy-start(bf16[512,1024]{1,0:T(8,128)(2,1)} %g_ref.5) | copy-start | bytes 3145732
  2.4 22.1 %copy-start.6 = (f32[512]{0:T(512)S(1)}, f32[512]{0:T(512)}, u32[]{:S(2)}) copy-start(f32[512]{0:T(512)} %param.15) | copy-start | bytes 6148
  2.4 16.3 %collective-permute-start.3 = (bf16[2,512,128]{2,1,0:T(8,128)(2,1)}, bf16[2,512,128]{2,1,0:T(8,128)(2,1)S(1)}, u32[]{:S(2)}, u32[]{:S(2)}) collective-permute-start(bf16[2,512,128]{2,1,0:T(8,128)(2,1)} %pad_maximum_fusion.2), channel_id=1, source_target_pairs={{0,4},{4,8},{8,12},{1,5},{5,9},{9,13},{2,6},{6,10},{10,14},{3,7},{... | collective-permute-start | bytes 786440 | tf_op jit(solution)/shard_map/ppermute | solution.py:28
  6.0 12.7 %collective-permute-start.2 = (bf16[2,512,128]{2,1,0:T(8,128)(2,1)}, bf16[2,512,128]{2,1,0:T(8,128)(2,1)}, u32[]{:S(2)}, u32[]{:S(2)}) collective-permute-start(bf16[2,512,128]{2,1,0:T(8,128)(2,1)} %pad_maximum_fusion.2), channel_id=1, source_target_pairs={{0,8},{1,9},{2,10},{3,11},{16,24},{17,25},{18,26},{19,27}} | collective-permute-start | bytes 786440 | tf_op jit(solution)/shard_map/ppermute | solution.py:348
  11.2 13.1 %collective-permute-start.1 = (bf16[2,512,128]{2,1,0:T(8,128)(2,1)}, bf16[2,512,128]{2,1,0:T(8,128)(2,1)}, u32[]{:S(2)}, u32[]{:S(2)}) collective-permute-start(bf16[2,512,128]{2,1,0:T(8,128)(2,1)} %pad_maximum_fusion.2), channel_id=1, source_target_pairs={{0,12},{1,13},{2,14},{3,15},{16,28},{17,29},{18,30},{19,31}} | collective-permute-start | bytes 786440 | tf_op jit(solution)/shard_map/ppermute | solution.py:348
  15.1 19.5 %collective-permute-start.4 = (bf16[1,1,8,128,128]{4,3,2,1,0:T(8,128)(2,1)}, bf16[1,1,8,128,128]{4,3,2,1,0:T(8,128)(2,1)S(1)}, u32[]{:S(2)}, u32[]{:S(2)}) collective-permute-start(bf16[1,1,8,128,128]{4,3,2,1,0:T(8,128)(2,1)} %get-tuple-element.53), channel_id=1, source_target_pairs={{0,4},{4,8},{8,12},{1,5},{5,9},{9,13},{2,6},{6,10},{10,14},{3,7},{... | collective-permute-start | bytes 786440 | tf_op jit(solution)/shard_map/ppermute | solution.py:28
  17.2 22.8 %collective-permute-start = (bf16[2,1,8,128,128]{4,3,2,1,0:T(8,128)(2,1)}, bf16[2,1,8,128,128]{4,3,2,1,0:T(8,128)(2,1)S(1)}, u32[]{:S(2)}, u32[]{:S(2)}) collective-permute-start(bf16[2,1,8,128,128]{4,3,2,1,0:T(8,128)(2,1)} %pad_maximum_fusion.1), channel_id=1, source_target_pairs={{0,4},{4,8},{8,12},{1,5},{5,9},{9,13},{2,6},{6,10},{10,14},{3,7},{... | collective-permute-start | bytes 1572872 | tf_op jit(solution)/shard_map/ppermute | solution.py:28
  24.5 10.1 %copy-start = (bf16[4,3,8,128,128]{4,3,2,1,0:T(8,128)(2,1)S(1)}, bf16[4,3,8,128,128]{4,3,2,1,0:T(8,128)(2,1)}, u32[]{:S(2)}) copy-start(bf16[4,3,8,128,128]{4,3,2,1,0:T(8,128)(2,1)} %rest_0_.5) | copy-start | bytes 9437188
  24.5 10.1 %copy-start.1 = (bf16[4,2,8,128,128]{4,3,2,1,0:T(8,128)(2,1)S(1)}, bf16[4,2,8,128,128]{4,3,2,1,0:T(8,128)(2,1)}, u32[]{:S(2)}) copy-start(bf16[4,2,8,128,128]{4,3,2,1,0:T(8,128)(2,1)} %rest_4_.5) | copy-start | bytes 6291460
  44.6 2.7 %collective-permute-start.5 = (f32[512]{0:T(512)S(1)}, f32[512]{0:T(512)S(1)}, u32[]{:S(2)}, u32[]{:S(2)}) collective-permute-start(f32[512]{0:T(512)S(1)} %bitcast.20), channel_id=1, source_target_pairs={{0,16},{16,0},{1,17},{17,1},{2,18},{18,2},{3,19},{19,3},{4,20},{20... | collective-permute-start | bytes 6152 | tf_op jit(solution)/shard_map/ppermute | solution.py:33
  44.8 8.2 %collective-permute-start.9 = (bf16[512,128]{1,0:T(8,128)(2,1)S(1)}, bf16[512,128]{1,0:T(8,128)(2,1)S(1)}, u32[]{:S(2)}, u32[]{:S(2)}) collective-permute-start(bf16[512,128]{1,0:T(8,128)(2,1)S(1)} %convert_element_type.23), channel_id=1, source_target_pairs={{4,0},{12,8},{5,1},{13,9},{6,2},{14,10},{7,3},{15,11},{20,16},{28,... | collective-permute-start | bytes 393224 | tf_op jit(solution)/shard_map/ppermute | solution.py:392
  46.1 9.7 %collective-permute-start.8 = (bf16[512,128]{1,0:T(8,128)(2,1)S(1)}, bf16[512,128]{1,0:T(8,128)(2,1)S(1)}, u32[]{:S(2)}, u32[]{:S(2)}) collective-permute-start(bf16[512,128]{1,0:T(8,128)(2,1)S(1)} %convert_element_type.22), channel_id=1, source_target_pairs={{4,0},{12,8},{5,1},{13,9},{6,2},{14,10},{7,3},{15,11},{20,16},{28,... | collective-permute-start | bytes 393224 | tf_op jit(solution)/shard_map/ppermute | solution.py:392
  47.4 3.7 %collective-permute-start.6 = (f32[512]{0:T(512)S(1)}, f32[512]{0:T(512)S(1)}, u32[]{:S(2)}, u32[]{:S(2)}) collective-permute-start(f32[512]{0:T(512)S(1)} %add.18), channel_id=1, source_target_pairs={{0,1},{1,0},{2,3},{3,2},{4,5},{5,4},{6,7},{7,6},{8,9},{9,8},{10,11... | collective-permute-start | bytes 6152 | tf_op jit(solution)/shard_map/ppermute | solution.py:33
  48.0 15.8 %collective-permute-start.7 = (bf16[2,2,128,128]{3,2,1,0:T(8,128)(2,1)S(1)}, bf16[2,2,128,128]{3,2,1,0:T(8,128)(2,1)S(1)}, u32[]{:S(2)}, u32[]{:S(2)}) collective-permute-start(bf16[2,2,128,128]{3,2,1,0:T(8,128)(2,1)S(1)} %add_convert_fusion.2), channel_id=1, source_target_pairs={{4,0},{8,4},{12,8},{5,1},{9,5},{13,9},{6,2},{10,6},{14,10},{7,3},{... | collective-permute-start | bytes 393224 | tf_op jit(solution)/shard_map/ppermute | solution.py:28
  53.0 15.0 %collective-permute-start.11 = (bf16[512,128]{1,0:T(8,128)(2,1)S(1)}, bf16[512,128]{1,0:T(8,128)(2,1)S(1)}, u32[]{:S(2)}, u32[]{:S(2)}) collective-permute-start(bf16[512,128]{1,0:T(8,128)(2,1)S(1)} %add_convert_fusion), channel_id=1, source_target_pairs={{8,0},{9,1},{10,2},{11,3},{24,16},{25,17},{26,18},{27,19}} | collective-permute-start | bytes 393224 | tf_op jit(solution)/shard_map/ppermute | solution.py:392
  55.8 12.2 %collective-permute-start.10 = (bf16[512,128]{1,0:T(8,128)(2,1)S(1)}, bf16[512,128]{1,0:T(8,128)(2,1)S(1)}, u32[]{:S(2)}, u32[]{:S(2)}) collective-permute-start(bf16[512,128]{1,0:T(8,128)(2,1)S(1)} %add_convert_fusion.1), channel_id=1, source_target_pairs={{8,0},{9,1},{10,2},{11,3},{24,16},{25,17},{26,18},{27,19}} | collective-permute-start | bytes 393224 | tf_op jit(solution)/shard_map/ppermute | solution.py:392
  63.8 3.6 %collective-permute-start.12 = (f32[512]{0:T(512)S(1)}, f32[512]{0:T(512)S(1)}, u32[]{:S(2)}, u32[]{:S(2)}) collective-permute-start(f32[512]{0:T(512)S(1)} %add.19), channel_id=1, source_target_pairs={{0,2},{1,3},{2,0},{3,1},{4,6},{5,7},{6,4},{7,5},{8,10},{9,11},{10,... | collective-permute-start | bytes 6152 | tf_op jit(solution)/shard_map/ppermute | solution.py:33

commit v9 on v8

--- a/solution.py
+++ b/solution.py
@@ -315,7 +315,7 @@
             scratch_shapes=[pltpu.VMEM((slots * BLK, heads * BLK), BF)] * 2
             + [pltpu.VMEM((2, slots * BLK, 2 * BLK), F32)] * 3,
         ),
-        compiler_params=pltpu.CompilerParams(vmem_limit_bytes=(28 if crossing else 48) * 1024 * 1024),
+        compiler_params=pltpu.CompilerParams(vmem_limit_bytes=(28 if crossing else 46) * 1024 * 1024),
         cost_estimate=pl.CostEstimate(
             flops=elements * E * 10, bytes_accessed=elements * 3, transcendentals=2 * elements
         ),
@@ -389,12 +389,13 @@
     arrived = []
     for number, route in enumerate(steps):
         low = [x.astype(BF) for x in sums]
+        if number == 1:
+            row_terms, low[0] = lax.optimization_barrier((row_terms, low[0]))
         came = [lax.ppermute(x, "seq", route) for x in low]
         if number == 0:
             returned = shift(back.astype(BF), "seq", -1)
         sums = [x + y.astype(F32) for x, y in zip(sums, came)]
         arrived += came
-    row_terms, returned = lax.optimization_barrier((row_terms, returned))
     row_loss = exchange_sum(row_terms, "head", late)
     root = where.astype(jnp.int32).reshape(1)
     grads = finish(root, dk, dv, dsk, dsv, returned, arrived)

time: 69.1 us -> 69.8 us (1.010)
  the two profiles are of different devices: /device:TPU:2 before, /device:TPU:0 now
where the time goes in v9:
time: 69.8 us; the launch traced here: 69.4 us
  starting transfers between devices  26.1 us (37%)
  Pallas kernels  20.7 us (30%)
  waiting for transfers between devices  13.2 us (19%)
  other arithmetic  4.43 us (6%)
  local copies, waits for them, and re-layouts  4.01 us (6%)
  between operations  0.87 us (1%)
    pallas_call x3, Pallas kernels, run_blocks(): pl.pallas_call(functools.partial(block_kernel, first, crossing, slots, ch...  19.9 us
    ppermute x4, starting transfers between devices, shift(): return lax.ppermute(block, axis, route)  11.3 us
    ppermute x4, waiting for transfers between devices, local(): came = [lax.ppermute(x, 'seq', route) for x in low]  8.21 us
    ppermute x2, starting transfers between devices, local(): more = lax.ppermute(known, 'seq', route)  6.51 us
    ppermute x4, starting transfers between devices, local(): came = [lax.ppermute(x, 'seq', route) for x in low]  5.16 us
    ppermute x2, waiting for transfers between devices, local(): more = lax.ppermute(known, 'seq', route)  4.23 us
    ppermute x3, starting transfers between devices, exchange_sum(): lax.ppermute(block, axis, [(i, i ^ step) for i in range(lax.axis_size(axi...  3.21 us
    slice x1, local copies, waits for them, and re-layouts, local(): teacher_window[blocks + block - d:blocks + block - d + 1, d:d + 1]  1.88 us
  transfers between devices with their start and end apart: 13, of which 6 were waited for; matrix products, arithmetic and copies ran while one was open for 8% of the time, Pallas kernels for 22%

profile of v9, /device:TPU:0, one launch (start us, length us, event | category | flops | bytes accessed | tf_op | source)
XLA Modules:
  0.0 69.4 jit_solution(14143932869872844779)
XLA Ops:
  0.7 1.8 %pad_maximum_fusion.2 = bf16[2,512,128]{2,1,0:T(8,128)(2,1)} fusion(bf16[1,512,128]{2,1,0:T(8,128)(2,1)} %bitcast.13, bf16[1,512,128]{2,1,0:T(8,128)(2,1)} %bitcast.11), kind=kLoop, calls=%fused_computation.2 | loop fusion | flops 131072 | bytes 524288 | tf_op jit(solution)/shard_map/stack | solution.py:337
  2.4 5.9 %collective-permute-start.3 = (bf16[2,512,128]{2,1,0:T(8,128)(2,1)}, bf16[2,512,128]{2,1,0:T(8,128)(2,1)}, u32[]{:S(2)}, u32[]{:S(2)}) collective-permute-start(bf16[2,512,128]{2,1,0:T(8,128)(2,1)} %pad_maximum_fusion.2), channel_id=1, source_target_pairs={{0,4},{4,8},{8,12},{1,5},{5,9},{9,13},{2,6},{6,10},{10,14},{3,7},{... | collective-permute-start | bytes 786440 | tf_op jit(solution)/shard_map/ppermute | solution.py:28
  8.3 4.5 %collective-permute-start.2 = (bf16[2,512,128]{2,1,0:T(8,128)(2,1)}, bf16[2,512,128]{2,1,0:T(8,128)(2,1)}, u32[]{:S(2)}, u32[]{:S(2)}) collective-permute-start(bf16[2,512,128]{2,1,0:T(8,128)(2,1)} %pad_maximum_fusion.2), channel_id=1, source_target_pairs={{0,8},{1,9},{2,10},{3,11},{16,24},{17,25},{18,26},{19,27}} | collective-permute-start | bytes 786440 | tf_op jit(solution)/shard_map/ppermute | solution.py:348
  12.8 2.0 %collective-permute-start.1 = (bf16[2,512,128]{2,1,0:T(8,128)(2,1)}, bf16[2,512,128]{2,1,0:T(8,128)(2,1)}, u32[]{:S(2)}, u32[]{:S(2)}) collective-permute-start(bf16[2,512,128]{2,1,0:T(8,128)(2,1)} %pad_maximum_fusion.2), channel_id=1, source_target_pairs={{0,12},{1,13},{2,14},{3,15},{16,28},{17,29},{18,30},{19,31}} | collective-permute-start | bytes 786440 | tf_op jit(solution)/shard_map/ppermute | solution.py:348
  14.8 1.9 %fusion = (bf16[1,1,8,128,128]{4,3,2,1,0:T(8,128)(2,1)S(1)}, bf16[1,1,8,128,128]{4,3,2,1,0:T(8,128)(2,1)}, bf16[1,1,8,128,128]{4,3,2,1,0:T(8,128)(2,1)S(1)}) fusion(bf16[4,3,8,128,128]{4,3,2,1,0:T(8,128)(2,1)} %rest_0_.5), kind=kLoop, calls=%fused_computation.10 | loop fusion | bytes 1572864 | tf_op jit(solution)/shard_map/slice | solution.py:357
  16.7 2.0 %collective-permute-start.4 = (bf16[1,1,8,128,128]{4,3,2,1,0:T(8,128)(2,1)}, bf16[1,1,8,128,128]{4,3,2,1,0:T(8,128)(2,1)}, u32[]{:S(2)}, u32[]{:S(2)}) collective-permute-start(bf16[1,1,8,128,128]{4,3,2,1,0:T(8,128)(2,1)} %get-tuple-element.53), channel_id=1, source_target_pairs={{0,4},{4,8},{8,12},{1,5},{5,9},{9,13},{2,6},{6,10},{10,14},{3,7},{... | collective-permute-start | bytes 786440 | tf_op jit(solution)/shard_map/ppermute | solution.py:28
  18.7 0.8 %pad_maximum_fusion.1 = bf16[2,1,8,128,128]{4,3,2,1,0:T(8,128)(2,1)} fusion(bf16[1,1,8,128,128]{4,3,2,1,0:T(8,128)(2,1)S(1)} %get-tuple-element.54, bf16[1,1,8,128,128]{4,3,2,1,0:T(8,128)(2,1)S(1)} %get-tuple-element.52), kind=kLoop, calls=%fused_computation.1 | loop fusion | flops 262144 | bytes 1048576 | tf_op jit(solution)/shard_map/concatenate | solution.py:356
  19.5 2.1 %collective-permute-start = (bf16[2,1,8,128,128]{4,3,2,1,0:T(8,128)(2,1)}, bf16[2,1,8,128,128]{4,3,2,1,0:T(8,128)(2,1)}, u32[]{:S(2)}, u32[]{:S(2)}) collective-permute-start(bf16[2,1,8,128,128]{4,3,2,1,0:T(8,128)(2,1)} %pad_maximum_fusion.1), channel_id=1, source_target_pairs={{0,4},{4,8},{8,12},{1,5},{5,9},{9,13},{2,6},{6,10},{10,14},{3,7},{... | collective-permute-start | bytes 1572872 | tf_op jit(solution)/shard_map/ppermute | solution.py:28
  21.6 0.1 copy.14.picks_ref
  21.7 4.2 %collective-permute-done.1 = bf16[2,512,128]{2,1,0:T(8,128)(2,1)} collective-permute-done((bf16[2,512,128]{2,1,0:T(8,128)(2,1)}, bf16[2,512,128]{2,1,0:T(8,128)(2,1)}, u32[]{:S(2)}, u32[]{:S(2)}) %collective-permute-start.1) | collective-permute-done | bytes 262176 | tf_op jit(solution)/shard_map/ppermute | solution.py:348
  26.0 0.1 select_select_fusion
  26.1 0.9 %slice.36 = bf16[2,256,128]{2,1,0:T(8,128)(2,1)S(1)} slice(bf16[2,512,128]{2,1,0:T(8,128)(2,1)} %collective-permute-done.3), slice={[0:2], [256:512], [0:128]} | slice | bytes 262144 | tf_op jit(solution)/shard_map/slice | solution.py:339
  27.0 9.9 %blocks_from_2.1 = (bf16[256,1024]{1,0:T(8,128)(2,1)S(1)}, f32[2,1,128]{2,1,0:T(1,128)S(1)}, f32[512,128]{1,0:T(8,128)S(1)}, f32[512,128]{1,0:T(8,128)S(1)}, f32...) custom-call(s32[1]{0:T(128)} %bitcast.base_ref, s32[4,2]{1,0:T(4,128)S(1)} %copy.14.picks_ref, ...), custom_call_target="tpu_custom_call" | custom-call | flops 1677721600 | bytes 3932160 | tf_op jit(solution)/shard_map/blocks_from_2/pallas_call | solution.py:307
  37.0 5.5 %blocks_from_1.1 = (bf16[128,1024]{1,0:T(8,128)(2,1)S(1)}, f32[1,1,128]{2,1,0:T(1,128)S(1)}, f32[512,128]{1,0:T(8,128)S(1)}, f32[512,128]{1,0:T(8,128)S(1)}, f32...) custom-call(s32[1]{0:T(128)} %bitcast.base_ref, s32[4,2]{1,0:T(4,128)S(1)} %copy.14.picks_ref, ...), custom_call_target="tpu_custom_call" | custom-call | flops 838860800 | bytes 1966080 | tf_op jit(solution)/shard_map/blocks_from_1/pallas_call | solution.py:307
  42.4 1.1 %fusion.1 = (bf16[1,1,8,128,128]{4,3,2,1,0:T(8,128)(2,1)S(1)}, bf16[1,1,8,128,128]{4,3,2,1,0:T(8,128)(2,1)S(1)}) fusion(bf16[2,1,8,128,128]{4,3,2,1,0:T(8,128)(2,1)} %collective-permute-done), kind=kLoop, calls=%fused_computation.11 | loop fusion | bytes 1048576 | tf_op jit(solution)/shard_map/slice | solution.py:360
  43.5 4.5 %blocks_from_0.1 = (bf16[128,1024]{1,0:T(8,128)(2,1)S(1)}, f32[1,1,128]{2,1,0:T(1,128)S(1)}, f32[512,128]{1,0:T(8,128)S(1)}, f32[512,128]{1,0:T(8,128)S(1)}, f32...) custom-call(s32[1]{0:T(128)} %bitcast.base_ref, s32[4,2]{1,0:T(4,128)S(1)} %copy.14.picks_ref, ...), custom_call_target="tpu_custom_call" | custom-call | flops 838860800 | bytes 1966080 | tf_op jit(solution)/shard_map/blocks_from_0/pallas_call | solution.py:307
  48.0 0.1 collective-permute-start.8
  48.2 1.3 %collective-permute-start.7 = (bf16[512,128]{1,0:T(8,128)(2,1)S(1)}, bf16[512,128]{1,0:T(8,128)(2,1)S(1)}, u32[]{:S(2)}, u32[]{:S(2)}) collective-permute-start(bf16[512,128]{1,0:T(8,128)(2,1)S(1)} %convert_element_type.23), channel_id=1, source_target_pairs={{4,0},{12,8},{5,1},{13,9},{6,2},{14,10},{7,3},{15,11},{20,16},{28,... | collective-permute-start | bytes 393224 | tf_op jit(solution)/shard_map/ppermute | solution.py:394
  49.5 1.3 %collective-permute-start.6 = (bf16[512,128]{1,0:T(8,128)(2,1)S(1)}, bf16[512,128]{1,0:T(8,128)(2,1)S(1)}, u32[]{:S(2)}, u32[]{:S(2)}) collective-permute-start(bf16[512,128]{1,0:T(8,128)(2,1)S(1)} %convert_element_type.22), channel_id=1, source_target_pairs={{4,0},{12,8},{5,1},{13,9},{6,2},{14,10},{7,3},{15,11},{20,16},{28,... | collective-permute-start | bytes 393224 | tf_op jit(solution)/shard_map/ppermute | solution.py:394
  50.8 1.6 %collective-permute-start.9 = (f32[512]{0:T(512)S(1)}, f32[512]{0:T(512)S(1)}, u32[]{:S(2)}, u32[]{:S(2)}) collective-permute-start(f32[512]{0:T(512)S(1)} %add.19), channel_id=1, source_target_pairs={{0,1},{1,0},{2,3},{3,2},{4,5},{5,4},{6,7},{7,6},{8,9},{9,8},{10,11... | collective-permute-start | bytes 6152 | tf_op jit(solution)/shard_map/ppermute | solution.py:33
  52.4 1.3 %collective-permute-start.5 = (bf16[2,2,128,128]{3,2,1,0:T(8,128)(2,1)S(1)}, bf16[2,2,128,128]{3,2,1,0:T(8,128)(2,1)S(1)}, u32[]{:S(2)}, u32[]{:S(2)}) collective-permute-start(bf16[2,2,128,128]{3,2,1,0:T(8,128)(2,1)S(1)} %add_convert_fusion.2), channel_id=1, source_target_pairs={{4,0},{8,4},{12,8},{5,1},{9,5},{13,9},{6,2},{10,6},{14,10},{7,3},{... | collective-permute-start | bytes 393224 | tf_op jit(solution)/shard_map/ppermute | solution.py:28
  53.7 0.8 %collective-permute-done.9 = f32[512]{0:T(512)S(1)} collective-permute-done((f32[512]{0:T(512)S(1)}, f32[512]{0:T(512)S(1)}, u32[]{:S(2)}, u32[]{:S(2)}) %collective-permute-start.9) | collective-permute-done | bytes 2080 | tf_op jit(solution)/shard_map/ppermute | solution.py:33
  54.4 1.9 %collective-permute-done.7.rest_1_ = bf16[512,128]{1,0:T(8,128)(2,1)S(1)} collective-permute-done((bf16[512,128]{1,0:T(8,128)(2,1)S(1)}, bf16[512,128]{1,0:T(8,128)(2,1)S(1)}, u32[]{:S(2)}, u32[]{:S(2)}) %collective-permute-start.7) | collective-permute-done | bytes 131104 | tf_op jit(solution)/shard_map/ppermute | solution.py:394
  56.4 1.3 %collective-permute-start.11 = (bf16[512,128]{1,0:T(8,128)(2,1)S(1)}, bf16[512,128]{1,0:T(8,128)(2,1)S(1)}, u32[]{:S(2)}, u32[]{:S(2)}) collective-permute-start(bf16[512,128]{1,0:T(8,128)(2,1)S(1)} %add_convert_fusion), channel_id=1, source_target_pairs={{8,0},{9,1},{10,2},{11,3},{24,16},{25,17},{26,18},{27,19}} | collective-permute-start | bytes 393224 | tf_op jit(solution)/shard_map/ppermute | solution.py:394
  57.7 1.5 %collective-permute-done.6.rest_0_ = bf16[512,128]{1,0:T(8,128)(2,1)S(1)} collective-permute-done((bf16[512,128]{1,0:T(8,128)(2,1)S(1)}, bf16[512,128]{1,0:T(8,128)(2,1)S(1)}, u32[]{:S(2)}, u32[]{:S(2)}) %collective-permute-start.6) | collective-permute-done | bytes 131104 | tf_op jit(solution)/shard_map/ppermute | solution.py:394
  59.2 1.6 %collective-permute-start.12 = (f32[512]{0:T(512)S(1)}, f32[512]{0:T(512)S(1)}, u32[]{:S(2)}, u32[]{:S(2)}) collective-permute-start(f32[512]{0:T(512)S(1)} %add.20), channel_id=1, source_target_pairs={{0,2},{1,3},{2,0},{3,1},{4,6},{5,7},{6,4},{7,5},{8,10},{9,11},{10,... | collective-permute-start | bytes 6152 | tf_op jit(solution)/shard_map/ppermute | solution.py:33
  60.8 1.3 %collective-permute-start.10 = (bf16[512,128]{1,0:T(8,128)(2,1)S(1)}, bf16[512,128]{1,0:T(8,128)(2,1)S(1)}, u32[]{:S(2)}, u32[]{:S(2)}) collective-permute-start(bf16[512,128]{1,0:T(8,128)(2,1)S(1)} %add_convert_fusion.1), channel_id=1, source_target_pairs={{8,0},{9,1},{10,2},{11,3},{24,16},{25,17},{26,18},{27,19}} | collective-permute-start | bytes 393224 | tf_op jit(solution)/shard_map/ppermute | solution.py:394
  62.1 1.0 %pad_maximum_fusion = bf16[512,1024]{1,0:T(8,128)(2,1)} fusion(bf16[256,1024]{1,0:T(8,128)(2,1)S(1)} %get-tuple-element.38, bf16[128,1024]{1,0:T(8,128)(2,1)S(1)} %get-tuple-element.37, bf16[128,1024]{1,0:T(8,128)(2,1)S(1)} %get-tuple-element.36), kind=kLoop, calls=%fused_computation | loop fusion | flops 3145728 | bytes 2097152 | tf_op jit(solution)/shard_map/concatenate | solution.py:376
  63.1 0.6 add.23
  63.7 0.8 %collective-permute-done.11.rest_3_ = bf16[512,128]{1,0:T(8,128)(2,1)S(1)} collective-permute-done((bf16[512,128]{1,0:T(8,128)(2,1)S(1)}, bf16[512,128]{1,0:T(8,128)(2,1)S(1)}, u32[]{:S(2)}, u32[]{:S(2)}) %collective-permute-start.11) | collective-permute-done | bytes 131104 | tf_op jit(solution)/shard_map/ppermute | solution.py:394
  64.5 4.0 %collective-permute-done.10.rest_2_ = bf16[512,128]{1,0:T(8,128)(2,1)S(1)} collective-permute-done((bf16[512,128]{1,0:T(8,128)(2,1)S(1)}, bf16[512,128]{1,0:T(8,128)(2,1)S(1)}, u32[]{:S(2)}, u32[]{:S(2)}) %collective-permute-start.10) | collective-permute-done | bytes 131104 | tf_op jit(solution)/shard_map/ppermute | solution.py:394
  68.5 0.8 %finish.1 = (bf16[512,128]{1,0:T(8,128)(2,1)}, bf16[512,128]{1,0:T(8,128)(2,1)}) custom-call(s32[1]{0:T(128)} %bitcast.7.root_ref, f32[512,128]{1,0:T(8,128)S(1)} %get-tuple-element.39.dk_ref, f32[512,128]{1,0:T(8,128)S(1)} %get-tuple-element.40.dv_ref, f32[512,128]{1,0:T(8,128)S(1)} %get-tuple-element.41.dsk_ref, f32[512,128]{1,0:T(8,128)S(1)} %get-tuple-element.42.dsv_ref, ...), custom_call_target="tpu_custom_call" | custom-call | flops 262144 | bytes 917504 | tf_op jit(solution)/shard_map/finish/pallas_call | solution.py:249
  (32 shorter events, 0.2 us)
Async XLA Ops:
  0.6 25.3 %copy-start.4 = (bf16[512,128]{1,0:T(8,128)(2,1)S(1)}, bf16[512,128]{1,0:T(8,128)(2,1)}, u32[]{:S(2)}) copy-start(bf16[512,128]{1,0:T(8,128)(2,1)} %rest_5_.5) | copy-start | bytes 393220
  0.6 25.3 %copy-start.5 = (bf16[512,128]{1,0:T(8,128)(2,1)S(1)}, bf16[512,128]{1,0:T(8,128)(2,1)}, u32[]{:S(2)}) copy-start(bf16[512,128]{1,0:T(8,128)(2,1)} %rest_6_.5) | copy-start | bytes 393220
  0.7 21.0 %copy-start.7 = (s32[4,2]{0,1:T(2,128)S(1)}, s32[4,2]{0,1:T(2,128)}, u32[]{:S(2)}) copy-start(s32[4,2]{0,1:T(2,128)} %param.14) | copy-start | bytes 100
  2.4 24.6 %copy-start.1 = (bf16[4,2,8,128,128]{4,3,2,1,0:T(8,128)(2,1)S(1)}, bf16[4,2,8,128,128]{4,3,2,1,0:T(8,128)(2,1)}, u32[]{:S(2)}) copy-start(bf16[4,2,8,128,128]{4,3,2,1,0:T(8,128)(2,1)} %rest_4_.5) | copy-start | bytes 6291460
  2.4 24.6 %copy-start.2 = (bf16[512,1024]{1,0:T(8,128)(2,1)S(1)}, bf16[512,1024]{1,0:T(8,128)(2,1)}, u32[]{:S(2)}) copy-start(bf16[512,1024]{1,0:T(8,128)(2,1)} %q_ref.5) | copy-start | bytes 3145732
  2.4 24.6 %copy-start.6 = (f32[512]{0:T(512)S(1)}, f32[512]{0:T(512)}, u32[]{:S(2)}) copy-start(f32[512]{0:T(512)} %param.15) | copy-start | bytes 6148
  2.4 19.3 %collective-permute-start.3 = (bf16[2,512,128]{2,1,0:T(8,128)(2,1)}, bf16[2,512,128]{2,1,0:T(8,128)(2,1)}, u32[]{:S(2)}, u32[]{:S(2)}) collective-permute-start(bf16[2,512,128]{2,1,0:T(8,128)(2,1)} %pad_maximum_fusion.2), channel_id=1, source_target_pairs={{0,4},{4,8},{8,12},{1,5},{5,9},{9,13},{2,6},{6,10},{10,14},{3,7},{... | collective-permute-start | bytes 786440 | tf_op jit(solution)/shard_map/ppermute | solution.py:28
  8.3 13.4 %collective-permute-start.2 = (bf16[2,512,128]{2,1,0:T(8,128)(2,1)}, bf16[2,512,128]{2,1,0:T(8,128)(2,1)}, u32[]{:S(2)}, u32[]{:S(2)}) collective-permute-start(bf16[2,512,128]{2,1,0:T(8,128)(2,1)} %pad_maximum_fusion.2), channel_id=1, source_target_pairs={{0,8},{1,9},{2,10},{3,11},{16,24},{17,25},{18,26},{19,27}} | collective-permute-start | bytes 786440 | tf_op jit(solution)/shard_map/ppermute | solution.py:348
  12.8 13.1 %collective-permute-start.1 = (bf16[2,512,128]{2,1,0:T(8,128)(2,1)}, bf16[2,512,128]{2,1,0:T(8,128)(2,1)}, u32[]{:S(2)}, u32[]{:S(2)}) collective-permute-start(bf16[2,512,128]{2,1,0:T(8,128)(2,1)} %pad_maximum_fusion.2), channel_id=1, source_target_pairs={{0,12},{1,13},{2,14},{3,15},{16,28},{17,29},{18,30},{19,31}} | collective-permute-start | bytes 786440 | tf_op jit(solution)/shard_map/ppermute | solution.py:348
  16.7 20.2 %collective-permute-start.4 = (bf16[1,1,8,128,128]{4,3,2,1,0:T(8,128)(2,1)}, bf16[1,1,8,128,128]{4,3,2,1,0:T(8,128)(2,1)}, u32[]{:S(2)}, u32[]{:S(2)}) collective-permute-start(bf16[1,1,8,128,128]{4,3,2,1,0:T(8,128)(2,1)} %get-tuple-element.53), channel_id=1, source_target_pairs={{0,4},{4,8},{8,12},{1,5},{5,9},{9,13},{2,6},{6,10},{10,14},{3,7},{... | collective-permute-start | bytes 786440 | tf_op jit(solution)/shard_map/ppermute | solution.py:28
  19.5 22.9 %collective-permute-start = (bf16[2,1,8,128,128]{4,3,2,1,0:T(8,128)(2,1)}, bf16[2,1,8,128,128]{4,3,2,1,0:T(8,128)(2,1)}, u32[]{:S(2)}, u32[]{:S(2)}) collective-permute-start(bf16[2,1,8,128,128]{4,3,2,1,0:T(8,128)(2,1)} %pad_maximum_fusion.1), channel_id=1, source_target_pairs={{0,4},{4,8},{8,12},{1,5},{5,9},{9,13},{2,6},{6,10},{10,14},{3,7},{... | collective-permute-start | bytes 1572872 | tf_op jit(solution)/shard_map/ppermute | solution.py:28
  21.7 5.3 %copy-start.3 = (bf16[512,1024]{1,0:T(8,128)(2,1)S(1)}, bf16[512,1024]{1,0:T(8,128)(2,1)}, u32[]{:S(2)}) copy-start(bf16[512,1024]{1,0:T(8,128)(2,1)} %g_ref.5) | copy-start | bytes 3145732
  27.0 9.9 %copy-start = (bf16[4,3,8,128,128]{4,3,2,1,0:T(8,128)(2,1)S(1)}, bf16[4,3,8,128,128]{4,3,2,1,0:T(8,128)(2,1)}, u32[]{:S(2)}) copy-start(bf16[4,3,8,128,128]{4,3,2,1,0:T(8,128)(2,1)} %rest_0_.5) | copy-start | bytes 9437188
  48.0 2.7 %collective-permute-start.8 = (f32[512]{0:T(512)S(1)}, f32[512]{0:T(512)S(1)}, u32[]{:S(2)}, u32[]{:S(2)}) collective-permute-start(f32[512]{0:T(512)S(1)} %bitcast.20), channel_id=1, source_target_pairs={{0,16},{16,0},{1,17},{17,1},{2,18},{18,2},{3,19},{19,3},{4,20},{20... | collective-permute-start | bytes 6152 | tf_op jit(solution)/shard_map/ppermute | solution.py:33
  48.2 8.2 %collective-permute-start.7 = (bf16[512,128]{1,0:T(8,128)(2,1)S(1)}, bf16[512,128]{1,0:T(8,128)(2,1)S(1)}, u32[]{:S(2)}, u32[]{:S(2)}) collective-permute-start(bf16[512,128]{1,0:T(8,128)(2,1)S(1)} %convert_element_type.23), channel_id=1, source_target_pairs={{4,0},{12,8},{5,1},{13,9},{6,2},{14,10},{7,3},{15,11},{20,16},{28,... | collective-permute-start | bytes 393224 | tf_op jit(solution)/shard_map/ppermute | solution.py:394
  49.5 9.7 %collective-permute-start.6 = (bf16[512,128]{1,0:T(8,128)(2,1)S(1)}, bf16[512,128]{1,0:T(8,128)(2,1)S(1)}, u32[]{:S(2)}, u32[]{:S(2)}) collective-permute-start(bf16[512,128]{1,0:T(8,128)(2,1)S(1)} %convert_element_type.22), channel_id=1, source_target_pairs={{4,0},{12,8},{5,1},{13,9},{6,2},{14,10},{7,3},{15,11},{20,16},{28,... | collective-permute-start | bytes 393224 | tf_op jit(solution)/shard_map/ppermute | solution.py:394
  50.8 3.7 %collective-permute-start.9 = (f32[512]{0:T(512)S(1)}, f32[512]{0:T(512)S(1)}, u32[]{:S(2)}, u32[]{:S(2)}) collective-permute-start(f32[512]{0:T(512)S(1)} %add.19), channel_id=1, source_target_pairs={{0,1},{1,0},{2,3},{3,2},{4,5},{5,4},{6,7},{7,6},{8,9},{9,8},{10,11... | collective-permute-start | bytes 6152 | tf_op jit(solution)/shard_map/ppermute | solution.py:33
  52.4 11.3 %collective-permute-start.5 = (bf16[2,2,128,128]{3,2,1,0:T(8,128)(2,1)S(1)}, bf16[2,2,128,128]{3,2,1,0:T(8,128)(2,1)S(1)}, u32[]{:S(2)}, u32[]{:S(2)}) collective-permute-start(bf16[2,2,128,128]{3,2,1,0:T(8,128)(2,1)S(1)} %add_convert_fusion.2), channel_id=1, source_target_pairs={{4,0},{8,4},{12,8},{5,1},{9,5},{13,9},{6,2},{10,6},{14,10},{7,3},{... | collective-permute-start | bytes 393224 | tf_op jit(solution)/shard_map/ppermute | solution.py:28
  56.4 8.1 %collective-permute-start.11 = (bf16[512,128]{1,0:T(8,128)(2,1)S(1)}, bf16[512,128]{1,0:T(8,128)(2,1)S(1)}, u32[]{:S(2)}, u32[]{:S(2)}) collective-permute-start(bf16[512,128]{1,0:T(8,128)(2,1)S(1)} %add_convert_fusion), channel_id=1, source_target_pairs={{8,0},{9,1},{10,2},{11,3},{24,16},{25,17},{26,18},{27,19}} | collective-permute-start | bytes 393224 | tf_op jit(solution)/shard_map/ppermute | solution.py:394
  59.2 3.9 %collective-permute-start.12 = (f32[512]{0:T(512)S(1)}, f32[512]{0:T(512)S(1)}, u32[]{:S(2)}, u32[]{:S(2)}) collective-permute-start(f32[512]{0:T(512)S(1)} %add.20), channel_id=1, source_target_pairs={{0,2},{1,3},{2,0},{3,1},{4,6},{5,7},{6,4},{7,5},{8,10},{9,11},{10,... | collective-permute-start | bytes 6152 | tf_op jit(solution)/shard_map/ppermute | solution.py:33
  60.8 7.7 %collective-permute-start.10 = (bf16[512,128]{1,0:T(8,128)(2,1)S(1)}, bf16[512,128]{1,0:T(8,128)(2,1)S(1)}, u32[]{:S(2)}, u32[]{:S(2)}) collective-permute-start(bf16[512,128]{1,0:T(8,128)(2,1)S(1)} %add_convert_fusion.1), channel_id=1, source_target_pairs={{8,0},{9,1},{10,2},{11,3},{24,16},{25,17},{26,18},{27,19}} | collective-permute-start | bytes 393224 | tf_op jit(solution)/shard_map/ppermute | solution.py:394

commit v10 on v9

--- a/solution.py
+++ b/solution.py
@@ -315,7 +315,7 @@
             scratch_shapes=[pltpu.VMEM((slots * BLK, heads * BLK), BF)] * 2
             + [pltpu.VMEM((2, slots * BLK, 2 * BLK), F32)] * 3,
         ),
-        compiler_params=pltpu.CompilerParams(vmem_limit_bytes=(28 if crossing else 46) * 1024 * 1024),
+        compiler_params=pltpu.CompilerParams(vmem_limit_bytes=(28 if crossing else 48) * 1024 * 1024),
         cost_estimate=pl.CostEstimate(
             flops=elements * E * 10, bytes_accessed=elements * 3, transcendentals=2 * elements
         ),

time: 69.8 us -> 67.8 us (0.971)
  waiting for transfers between devices: 13.2 us -> 15.6 us
  local copies, waits for them, and re-layouts: 4.01 us -> 2.08 us
  starting transfers between devices: 26.1 us -> 24.5 us
  Pallas kernels: 20.7 us -> 19.8 us
    ppermute x4, starting transfers between devices: 11.3 us -> 8.96 us  [shift(): return lax.ppermute(block, axis, route)]
    ppermute x2, waiting for transfers between devices: 4.23 us -> 5.67 us  [local(): more = lax.ppermute(known, 'seq', route)]
    slice x1, local copies, waits for them, and re-layouts: 1.07 us -> 0.03 us  [local(): incoming[block] = {d: came[i:i + 1] for i, d in enumerate(offsets)}]
    ppermute x4, waiting for transfers between devices: 0.01 us -> 0.98 us  [shift(): return lax.ppermute(block, axis, route)]
    slice x1, local copies, waits for them, and re-layouts: 0.92 us -> 0.01 us  [local(): before = got[:, tail].reshape(2, LEAD, BLK, E)]
    pallas_call x3, Pallas kernels: 19.9 us -> 19 us  [run_blocks(): pl.pallas_call(functools.partial(block_kernel, first, crossing, slots, ch...]
  transfers between devices with their start and end apart: 13 -> 13, of which waited for: 6 -> 7; matrix products, arithmetic and copies ran while one was open for 8% -> 7% of each run, Pallas kernels for 22% -> 22%
where the time goes in v10:
time: 67.8 us; the launch traced here: 67.4 us
  starting transfers between devices  24.5 us (36%)
  Pallas kernels  19.8 us (29%)
  waiting for transfers between devices  15.6 us (23%)
  other arithmetic  4.43 us (7%)
  local copies, waits for them, and re-layouts  2.08 us (3%)
  between operations  0.92 us (1%)
    pallas_call x3, Pallas kernels, run_blocks(): pl.pallas_call(functools.partial(block_kernel, first, crossing, slots, ch...  19 us
    ppermute x4, starting transfers between devices, shift(): return lax.ppermute(block, axis, route)  8.96 us
    ppermute x4, waiting for transfers between devices, local(): came = [lax.ppermute(x, 'seq', route) for x in low]  8.21 us
    ppermute x2, starting transfers between devices, local(): more = lax.ppermute(known, 'seq', route)  7.18 us
    ppermute x2, waiting for transfers between devices, local(): more = lax.ppermute(known, 'seq', route)  5.67 us
    ppermute x4, starting transfers between devices, local(): came = [lax.ppermute(x, 'seq', route) for x in low]  5.16 us
    ppermute x3, starting transfers between devices, exchange_sum(): lax.ppermute(block, axis, [(i, i ^ step) for i in range(lax.axis_size(axi...  3.21 us
    slice x1, local copies, waits for them, and re-layouts, local(): teacher_window[blocks + block - d:blocks + block - d + 1, d:d + 1]  1.89 us
  transfers between devices with their start and end apart: 13, of which 7 were waited for; matrix products, arithmetic and copies ran while one was open for 7% of the time, Pallas kernels for 22%

profile of v10, /device:TPU:0, one launch (start us, length us, event | category | flops | bytes accessed | tf_op | source)
XLA Modules:
  0.0 67.4 jit_solution(15733308536681182566)
XLA Ops:
  0.7 1.7 %pad_maximum_fusion.2 = bf16[2,512,128]{2,1,0:T(8,128)(2,1)} fusion(bf16[1,512,128]{2,1,0:T(8,128)(2,1)} %bitcast.13, bf16[1,512,128]{2,1,0:T(8,128)(2,1)} %bitcast.11), kind=kLoop, calls=%fused_computation.2 | loop fusion | flops 131072 | bytes 524288 | tf_op jit(solution)/shard_map/stack | solution.py:337
  2.4 5.1 %collective-permute-start.3 = (bf16[2,512,128]{2,1,0:T(8,128)(2,1)}, bf16[2,512,128]{2,1,0:T(8,128)(2,1)S(1)}, u32[]{:S(2)}, u32[]{:S(2)}) collective-permute-start(bf16[2,512,128]{2,1,0:T(8,128)(2,1)} %pad_maximum_fusion.2), channel_id=1, source_target_pairs={{0,4},{4,8},{8,12},{1,5},{5,9},{9,13},{2,6},{6,10},{10,14},{3,7},{... | collective-permute-start | bytes 786440 | tf_op jit(solution)/shard_map/ppermute | solution.py:28
  7.5 5.2 %collective-permute-start.2 = (bf16[2,512,128]{2,1,0:T(8,128)(2,1)}, bf16[2,512,128]{2,1,0:T(8,128)(2,1)}, u32[]{:S(2)}, u32[]{:S(2)}) collective-permute-start(bf16[2,512,128]{2,1,0:T(8,128)(2,1)} %pad_maximum_fusion.2), channel_id=1, source_target_pairs={{0,8},{1,9},{2,10},{3,11},{16,24},{17,25},{18,26},{19,27}} | collective-permute-start | bytes 786440 | tf_op jit(solution)/shard_map/ppermute | solution.py:348
  12.7 2.0 %collective-permute-start.1 = (bf16[2,512,128]{2,1,0:T(8,128)(2,1)}, bf16[2,512,128]{2,1,0:T(8,128)(2,1)}, u32[]{:S(2)}, u32[]{:S(2)}) collective-permute-start(bf16[2,512,128]{2,1,0:T(8,128)(2,1)} %pad_maximum_fusion.2), channel_id=1, source_target_pairs={{0,12},{1,13},{2,14},{3,15},{16,28},{17,29},{18,30},{19,31}} | collective-permute-start | bytes 786440 | tf_op jit(solution)/shard_map/ppermute | solution.py:348
  14.7 1.9 %fusion = (bf16[1,1,8,128,128]{4,3,2,1,0:T(8,128)(2,1)S(1)}, bf16[1,1,8,128,128]{4,3,2,1,0:T(8,128)(2,1)}, bf16[1,1,8,128,128]{4,3,2,1,0:T(8,128)(2,1)S(1)}) fusion(bf16[4,3,8,128,128]{4,3,2,1,0:T(8,128)(2,1)} %rest_0_.5), kind=kLoop, calls=%fused_computation.10 | loop fusion | bytes 1572864 | tf_op jit(solution)/shard_map/slice | solution.py:357
  16.6 1.3 %collective-permute-start.4 = (bf16[1,1,8,128,128]{4,3,2,1,0:T(8,128)(2,1)}, bf16[1,1,8,128,128]{4,3,2,1,0:T(8,128)(2,1)S(1)}, u32[]{:S(2)}, u32[]{:S(2)}) collective-permute-start(bf16[1,1,8,128,128]{4,3,2,1,0:T(8,128)(2,1)} %get-tuple-element.53), channel_id=1, source_target_pairs={{0,4},{4,8},{8,12},{1,5},{5,9},{9,13},{2,6},{6,10},{10,14},{3,7},{... | collective-permute-start | bytes 786440 | tf_op jit(solution)/shard_map/ppermute | solution.py:28
  17.9 0.8 %pad_maximum_fusion.1 = bf16[2,1,8,128,128]{4,3,2,1,0:T(8,128)(2,1)} fusion(bf16[1,1,8,128,128]{4,3,2,1,0:T(8,128)(2,1)S(1)} %get-tuple-element.54, bf16[1,1,8,128,128]{4,3,2,1,0:T(8,128)(2,1)S(1)} %get-tuple-element.52), kind=kLoop, calls=%fused_computation.1 | loop fusion | flops 262144 | bytes 1048576 | tf_op jit(solution)/shard_map/concatenate | solution.py:356
  18.7 1.3 %collective-permute-start = (bf16[2,1,8,128,128]{4,3,2,1,0:T(8,128)(2,1)}, bf16[2,1,8,128,128]{4,3,2,1,0:T(8,128)(2,1)S(1)}, u32[]{:S(2)}, u32[]{:S(2)}) collective-permute-start(bf16[2,1,8,128,128]{4,3,2,1,0:T(8,128)(2,1)} %pad_maximum_fusion.1), channel_id=1, source_target_pairs={{0,4},{4,8},{8,12},{1,5},{5,9},{9,13},{2,6},{6,10},{10,14},{3,7},{... | collective-permute-start | bytes 1572872 | tf_op jit(solution)/shard_map/ppermute | solution.py:28
  20.0 0.1 copy.14.picks_ref
  20.1 0.0 collective-permute-done.2
  20.1 5.7 %collective-permute-done.1 = bf16[2,512,128]{2,1,0:T(8,128)(2,1)} collective-permute-done((bf16[2,512,128]{2,1,0:T(8,128)(2,1)}, bf16[2,512,128]{2,1,0:T(8,128)(2,1)}, u32[]{:S(2)}, u32[]{:S(2)}) %collective-permute-start.1) | collective-permute-done | bytes 262176 | tf_op jit(solution)/shard_map/ppermute | solution.py:348
  25.8 0.1 select_select_fusion
  26.0 10.0 %blocks_from_2.1 = (bf16[256,1024]{1,0:T(8,128)(2,1)S(1)}, f32[2,1,128]{2,1,0:T(1,128)S(1)}, f32[512,128]{1,0:T(8,128)S(1)}, f32[512,128]{1,0:T(8,128)S(1)}, f32...) custom-call(s32[1]{0:T(128)} %bitcast.base_ref, s32[4,2]{1,0:T(4,128)S(1)} %copy.14.picks_ref, ...), custom_call_target="tpu_custom_call" | custom-call | flops 1677721600 | bytes 3932160 | tf_op jit(solution)/shard_map/blocks_from_2/pallas_call | solution.py:307
  36.1 4.5 %blocks_from_1.1 = (bf16[128,1024]{1,0:T(8,128)(2,1)S(1)}, f32[1,1,128]{2,1,0:T(1,128)S(1)}, f32[512,128]{1,0:T(8,128)S(1)}, f32[512,128]{1,0:T(8,128)S(1)}, f32...) custom-call(s32[1]{0:T(128)} %bitcast.base_ref, s32[4,2]{1,0:T(4,128)S(1)} %copy.14.picks_ref, ...), custom_call_target="tpu_custom_call" | custom-call | flops 838860800 | bytes 1966080 | tf_op jit(solution)/shard_map/blocks_from_1/pallas_call | solution.py:307
  40.5 1.0 %collective-permute-done = bf16[2,1,8,128,128]{4,3,2,1,0:T(8,128)(2,1)S(1)} collective-permute-done((bf16[2,1,8,128,128]{4,3,2,1,0:T(8,128)(2,1)}, bf16[2,1,8,128,128]{4,3,2,1,0:T(8,128)(2,1)S(1)}, u32[]{:S(2)}, u32[]{:S(2)}) %collective-permute-start) | collective-permute-done | bytes 524320 | tf_op jit(solution)/shard_map/ppermute | solution.py:28
  41.6 4.5 %blocks_from_0.1 = (bf16[128,1024]{1,0:T(8,128)(2,1)S(1)}, f32[1,1,128]{2,1,0:T(1,128)S(1)}, f32[512,128]{1,0:T(8,128)S(1)}, f32[512,128]{1,0:T(8,128)S(1)}, f32...) custom-call(s32[1]{0:T(128)} %bitcast.base_ref, s32[4,2]{1,0:T(4,128)S(1)} %copy.14.picks_ref, ...), custom_call_target="tpu_custom_call" | custom-call | flops 838860800 | bytes 1966080 | tf_op jit(solution)/shard_map/blocks_from_0/pallas_call | solution.py:307
  46.1 0.1 collective-permute-start.8
  46.2 1.3 %collective-permute-start.7 = (bf16[512,128]{1,0:T(8,128)(2,1)S(1)}, bf16[512,128]{1,0:T(8,128)(2,1)S(1)}, u32[]{:S(2)}, u32[]{:S(2)}) collective-permute-start(bf16[512,128]{1,0:T(8,128)(2,1)S(1)} %convert_element_type.23), channel_id=1, source_target_pairs={{4,0},{12,8},{5,1},{13,9},{6,2},{14,10},{7,3},{15,11},{20,16},{28,... | collective-permute-start | bytes 393224 | tf_op jit(solution)/shard_map/ppermute | solution.py:394
  47.5 1.3 %collective-permute-start.6 = (bf16[512,128]{1,0:T(8,128)(2,1)S(1)}, bf16[512,128]{1,0:T(8,128)(2,1)S(1)}, u32[]{:S(2)}, u32[]{:S(2)}) collective-permute-start(bf16[512,128]{1,0:T(8,128)(2,1)S(1)} %convert_element_type.22), channel_id=1, source_target_pairs={{4,0},{12,8},{5,1},{13,9},{6,2},{14,10},{7,3},{15,11},{20,16},{28,... | collective-permute-start | bytes 393224 | tf_op jit(solution)/shard_map/ppermute | solution.py:394
  48.8 1.6 %collective-permute-start.9 = (f32[512]{0:T(512)S(1)}, f32[512]{0:T(512)S(1)}, u32[]{:S(2)}, u32[]{:S(2)}) collective-permute-start(f32[512]{0:T(512)S(1)} %add.19), channel_id=1, source_target_pairs={{0,1},{1,0},{2,3},{3,2},{4,5},{5,4},{6,7},{7,6},{8,9},{9,8},{10,11... | collective-permute-start | bytes 6152 | tf_op jit(solution)/shard_map/ppermute | solution.py:33
  50.4 1.3 %collective-permute-start.5 = (bf16[2,2,128,128]{3,2,1,0:T(8,128)(2,1)S(1)}, bf16[2,2,128,128]{3,2,1,0:T(8,128)(2,1)S(1)}, u32[]{:S(2)}, u32[]{:S(2)}) collective-permute-start(bf16[2,2,128,128]{3,2,1,0:T(8,128)(2,1)S(1)} %add_convert_fusion.2), channel_id=1, source_target_pairs={{4,0},{8,4},{12,8},{5,1},{9,5},{13,9},{6,2},{10,6},{14,10},{7,3},{... | collective-permute-start | bytes 393224 | tf_op jit(solution)/shard_map/ppermute | solution.py:28
  51.7 0.8 %collective-permute-done.9 = f32[512]{0:T(512)S(1)} collective-permute-done((f32[512]{0:T(512)S(1)}, f32[512]{0:T(512)S(1)}, u32[]{:S(2)}, u32[]{:S(2)}) %collective-permute-start.9) | collective-permute-done | bytes 2080 | tf_op jit(solution)/shard_map/ppermute | solution.py:33
  52.5 1.9 %collective-permute-done.7.rest_1_ = bf16[512,128]{1,0:T(8,128)(2,1)S(1)} collective-permute-done((bf16[512,128]{1,0:T(8,128)(2,1)S(1)}, bf16[512,128]{1,0:T(8,128)(2,1)S(1)}, u32[]{:S(2)}, u32[]{:S(2)}) %collective-permute-start.7) | collective-permute-done | bytes 131104 | tf_op jit(solution)/shard_map/ppermute | solution.py:394
  54.4 1.3 %collective-permute-start.11 = (bf16[512,128]{1,0:T(8,128)(2,1)S(1)}, bf16[512,128]{1,0:T(8,128)(2,1)S(1)}, u32[]{:S(2)}, u32[]{:S(2)}) collective-permute-start(bf16[512,128]{1,0:T(8,128)(2,1)S(1)} %add_convert_fusion), channel_id=1, source_target_pairs={{8,0},{9,1},{10,2},{11,3},{24,16},{25,17},{26,18},{27,19}} | collective-permute-start | bytes 393224 | tf_op jit(solution)/shard_map/ppermute | solution.py:394
  55.7 1.5 %collective-permute-done.6.rest_0_ = bf16[512,128]{1,0:T(8,128)(2,1)S(1)} collective-permute-done((bf16[512,128]{1,0:T(8,128)(2,1)S(1)}, bf16[512,128]{1,0:T(8,128)(2,1)S(1)}, u32[]{:S(2)}, u32[]{:S(2)}) %collective-permute-start.6) | collective-permute-done | bytes 131104 | tf_op jit(solution)/shard_map/ppermute | solution.py:394
  57.2 1.6 %collective-permute-start.12 = (f32[512]{0:T(512)S(1)}, f32[512]{0:T(512)S(1)}, u32[]{:S(2)}, u32[]{:S(2)}) collective-permute-start(f32[512]{0:T(512)S(1)} %add.20), channel_id=1, source_target_pairs={{0,2},{1,3},{2,0},{3,1},{4,6},{5,7},{6,4},{7,5},{8,10},{9,11},{10,... | collective-permute-start | bytes 6152 | tf_op jit(solution)/shard_map/ppermute | solution.py:33
  58.8 1.3 %collective-permute-start.10 = (bf16[512,128]{1,0:T(8,128)(2,1)S(1)}, bf16[512,128]{1,0:T(8,128)(2,1)S(1)}, u32[]{:S(2)}, u32[]{:S(2)}) collective-permute-start(bf16[512,128]{1,0:T(8,128)(2,1)S(1)} %add_convert_fusion.1), channel_id=1, source_target_pairs={{8,0},{9,1},{10,2},{11,3},{24,16},{25,17},{26,18},{27,19}} | collective-permute-start | bytes 393224 | tf_op jit(solution)/shard_map/ppermute | solution.py:394
  60.1 1.0 %pad_maximum_fusion = bf16[512,1024]{1,0:T(8,128)(2,1)} fusion(bf16[256,1024]{1,0:T(8,128)(2,1)S(1)} %get-tuple-element.38, bf16[128,1024]{1,0:T(8,128)(2,1)S(1)} %get-tuple-element.37, bf16[128,1024]{1,0:T(8,128)(2,1)S(1)} %get-tuple-element.36), kind=kLoop, calls=%fused_computation | loop fusion | flops 3145728 | bytes 2097152 | tf_op jit(solution)/shard_map/concatenate | solution.py:376
  61.2 0.6 add.23
  61.7 0.8 %collective-permute-done.11.rest_3_ = bf16[512,128]{1,0:T(8,128)(2,1)S(1)} collective-permute-done((bf16[512,128]{1,0:T(8,128)(2,1)S(1)}, bf16[512,128]{1,0:T(8,128)(2,1)S(1)}, u32[]{:S(2)}, u32[]{:S(2)}) %collective-permute-start.11) | collective-permute-done | bytes 131104 | tf_op jit(solution)/shard_map/ppermute | solution.py:394
  62.6 4.0 %collective-permute-done.10.rest_2_ = bf16[512,128]{1,0:T(8,128)(2,1)S(1)} collective-permute-done((bf16[512,128]{1,0:T(8,128)(2,1)S(1)}, bf16[512,128]{1,0:T(8,128)(2,1)S(1)}, u32[]{:S(2)}, u32[]{:S(2)}) %collective-permute-start.10) | collective-permute-done | bytes 131104 | tf_op jit(solution)/shard_map/ppermute | solution.py:394
  66.6 0.8 %finish.1 = (bf16[512,128]{1,0:T(8,128)(2,1)}, bf16[512,128]{1,0:T(8,128)(2,1)}) custom-call(s32[1]{0:T(128)} %bitcast.7.root_ref, f32[512,128]{1,0:T(8,128)S(1)} %get-tuple-element.39.dk_ref, f32[512,128]{1,0:T(8,128)S(1)} %get-tuple-element.40.dv_ref, f32[512,128]{1,0:T(8,128)S(1)} %get-tuple-element.41.dsk_ref, f32[512,128]{1,0:T(8,128)S(1)} %get-tuple-element.42.dsv_ref, ...), custom_call_target="tpu_custom_call" | custom-call | flops 262144 | bytes 917504 | tf_op jit(solution)/shard_map/finish/pallas_call | solution.py:249
  (32 shorter events, 0.3 us)
Async XLA Ops:
  0.6 25.2 %copy-start.4 = (bf16[512,128]{1,0:T(8,128)(2,1)S(1)}, bf16[512,128]{1,0:T(8,128)(2,1)}, u32[]{:S(2)}) copy-start(bf16[512,128]{1,0:T(8,128)(2,1)} %rest_5_.5) | copy-start | bytes 393220
  0.6 25.2 %copy-start.5 = (bf16[512,128]{1,0:T(8,128)(2,1)S(1)}, bf16[512,128]{1,0:T(8,128)(2,1)}, u32[]{:S(2)}) copy-start(bf16[512,128]{1,0:T(8,128)(2,1)} %rest_6_.5) | copy-start | bytes 393220
  0.7 19.4 %copy-start.7 = (s32[4,2]{0,1:T(2,128)S(1)}, s32[4,2]{0,1:T(2,128)}, u32[]{:S(2)}) copy-start(s32[4,2]{0,1:T(2,128)} %param.14) | copy-start | bytes 100
  2.4 23.5 %copy-start.2 = (bf16[512,1024]{1,0:T(8,128)(2,1)S(1)}, bf16[512,1024]{1,0:T(8,128)(2,1)}, u32[]{:S(2)}) copy-start(bf16[512,1024]{1,0:T(8,128)(2,1)} %q_ref.5) | copy-start | bytes 3145732
  2.4 23.5 %copy-start.3 = (bf16[512,1024]{1,0:T(8,128)(2,1)S(1)}, bf16[512,1024]{1,0:T(8,128)(2,1)}, u32[]{:S(2)}) copy-start(bf16[512,1024]{1,0:T(8,128)(2,1)} %g_ref.5) | copy-start | bytes 3145732
  2.4 23.5 %copy-start.6 = (f32[512]{0:T(512)S(1)}, f32[512]{0:T(512)}, u32[]{:S(2)}) copy-start(f32[512]{0:T(512)} %param.15) | copy-start | bytes 6148
  2.4 17.7 %collective-permute-start.3 = (bf16[2,512,128]{2,1,0:T(8,128)(2,1)}, bf16[2,512,128]{2,1,0:T(8,128)(2,1)S(1)}, u32[]{:S(2)}, u32[]{:S(2)}) collective-permute-start(bf16[2,512,128]{2,1,0:T(8,128)(2,1)} %pad_maximum_fusion.2), channel_id=1, source_target_pairs={{0,4},{4,8},{8,12},{1,5},{5,9},{9,13},{2,6},{6,10},{10,14},{3,7},{... | collective-permute-start | bytes 786440 | tf_op jit(solution)/shard_map/ppermute | solution.py:28
  7.5 12.7 %collective-permute-start.2 = (bf16[2,512,128]{2,1,0:T(8,128)(2,1)}, bf16[2,512,128]{2,1,0:T(8,128)(2,1)}, u32[]{:S(2)}, u32[]{:S(2)}) collective-permute-start(bf16[2,512,128]{2,1,0:T(8,128)(2,1)} %pad_maximum_fusion.2), channel_id=1, source_target_pairs={{0,8},{1,9},{2,10},{3,11},{16,24},{17,25},{18,26},{19,27}} | collective-permute-start | bytes 786440 | tf_op jit(solution)/shard_map/ppermute | solution.py:348
  12.7 13.1 %collective-permute-start.1 = (bf16[2,512,128]{2,1,0:T(8,128)(2,1)}, bf16[2,512,128]{2,1,0:T(8,128)(2,1)}, u32[]{:S(2)}, u32[]{:S(2)}) collective-permute-start(bf16[2,512,128]{2,1,0:T(8,128)(2,1)} %pad_maximum_fusion.2), channel_id=1, source_target_pairs={{0,12},{1,13},{2,14},{3,15},{16,28},{17,29},{18,30},{19,31}} | collective-permute-start | bytes 786440 | tf_op jit(solution)/shard_map/ppermute | solution.py:348
  16.6 19.5 %collective-permute-start.4 = (bf16[1,1,8,128,128]{4,3,2,1,0:T(8,128)(2,1)}, bf16[1,1,8,128,128]{4,3,2,1,0:T(8,128)(2,1)S(1)}, u32[]{:S(2)}, u32[]{:S(2)}) collective-permute-start(bf16[1,1,8,128,128]{4,3,2,1,0:T(8,128)(2,1)} %get-tuple-element.53), channel_id=1, source_target_pairs={{0,4},{4,8},{8,12},{1,5},{5,9},{9,13},{2,6},{6,10},{10,14},{3,7},{... | collective-permute-start | bytes 786440 | tf_op jit(solution)/shard_map/ppermute | solution.py:28
  18.7 22.8 %collective-permute-start = (bf16[2,1,8,128,128]{4,3,2,1,0:T(8,128)(2,1)}, bf16[2,1,8,128,128]{4,3,2,1,0:T(8,128)(2,1)S(1)}, u32[]{:S(2)}, u32[]{:S(2)}) collective-permute-start(bf16[2,1,8,128,128]{4,3,2,1,0:T(8,128)(2,1)} %pad_maximum_fusion.1), channel_id=1, source_target_pairs={{0,4},{4,8},{8,12},{1,5},{5,9},{9,13},{2,6},{6,10},{10,14},{3,7},{... | collective-permute-start | bytes 1572872 | tf_op jit(solution)/shard_map/ppermute | solution.py:28
  26.0 10.1 %copy-start = (bf16[4,3,8,128,128]{4,3,2,1,0:T(8,128)(2,1)S(1)}, bf16[4,3,8,128,128]{4,3,2,1,0:T(8,128)(2,1)}, u32[]{:S(2)}) copy-start(bf16[4,3,8,128,128]{4,3,2,1,0:T(8,128)(2,1)} %rest_0_.5) | copy-start | bytes 9437188
  26.0 10.1 %copy-start.1 = (bf16[4,2,8,128,128]{4,3,2,1,0:T(8,128)(2,1)S(1)}, bf16[4,2,8,128,128]{4,3,2,1,0:T(8,128)(2,1)}, u32[]{:S(2)}) copy-start(bf16[4,2,8,128,128]{4,3,2,1,0:T(8,128)(2,1)} %rest_4_.5) | copy-start | bytes 6291460
  46.1 2.7 %collective-permute-start.8 = (f32[512]{0:T(512)S(1)}, f32[512]{0:T(512)S(1)}, u32[]{:S(2)}, u32[]{:S(2)}) collective-permute-start(f32[512]{0:T(512)S(1)} %bitcast.20), channel_id=1, source_target_pairs={{0,16},{16,0},{1,17},{17,1},{2,18},{18,2},{3,19},{19,3},{4,20},{20... | collective-permute-start | bytes 6152 | tf_op jit(solution)/shard_map/ppermute | solution.py:33
  46.2 8.2 %collective-permute-start.7 = (bf16[512,128]{1,0:T(8,128)(2,1)S(1)}, bf16[512,128]{1,0:T(8,128)(2,1)S(1)}, u32[]{:S(2)}, u32[]{:S(2)}) collective-permute-start(bf16[512,128]{1,0:T(8,128)(2,1)S(1)} %convert_element_type.23), channel_id=1, source_target_pairs={{4,0},{12,8},{5,1},{13,9},{6,2},{14,10},{7,3},{15,11},{20,16},{28,... | collective-permute-start | bytes 393224 | tf_op jit(solution)/shard_map/ppermute | solution.py:394
  47.5 9.7 %collective-permute-start.6 = (bf16[512,128]{1,0:T(8,128)(2,1)S(1)}, bf16[512,128]{1,0:T(8,128)(2,1)S(1)}, u32[]{:S(2)}, u32[]{:S(2)}) collective-permute-start(bf16[512,128]{1,0:T(8,128)(2,1)S(1)} %convert_element_type.22), channel_id=1, source_target_pairs={{4,0},{12,8},{5,1},{13,9},{6,2},{14,10},{7,3},{15,11},{20,16},{28,... | collective-permute-start | bytes 393224 | tf_op jit(solution)/shard_map/ppermute | solution.py:394
  48.8 3.7 %collective-permute-start.9 = (f32[512]{0:T(512)S(1)}, f32[512]{0:T(512)S(1)}, u32[]{:S(2)}, u32[]{:S(2)}) collective-permute-start(f32[512]{0:T(512)S(1)} %add.19), channel_id=1, source_target_pairs={{0,1},{1,0},{2,3},{3,2},{4,5},{5,4},{6,7},{7,6},{8,9},{9,8},{10,11... | collective-permute-start | bytes 6152 | tf_op jit(solution)/shard_map/ppermute | solution.py:33
  50.4 11.3 %collective-permute-start.5 = (bf16[2,2,128,128]{3,2,1,0:T(8,128)(2,1)S(1)}, bf16[2,2,128,128]{3,2,1,0:T(8,128)(2,1)S(1)}, u32[]{:S(2)}, u32[]{:S(2)}) collective-permute-start(bf16[2,2,128,128]{3,2,1,0:T(8,128)(2,1)S(1)} %add_convert_fusion.2), channel_id=1, source_target_pairs={{4,0},{8,4},{12,8},{5,1},{9,5},{13,9},{6,2},{10,6},{14,10},{7,3},{... | collective-permute-start | bytes 393224 | tf_op jit(solution)/shard_map/ppermute | solution.py:28
  54.4 8.1 %collective-permute-start.11 = (bf16[512,128]{1,0:T(8,128)(2,1)S(1)}, bf16[512,128]{1,0:T(8,128)(2,1)S(1)}, u32[]{:S(2)}, u32[]{:S(2)}) collective-permute-start(bf16[512,128]{1,0:T(8,128)(2,1)S(1)} %add_convert_fusion), channel_id=1, source_target_pairs={{8,0},{9,1},{10,2},{11,3},{24,16},{25,17},{26,18},{27,19}} | collective-permute-start | bytes 393224 | tf_op jit(solution)/shard_map/ppermute | solution.py:394
  57.2 3.9 %collective-permute-start.12 = (f32[512]{0:T(512)S(1)}, f32[512]{0:T(512)S(1)}, u32[]{:S(2)}, u32[]{:S(2)}) collective-permute-start(f32[512]{0:T(512)S(1)} %add.20), channel_id=1, source_target_pairs={{0,2},{1,3},{2,0},{3,1},{4,6},{5,7},{6,4},{7,5},{8,10},{9,11},{10,... | collective-permute-start | bytes 6152 | tf_op jit(solution)/shard_map/ppermute | solution.py:33
  58.8 7.7 %collective-permute-start.10 = (bf16[512,128]{1,0:T(8,128)(2,1)S(1)}, bf16[512,128]{1,0:T(8,128)(2,1)S(1)}, u32[]{:S(2)}, u32[]{:S(2)}) collective-permute-start(bf16[512,128]{1,0:T(8,128)(2,1)S(1)} %add_convert_fusion.1), channel_id=1, source_target_pairs={{8,0},{9,1},{10,2},{11,3},{24,16},{25,17},{26,18},{27,19}} | collective-permute-start | bytes 393224 | tf_op jit(solution)/shard_map/ppermute | solution.py:394

commit v11 on v10

--- a/solution.py
+++ b/solution.py
@@ -392,8 +392,9 @@
         if number == 1:
             row_terms, low[0] = lax.optimization_barrier((row_terms, low[0]))
         came = [lax.ppermute(x, "seq", route) for x in low]
-        if number == 0:
-            returned = shift(back.astype(BF), "seq", -1)
+        if number == min(1, len(steps) - 1):
+            leaving, low[1] = lax.optimization_barrier((back.astype(BF), low[1]))
+            returned = shift(leaving, "seq", -1)
         sums = [x + y.astype(F32) for x, y in zip(sums, came)]
         arrived += came
     row_loss = exchange_sum(row_terms, "head", late)

time: 67.8 us -> 69 us (1.018)
  waiting for transfers between devices: 15.6 us -> 16.9 us
    ppermute x4, waiting for transfers between devices: 8.21 us -> 4.07 us  [local(): came = [lax.ppermute(x, 'seq', route) for x in low]]
    ppermute x4, waiting for transfers between devices: 0.98 us -> 5.05 us  [shift(): return lax.ppermute(block, axis, route)]
    ppermute x3, waiting for transfers between devices: 0.76 us -> 2.06 us  [exchange_sum(): lax.ppermute(block, axis, [(i, i ^ step) for i in range(lax.axis_size(axi...]
  transfers between devices with their start and end apart: 13 -> 13, of which waited for: 7 -> 6; matrix products, arithmetic and copies ran while one was open for 7% -> 7% of each run, Pallas kernels for 22% -> 21%
where the time goes in v11:
time: 69 us; the launch traced here: 68.6 us
  starting transfers between devices  24.5 us (36%)
  Pallas kernels  19.8 us (29%)
  waiting for transfers between devices  16.9 us (24%)
  other arithmetic  4.43 us (6%)
  local copies, waits for them, and re-layouts  2.08 us (3%)
  between operations  0.93 us (1%)
    pallas_call x3, Pallas kernels, run_blocks(): pl.pallas_call(functools.partial(block_kernel, first, crossing, slots, ch...  19 us
    ppermute x4, starting transfers between devices, shift(): return lax.ppermute(block, axis, route)  8.96 us
    ppermute x2, starting transfers between devices, local(): more = lax.ppermute(known, 'seq', route)  7.18 us
    ppermute x2, waiting for transfers between devices, local(): more = lax.ppermute(known, 'seq', route)  5.67 us
    ppermute x4, starting transfers between devices, local(): came = [lax.ppermute(x, 'seq', route) for x in low]  5.16 us
    ppermute x4, waiting for transfers between devices, shift(): return lax.ppermute(block, axis, route)  5.05 us
    ppermute x4, waiting for transfers between devices, local(): came = [lax.ppermute(x, 'seq', route) for x in low]  4.07 us
    ppermute x3, starting transfers between devices, exchange_sum(): lax.ppermute(block, axis, [(i, i ^ step) for i in range(lax.axis_size(axi...  3.21 us
  transfers between devices with their start and end apart: 13, of which 6 were waited for; matrix products, arithmetic and copies ran while one was open for 7% of the time, Pallas kernels for 21%

profile of v11, /device:TPU:0, one launch (start us, length us, event | category | flops | bytes accessed | tf_op | source)
XLA Modules:
  0.0 68.6 jit_solution(6072864619934269402)
XLA Ops:
  0.7 1.7 %pad_maximum_fusion.2 = bf16[2,512,128]{2,1,0:T(8,128)(2,1)} fusion(bf16[1,512,128]{2,1,0:T(8,128)(2,1)} %bitcast.13, bf16[1,512,128]{2,1,0:T(8,128)(2,1)} %bitcast.11), kind=kLoop, calls=%fused_computation.2 | loop fusion | flops 131072 | bytes 524288 | tf_op jit(solution)/shard_map/stack | solution.py:337
  2.4 5.1 %collective-permute-start.3 = (bf16[2,512,128]{2,1,0:T(8,128)(2,1)}, bf16[2,512,128]{2,1,0:T(8,128)(2,1)S(1)}, u32[]{:S(2)}, u32[]{:S(2)}) collective-permute-start(bf16[2,512,128]{2,1,0:T(8,128)(2,1)} %pad_maximum_fusion.2), channel_id=1, source_target_pairs={{0,4},{4,8},{8,12},{1,5},{5,9},{9,13},{2,6},{6,10},{10,14},{3,7},{... | collective-permute-start | bytes 786440 | tf_op jit(solution)/shard_map/ppermute | solution.py:28
  7.5 5.2 %collective-permute-start.2 = (bf16[2,512,128]{2,1,0:T(8,128)(2,1)}, bf16[2,512,128]{2,1,0:T(8,128)(2,1)}, u32[]{:S(2)}, u32[]{:S(2)}) collective-permute-start(bf16[2,512,128]{2,1,0:T(8,128)(2,1)} %pad_maximum_fusion.2), channel_id=1, source_target_pairs={{0,8},{1,9},{2,10},{3,11},{16,24},{17,25},{18,26},{19,27}} | collective-permute-start | bytes 786440 | tf_op jit(solution)/shard_map/ppermute | solution.py:348
  12.7 2.0 %collective-permute-start.1 = (bf16[2,512,128]{2,1,0:T(8,128)(2,1)}, bf16[2,512,128]{2,1,0:T(8,128)(2,1)}, u32[]{:S(2)}, u32[]{:S(2)}) collective-permute-start(bf16[2,512,128]{2,1,0:T(8,128)(2,1)} %pad_maximum_fusion.2), channel_id=1, source_target_pairs={{0,12},{1,13},{2,14},{3,15},{16,28},{17,29},{18,30},{19,31}} | collective-permute-start | bytes 786440 | tf_op jit(solution)/shard_map/ppermute | solution.py:348
  14.7 1.9 %fusion = (bf16[1,1,8,128,128]{4,3,2,1,0:T(8,128)(2,1)S(1)}, bf16[1,1,8,128,128]{4,3,2,1,0:T(8,128)(2,1)}, bf16[1,1,8,128,128]{4,3,2,1,0:T(8,128)(2,1)S(1)}) fusion(bf16[4,3,8,128,128]{4,3,2,1,0:T(8,128)(2,1)} %rest_0_.5), kind=kLoop, calls=%fused_computation.10 | loop fusion | bytes 1572864 | tf_op jit(solution)/shard_map/slice | solution.py:357
  16.6 1.3 %collective-permute-start.4 = (bf16[1,1,8,128,128]{4,3,2,1,0:T(8,128)(2,1)}, bf16[1,1,8,128,128]{4,3,2,1,0:T(8,128)(2,1)S(1)}, u32[]{:S(2)}, u32[]{:S(2)}) collective-permute-start(bf16[1,1,8,128,128]{4,3,2,1,0:T(8,128)(2,1)} %get-tuple-element.55), channel_id=1, source_target_pairs={{0,4},{4,8},{8,12},{1,5},{5,9},{9,13},{2,6},{6,10},{10,14},{3,7},{... | collective-permute-start | bytes 786440 | tf_op jit(solution)/shard_map/ppermute | solution.py:28
  17.9 0.8 %pad_maximum_fusion.1 = bf16[2,1,8,128,128]{4,3,2,1,0:T(8,128)(2,1)} fusion(bf16[1,1,8,128,128]{4,3,2,1,0:T(8,128)(2,1)S(1)} %get-tuple-element.56, bf16[1,1,8,128,128]{4,3,2,1,0:T(8,128)(2,1)S(1)} %get-tuple-element.54), kind=kLoop, calls=%fused_computation.1 | loop fusion | flops 262144 | bytes 1048576 | tf_op jit(solution)/shard_map/concatenate | solution.py:356
  18.7 1.3 %collective-permute-start = (bf16[2,1,8,128,128]{4,3,2,1,0:T(8,128)(2,1)}, bf16[2,1,8,128,128]{4,3,2,1,0:T(8,128)(2,1)S(1)}, u32[]{:S(2)}, u32[]{:S(2)}) collective-permute-start(bf16[2,1,8,128,128]{4,3,2,1,0:T(8,128)(2,1)} %pad_maximum_fusion.1), channel_id=1, source_target_pairs={{0,4},{4,8},{8,12},{1,5},{5,9},{9,13},{2,6},{6,10},{10,14},{3,7},{... | collective-permute-start | bytes 1572872 | tf_op jit(solution)/shard_map/ppermute | solution.py:28
  20.0 0.1 copy.14.picks_ref
  20.1 0.0 collective-permute-done.2
  20.1 5.7 %collective-permute-done.1 = bf16[2,512,128]{2,1,0:T(8,128)(2,1)} collective-permute-done((bf16[2,512,128]{2,1,0:T(8,128)(2,1)}, bf16[2,512,128]{2,1,0:T(8,128)(2,1)}, u32[]{:S(2)}, u32[]{:S(2)}) %collective-permute-start.1) | collective-permute-done | bytes 262176 | tf_op jit(solution)/shard_map/ppermute | solution.py:348
  25.8 0.1 select_select_fusion
  26.0 0.0 copy-start
  26.0 10.0 %blocks_from_2.1 = (bf16[256,1024]{1,0:T(8,128)(2,1)S(1)}, f32[2,1,128]{2,1,0:T(1,128)S(1)}, f32[512,128]{1,0:T(8,128)S(1)}, f32[512,128]{1,0:T(8,128)S(1)}, f32...) custom-call(s32[1]{0:T(128)} %bitcast.base_ref, s32[4,2]{1,0:T(4,128)S(1)} %copy.14.picks_ref, ...), custom_call_target="tpu_custom_call" | custom-call | flops 1677721600 | bytes 3932160 | tf_op jit(solution)/shard_map/blocks_from_2/pallas_call | solution.py:307
  36.1 4.5 %blocks_from_1.1 = (bf16[128,1024]{1,0:T(8,128)(2,1)S(1)}, f32[1,1,128]{2,1,0:T(1,128)S(1)}, f32[512,128]{1,0:T(8,128)S(1)}, f32[512,128]{1,0:T(8,128)S(1)}, f32...) custom-call(s32[1]{0:T(128)} %bitcast.base_ref, s32[4,2]{1,0:T(4,128)S(1)} %copy.14.picks_ref, ...), custom_call_target="tpu_custom_call" | custom-call | flops 838860800 | bytes 1966080 | tf_op jit(solution)/shard_map/blocks_from_1/pallas_call | solution.py:307
  40.5 1.0 %collective-permute-done = bf16[2,1,8,128,128]{4,3,2,1,0:T(8,128)(2,1)S(1)} collective-permute-done((bf16[2,1,8,128,128]{4,3,2,1,0:T(8,128)(2,1)}, bf16[2,1,8,128,128]{4,3,2,1,0:T(8,128)(2,1)S(1)}, u32[]{:S(2)}, u32[]{:S(2)}) %collective-permute-start) | collective-permute-done | bytes 524320 | tf_op jit(solution)/shard_map/ppermute | solution.py:28
  41.6 4.5 %blocks_from_0.1 = (bf16[128,1024]{1,0:T(8,128)(2,1)S(1)}, f32[1,1,128]{2,1,0:T(1,128)S(1)}, f32[512,128]{1,0:T(8,128)S(1)}, f32[512,128]{1,0:T(8,128)S(1)}, f32...) custom-call(s32[1]{0:T(128)} %bitcast.base_ref, s32[4,2]{1,0:T(4,128)S(1)} %copy.14.picks_ref, ...), custom_call_target="tpu_custom_call" | custom-call | flops 838860800 | bytes 1966080 | tf_op jit(solution)/shard_map/blocks_from_0/pallas_call | solution.py:307
  46.1 0.1 collective-permute-start.8
  46.2 1.3 %collective-permute-start.5 = (bf16[512,128]{1,0:T(8,128)(2,1)S(1)}, bf16[512,128]{1,0:T(8,128)(2,1)S(1)}, u32[]{:S(2)}, u32[]{:S(2)}) collective-permute-start(bf16[512,128]{1,0:T(8,128)(2,1)S(1)} %convert_element_type.22), channel_id=1, source_target_pairs={{4,0},{12,8},{5,1},{13,9},{6,2},{14,10},{7,3},{15,11},{20,16},{28,... | collective-permute-start | bytes 393224 | tf_op jit(solution)/shard_map/ppermute | solution.py:394
  47.5 1.3 %collective-permute-start.7 = (bf16[512,128]{1,0:T(8,128)(2,1)S(1)}, bf16[512,128]{1,0:T(8,128)(2,1)S(1)}, u32[]{:S(2)}, u32[]{:S(2)}) collective-permute-start(bf16[512,128]{1,0:T(8,128)(2,1)S(1)} %convert_element_type.25), channel_id=1, source_target_pairs={{4,0},{12,8},{5,1},{13,9},{6,2},{14,10},{7,3},{15,11},{20,16},{28,... | collective-permute-start | bytes 393224 | tf_op jit(solution)/shard_map/ppermute | solution.py:394
  48.8 1.6 %collective-permute-start.9 = (f32[512]{0:T(512)S(1)}, f32[512]{0:T(512)S(1)}, u32[]{:S(2)}, u32[]{:S(2)}) collective-permute-start(f32[512]{0:T(512)S(1)} %add.20), channel_id=1, source_target_pairs={{0,1},{1,0},{2,3},{3,2},{4,5},{5,4},{6,7},{7,6},{8,9},{9,8},{10,11... | collective-permute-start | bytes 6152 | tf_op jit(solution)/shard_map/ppermute | solution.py:33
  50.4 2.1 %collective-permute-done.9 = f32[512]{0:T(512)S(1)} collective-permute-done((f32[512]{0:T(512)S(1)}, f32[512]{0:T(512)S(1)}, u32[]{:S(2)}, u32[]{:S(2)}) %collective-permute-start.9) | collective-permute-done | bytes 2080 | tf_op jit(solution)/shard_map/ppermute | solution.py:33
  52.5 1.9 %collective-permute-done.5.rest_1_ = bf16[512,128]{1,0:T(8,128)(2,1)S(1)} collective-permute-done((bf16[512,128]{1,0:T(8,128)(2,1)S(1)}, bf16[512,128]{1,0:T(8,128)(2,1)S(1)}, u32[]{:S(2)}, u32[]{:S(2)}) %collective-permute-start.5) | collective-permute-done | bytes 131104 | tf_op jit(solution)/shard_map/ppermute | solution.py:394
  54.4 1.3 %collective-permute-start.11 = (bf16[512,128]{1,0:T(8,128)(2,1)S(1)}, bf16[512,128]{1,0:T(8,128)(2,1)S(1)}, u32[]{:S(2)}, u32[]{:S(2)}) collective-permute-start(bf16[512,128]{1,0:T(8,128)(2,1)S(1)} %add_convert_fusion.1), channel_id=1, source_target_pairs={{8,0},{9,1},{10,2},{11,3},{24,16},{25,17},{26,18},{27,19}} | collective-permute-start | bytes 393224 | tf_op jit(solution)/shard_map/ppermute | solution.py:394
  55.7 1.3 %collective-permute-start.6 = (bf16[2,2,128,128]{3,2,1,0:T(8,128)(2,1)S(1)}, bf16[2,2,128,128]{3,2,1,0:T(8,128)(2,1)S(1)}, u32[]{:S(2)}, u32[]{:S(2)}) collective-permute-start(bf16[2,2,128,128]{3,2,1,0:T(8,128)(2,1)S(1)} %add_convert_fusion.2), channel_id=1, source_target_pairs={{4,0},{8,4},{12,8},{5,1},{9,5},{13,9},{6,2},{10,6},{14,10},{7,3},{... | collective-permute-start | bytes 393224 | tf_op jit(solution)/shard_map/ppermute | solution.py:28
  57.1 1.6 %collective-permute-start.12 = (f32[512]{0:T(512)S(1)}, f32[512]{0:T(512)S(1)}, u32[]{:S(2)}, u32[]{:S(2)}) collective-permute-start(f32[512]{0:T(512)S(1)} %add.21), channel_id=1, source_target_pairs={{0,2},{1,3},{2,0},{3,1},{4,6},{5,7},{6,4},{7,5},{8,10},{9,11},{10,... | collective-permute-start | bytes 6152 | tf_op jit(solution)/shard_map/ppermute | solution.py:33
  58.7 1.3 %collective-permute-start.10 = (bf16[512,128]{1,0:T(8,128)(2,1)S(1)}, bf16[512,128]{1,0:T(8,128)(2,1)S(1)}, u32[]{:S(2)}, u32[]{:S(2)}) collective-permute-start(bf16[512,128]{1,0:T(8,128)(2,1)S(1)} %add_convert_fusion), channel_id=1, source_target_pairs={{8,0},{9,1},{10,2},{11,3},{24,16},{25,17},{26,18},{27,19}} | collective-permute-start | bytes 393224 | tf_op jit(solution)/shard_map/ppermute | solution.py:394
  60.0 1.0 %pad_maximum_fusion = bf16[512,1024]{1,0:T(8,128)(2,1)} fusion(bf16[256,1024]{1,0:T(8,128)(2,1)S(1)} %get-tuple-element.39, bf16[128,1024]{1,0:T(8,128)(2,1)S(1)} %get-tuple-element.38, bf16[128,1024]{1,0:T(8,128)(2,1)S(1)} %get-tuple-element.37), kind=kLoop, calls=%fused_computation | loop fusion | flops 3145728 | bytes 2097152 | tf_op jit(solution)/shard_map/concatenate | solution.py:376
  61.0 0.6 add.23
  61.6 4.1 %collective-permute-done.6.back_ref = bf16[2,2,128,128]{3,2,1,0:T(8,128)(2,1)S(1)} collective-permute-done((bf16[2,2,128,128]{3,2,1,0:T(8,128)(2,1)S(1)}, bf16[2,2,128,128]{3,2,1,0:T(8,128)(2,1)S(1)}, u32[]{:S(2)}, u32[]{:S(2)}) %collective-permute-start.6) | collective-permute-done | bytes 131104 | tf_op jit(solution)/shard_map/ppermute | solution.py:28
  65.7 2.2 %collective-permute-done.10.rest_2_ = bf16[512,128]{1,0:T(8,128)(2,1)S(1)} collective-permute-done((bf16[512,128]{1,0:T(8,128)(2,1)S(1)}, bf16[512,128]{1,0:T(8,128)(2,1)S(1)}, u32[]{:S(2)}, u32[]{:S(2)}) %collective-permute-start.10) | collective-permute-done | bytes 131104 | tf_op jit(solution)/shard_map/ppermute | solution.py:394
  67.8 0.8 %finish.1 = (bf16[512,128]{1,0:T(8,128)(2,1)}, bf16[512,128]{1,0:T(8,128)(2,1)}) custom-call(s32[1]{0:T(128)} %bitcast.7.root_ref, f32[512,128]{1,0:T(8,128)S(1)} %get-tuple-element.40.dk_ref, f32[512,128]{1,0:T(8,128)S(1)} %get-tuple-element.41.dv_ref, f32[512,128]{1,0:T(8,128)S(1)} %get-tuple-element.42.dsk_ref, f32[512,128]{1,0:T(8,128)S(1)} %get-tuple-element.43.dsv_ref, ...), custom_call_target="tpu_custom_call" | custom-call | flops 262144 | bytes 917504 | tf_op jit(solution)/shard_map/finish/pallas_call | solution.py:249
  (32 shorter events, 0.3 us)
Async XLA Ops:
  0.6 25.2 %copy-start.4 = (bf16[512,128]{1,0:T(8,128)(2,1)S(1)}, bf16[512,128]{1,0:T(8,128)(2,1)}, u32[]{:S(2)}) copy-start(bf16[512,128]{1,0:T(8,128)(2,1)} %rest_5_.5) | copy-start | bytes 393220
  0.6 25.2 %copy-start.5 = (bf16[512,128]{1,0:T(8,128)(2,1)S(1)}, bf16[512,128]{1,0:T(8,128)(2,1)}, u32[]{:S(2)}) copy-start(bf16[512,128]{1,0:T(8,128)(2,1)} %rest_6_.5) | copy-start | bytes 393220
  0.7 19.4 %copy-start.7 = (s32[4,2]{0,1:T(2,128)S(1)}, s32[4,2]{0,1:T(2,128)}, u32[]{:S(2)}) copy-start(s32[4,2]{0,1:T(2,128)} %param.14) | copy-start | bytes 100
  2.4 23.5 %copy-start.2 = (bf16[512,1024]{1,0:T(8,128)(2,1)S(1)}, bf16[512,1024]{1,0:T(8,128)(2,1)}, u32[]{:S(2)}) copy-start(bf16[512,1024]{1,0:T(8,128)(2,1)} %q_ref.5) | copy-start | bytes 3145732
  2.4 23.5 %copy-start.3 = (bf16[512,1024]{1,0:T(8,128)(2,1)S(1)}, bf16[512,1024]{1,0:T(8,128)(2,1)}, u32[]{:S(2)}) copy-start(bf16[512,1024]{1,0:T(8,128)(2,1)} %g_ref.5) | copy-start | bytes 3145732
  2.4 23.5 %copy-start.6 = (f32[512]{0:T(512)S(1)}, f32[512]{0:T(512)}, u32[]{:S(2)}) copy-start(f32[512]{0:T(512)} %param.15) | copy-start | bytes 6148
  2.4 17.7 %collective-permute-start.3 = (bf16[2,512,128]{2,1,0:T(8,128)(2,1)}, bf16[2,512,128]{2,1,0:T(8,128)(2,1)S(1)}, u32[]{:S(2)}, u32[]{:S(2)}) collective-permute-start(bf16[2,512,128]{2,1,0:T(8,128)(2,1)} %pad_maximum_fusion.2), channel_id=1, source_target_pairs={{0,4},{4,8},{8,12},{1,5},{5,9},{9,13},{2,6},{6,10},{10,14},{3,7},{... | collective-permute-start | bytes 786440 | tf_op jit(solution)/shard_map/ppermute | solution.py:28
  7.5 12.7 %collective-permute-start.2 = (bf16[2,512,128]{2,1,0:T(8,128)(2,1)}, bf16[2,512,128]{2,1,0:T(8,128)(2,1)}, u32[]{:S(2)}, u32[]{:S(2)}) collective-permute-start(bf16[2,512,128]{2,1,0:T(8,128)(2,1)} %pad_maximum_fusion.2), channel_id=1, source_target_pairs={{0,8},{1,9},{2,10},{3,11},{16,24},{17,25},{18,26},{19,27}} | collective-permute-start | bytes 786440 | tf_op jit(solution)/shard_map/ppermute | solution.py:348
  12.7 13.1 %collective-permute-start.1 = (bf16[2,512,128]{2,1,0:T(8,128)(2,1)}, bf16[2,512,128]{2,1,0:T(8,128)(2,1)}, u32[]{:S(2)}, u32[]{:S(2)}) collective-permute-start(bf16[2,512,128]{2,1,0:T(8,128)(2,1)} %pad_maximum_fusion.2), channel_id=1, source_target_pairs={{0,12},{1,13},{2,14},{3,15},{16,28},{17,29},{18,30},{19,31}} | collective-permute-start | bytes 786440 | tf_op jit(solution)/shard_map/ppermute | solution.py:348
  16.6 19.5 %collective-permute-start.4 = (bf16[1,1,8,128,128]{4,3,2,1,0:T(8,128)(2,1)}, bf16[1,1,8,128,128]{4,3,2,1,0:T(8,128)(2,1)S(1)}, u32[]{:S(2)}, u32[]{:S(2)}) collective-permute-start(bf16[1,1,8,128,128]{4,3,2,1,0:T(8,128)(2,1)} %get-tuple-element.55), channel_id=1, source_target_pairs={{0,4},{4,8},{8,12},{1,5},{5,9},{9,13},{2,6},{6,10},{10,14},{3,7},{... | collective-permute-start | bytes 786440 | tf_op jit(solution)/shard_map/ppermute | solution.py:28
  18.7 22.8 %collective-permute-start = (bf16[2,1,8,128,128]{4,3,2,1,0:T(8,128)(2,1)}, bf16[2,1,8,128,128]{4,3,2,1,0:T(8,128)(2,1)S(1)}, u32[]{:S(2)}, u32[]{:S(2)}) collective-permute-start(bf16[2,1,8,128,128]{4,3,2,1,0:T(8,128)(2,1)} %pad_maximum_fusion.1), channel_id=1, source_target_pairs={{0,4},{4,8},{8,12},{1,5},{5,9},{9,13},{2,6},{6,10},{10,14},{3,7},{... | collective-permute-start | bytes 1572872 | tf_op jit(solution)/shard_map/ppermute | solution.py:28
  26.0 10.1 %copy-start = (bf16[4,3,8,128,128]{4,3,2,1,0:T(8,128)(2,1)S(1)}, bf16[4,3,8,128,128]{4,3,2,1,0:T(8,128)(2,1)}, u32[]{:S(2)}) copy-start(bf16[4,3,8,128,128]{4,3,2,1,0:T(8,128)(2,1)} %rest_0_.5) | copy-start | bytes 9437188
  26.0 10.1 %copy-start.1 = (bf16[4,2,8,128,128]{4,3,2,1,0:T(8,128)(2,1)S(1)}, bf16[4,2,8,128,128]{4,3,2,1,0:T(8,128)(2,1)}, u32[]{:S(2)}) copy-start(bf16[4,2,8,128,128]{4,3,2,1,0:T(8,128)(2,1)} %rest_4_.5) | copy-start | bytes 6291460
  46.1 2.7 %collective-permute-start.8 = (f32[512]{0:T(512)S(1)}, f32[512]{0:T(512)S(1)}, u32[]{:S(2)}, u32[]{:S(2)}) collective-permute-start(f32[512]{0:T(512)S(1)} %bitcast.20), channel_id=1, source_target_pairs={{0,16},{16,0},{1,17},{17,1},{2,18},{18,2},{3,19},{19,3},{4,20},{20... | collective-permute-start | bytes 6152 | tf_op jit(solution)/shard_map/ppermute | solution.py:33
  46.2 8.2 %collective-permute-start.5 = (bf16[512,128]{1,0:T(8,128)(2,1)S(1)}, bf16[512,128]{1,0:T(8,128)(2,1)S(1)}, u32[]{:S(2)}, u32[]{:S(2)}) collective-permute-start(bf16[512,128]{1,0:T(8,128)(2,1)S(1)} %convert_element_type.22), channel_id=1, source_target_pairs={{4,0},{12,8},{5,1},{13,9},{6,2},{14,10},{7,3},{15,11},{20,16},{28,... | collective-permute-start | bytes 393224 | tf_op jit(solution)/shard_map/ppermute | solution.py:394
  47.5 9.5 %collective-permute-start.7 = (bf16[512,128]{1,0:T(8,128)(2,1)S(1)}, bf16[512,128]{1,0:T(8,128)(2,1)S(1)}, u32[]{:S(2)}, u32[]{:S(2)}) collective-permute-start(bf16[512,128]{1,0:T(8,128)(2,1)S(1)} %convert_element_type.25), channel_id=1, source_target_pairs={{4,0},{12,8},{5,1},{13,9},{6,2},{14,10},{7,3},{15,11},{20,16},{28,... | collective-permute-start | bytes 393224 | tf_op jit(solution)/shard_map/ppermute | solution.py:394
  48.8 3.7 %collective-permute-start.9 = (f32[512]{0:T(512)S(1)}, f32[512]{0:T(512)S(1)}, u32[]{:S(2)}, u32[]{:S(2)}) collective-permute-start(f32[512]{0:T(512)S(1)} %add.20), channel_id=1, source_target_pairs={{0,1},{1,0},{2,3},{3,2},{4,5},{5,4},{6,7},{7,6},{8,9},{9,8},{10,11... | collective-permute-start | bytes 6152 | tf_op jit(solution)/shard_map/ppermute | solution.py:33
  54.4 11.2 %collective-permute-start.11 = (bf16[512,128]{1,0:T(8,128)(2,1)S(1)}, bf16[512,128]{1,0:T(8,128)(2,1)S(1)}, u32[]{:S(2)}, u32[]{:S(2)}) collective-permute-start(bf16[512,128]{1,0:T(8,128)(2,1)S(1)} %add_convert_fusion.1), channel_id=1, source_target_pairs={{8,0},{9,1},{10,2},{11,3},{24,16},{25,17},{26,18},{27,19}} | collective-permute-start | bytes 393224 | tf_op jit(solution)/shard_map/ppermute | solution.py:394
  55.7 9.9 %collective-permute-start.6 = (bf16[2,2,128,128]{3,2,1,0:T(8,128)(2,1)S(1)}, bf16[2,2,128,128]{3,2,1,0:T(8,128)(2,1)S(1)}, u32[]{:S(2)}, u32[]{:S(2)}) collective-permute-start(bf16[2,2,128,128]{3,2,1,0:T(8,128)(2,1)S(1)} %add_convert_fusion.2), channel_id=1, source_target_pairs={{4,0},{8,4},{12,8},{5,1},{9,5},{13,9},{6,2},{10,6},{14,10},{7,3},{... | collective-permute-start | bytes 393224 | tf_op jit(solution)/shard_map/ppermute | solution.py:28
  57.1 3.9 %collective-permute-start.12 = (f32[512]{0:T(512)S(1)}, f32[512]{0:T(512)S(1)}, u32[]{:S(2)}, u32[]{:S(2)}) collective-permute-start(f32[512]{0:T(512)S(1)} %add.21), channel_id=1, source_target_pairs={{0,2},{1,3},{2,0},{3,1},{4,6},{5,7},{6,4},{7,5},{8,10},{9,11},{10,... | collective-permute-start | bytes 6152 | tf_op jit(solution)/shard_map/ppermute | solution.py:33
  58.7 9.1 %collective-permute-start.10 = (bf16[512,128]{1,0:T(8,128)(2,1)S(1)}, bf16[512,128]{1,0:T(8,128)(2,1)S(1)}, u32[]{:S(2)}, u32[]{:S(2)}) collective-permute-start(bf16[512,128]{1,0:T(8,128)(2,1)S(1)} %add_convert_fusion), channel_id=1, source_target_pairs={{8,0},{9,1},{10,2},{11,3},{24,16},{25,17},{26,18},{27,19}} | collective-permute-start | bytes 393224 | tf_op jit(solution)/shard_map/ppermute | solution.py:394
